TPU v7x, 512 devices: a whole 4x4x16 slice. The times are simulated.
512 devices in a mesh: lat: 16 (over z_hi, x, core), lon: 32 (over z_lo, y).
Axes of the slice: x: 4, y: 4, z: 16 (z_hi: 2, z_lo: 8; z = z_hi * 8 + z_lo), core: 2. Of those that a mesh axis runs over, the one named last changes fastest.
Arguments:
- tokens: bfloat16 [2, 128, 512, 384], P(None, 'lat', 'lon'), may hold values from -6 to 6
- cotangent: bfloat16 [2, 128, 512, 384], P(None, 'lat', 'lon'), may hold values from -6 to 6
- ocean_mask: int32 [16, 64], P(None, 'lon'), may hold values from 0 to 1, as said below
- gain: bfloat16 [384], replicated, may hold values from 0.25 to 1.75
- w_qkv: bfloat16 [384, 1152], replicated, may hold values from -0.3125 to 0.3125
- w_out: bfloat16 [384, 384], replicated, may hold values from -0.3125 to 0.3125
Outputs:
- token_grad: bfloat16 [2, 128, 512, 384], P(None, 'lat', 'lon')
- qkv_grad: bfloat16 [384, 1152], replicated
- out_grad: bfloat16 [384, 384], replicated
- gain_grad: bfloat16 [384], replicated
Inputs may be any that keep to these rules, and one draw needn't show every extreme that they name: `ocean_mask`: among the windows of one lon index (all 16 window rows times its 2 window columns) at most 32 are ocean, and the first lon index has exactly that many.
All inputs are finite; a program needn't handle non-finite values.
Results may differ from a plain program's by a relative error of at most 0.014.
Values may be sent and summed in bfloat16 or wider, within the bound.
No kernel may reach another device: no remote copies, remote signals or barrier semaphores. Data moves between devices by JAX's collectives and lax.ppermute only.
A program may use at most 64 MiB of HBM per device.

v0:
```python
import jax
import jax.numpy as jnp
from jax import lax
from jax.sharding import PartitionSpec as P

HEADS = 12
HDIM = 32


def passed_along(block, axis, distance):
    devices = range(lax.axis_size(axis))
    route = [((i - distance) % len(devices), i) for i in devices]
    return lax.ppermute(block, axis, route)


def contract(form, left, right):
    return jnp.einsum(form, left, right, preferred_element_type=jnp.float32)


def window_grads(x_win, g_win, region, gain, w_qkv, w_out):
    count, width, dim = x_win.shape
    scale = HDIM ** (-0.5)
    gain_float32 = gain.astype(jnp.float32)
    x_full = x_win.astype(jnp.float32)
    centered_input = x_full - jnp.mean(x_full, -1, keepdims=True)
    inverse_deviation = lax.rsqrt(
        jnp.mean(centered_input * centered_input, -1, keepdims=True) + 1e-05
    )
    normalized_input = centered_input * inverse_deviation
    norm_output = (normalized_input * gain_float32).astype(jnp.bfloat16)
    packed = contract("ntd,de->nte", norm_output, w_qkv).astype(jnp.bfloat16)
    packed = packed.reshape(count, width, 3, HEADS, HDIM)
    query = packed[:, :, 0]
    keys = packed[:, :, 1]
    values = packed[:, :, 2]
    scores = contract("nqhc,nkhc->nhqk", query, keys) * scale
    allowed = (region[:, :, None] == region[:, None, :])[:, None]
    scores = jnp.where(allowed, scores, -1e30)
    expo = jnp.exp(scores - jnp.max(scores, -1, keepdims=True))
    probs = expo / jnp.sum(expo, -1, keepdims=True)
    weights = probs.astype(jnp.bfloat16)
    attended = (
        contract("nhqk,nkhc->nqhc", weights, values).astype(jnp.bfloat16).reshape(count, width, dim)
    )
    out_term = contract("ntd,nte->de", attended, g_win)
    d_att = (
        contract("nte,de->ntd", g_win, w_out)
        .astype(jnp.bfloat16)
        .reshape(count, width, HEADS, HDIM)
    )
    d_probs = contract("nqhc,nkhc->nhqk", d_att, values)
    d_values = contract("nhqk,nqhc->nkhc", weights, d_att)
    d_scores = (probs * (d_probs - jnp.sum(d_probs * probs, -1, keepdims=True)) * scale).astype(
        jnp.bfloat16
    )
    d_query = contract("nhqk,nkhc->nqhc", d_scores, keys)
    d_keys = contract("nhqk,nqhc->nkhc", d_scores, query)
    d_packed = (
        jnp.stack([d_query, d_keys, d_values], 2)
        .reshape(count, width, 3 * dim)
        .astype(jnp.bfloat16)
    )
    qkv_term = contract("ntd,nte->de", norm_output, d_packed)
    gradient_after_norm = contract("nte,de->ntd", d_packed, w_qkv)
    gain_product = jnp.sum(gradient_after_norm * normalized_input, (0, 1))
    normalized_gradient = gradient_after_norm * gain_float32
    branch_gradient = inverse_deviation * (
        normalized_gradient
        - jnp.mean(normalized_gradient, -1, keepdims=True)
        - normalized_input * jnp.mean(normalized_gradient * normalized_input, -1, keepdims=True)
    )
    return (branch_gradient.astype(jnp.bfloat16), qkv_term, out_term, gain_product)


def to_windows(grid):
    levels, rows, cols, dim = grid.shape
    split = grid.reshape(levels, rows // 8, 8, cols // 8, 8, dim)
    return split.transpose(1, 3, 0, 2, 4, 5).reshape(rows // 8 * (cols // 8), levels * 64, dim)


def from_windows(blocks, levels, lat_w, lon_w):
    count, width, dim = blocks.shape
    split = blocks.reshape(lat_w, lon_w, levels, 8, 8, dim)
    return split.transpose(2, 0, 3, 1, 4, 5).reshape(levels, lat_w * 8, lon_w * 8, dim)


def edge_lon(stacked, step):
    if step < 0:
        piece = stacked[:, :, :, :4]
    else:
        piece = stacked[:, :, :, -4:]
    moved = passed_along(piece, "lon", step)
    if step < 0:
        return jnp.concatenate([stacked[:, :, :, 4:], moved], 3)
    return jnp.concatenate([moved, stacked[:, :, :, :-4]], 3)


def edge_lat(stacked, step):
    if step < 0:
        piece = stacked[:, :, :4]
    else:
        piece = stacked[:, :, -4:]
    moved = passed_along(piece, "lat", step)
    if step < 0:
        return jnp.concatenate([stacked[:, :, 4:], moved], 2)
    return jnp.concatenate([moved, stacked[:, :, :-4]], 2)


def local(tokens, cotangent, ocean_mask, gain, w_qkv, w_out):
    levels, rows, cols, dim = tokens.shape
    lat_w = rows // 8
    lon_w = cols // 8
    count = lat_w * lon_w
    n_lat = lax.axis_size("lat")
    lat_index = lax.axis_index("lat")
    stacked = edge_lat(edge_lon(jnp.stack([tokens, cotangent]), -1), -1)
    x_blocks = to_windows(stacked[0])
    g_blocks = to_windows(stacked[1])
    width = x_blocks.shape[1]
    token_row = jnp.arange(width) // 8 % 8
    flat = ocean_mask.reshape(-1)
    start = lat_index * count
    local_ocean = lax.dynamic_slice_in_dim(flat, start, count, 0)
    g_masked = g_blocks * local_ocean.astype(jnp.bfloat16)[:, None, None]
    last_window = (lat_index == n_lat - 1) & (jnp.arange(count) // lon_w == lat_w - 1)
    wrapped = last_window[:, None] & (token_row >= 4)[None, :]
    d_blocks, qkv_term, out_term, gain_product = window_grads(
        x_blocks, g_masked, wrapped.astype(jnp.int32), gain, w_qkv, w_out
    )
    d_grid = from_windows(d_blocks, levels, lat_w, lon_w)
    d_grid = edge_lon(edge_lat(d_grid[None], 1), 1)[0]
    token_grad = (cotangent.astype(jnp.float32) + d_grid.astype(jnp.float32)).astype(jnp.bfloat16)
    totals = lax.psum((qkv_term, out_term, gain_product), ("lat", "lon"))
    qkv_total, out_total, gain_total = (totals[0], totals[1], totals[2])
    return (
        token_grad,
        qkv_total.astype(jnp.bfloat16),
        out_total.astype(jnp.bfloat16),
        gain_total.astype(jnp.bfloat16),
    )


def solution(mesh):
    return jax.shard_map(
        local,
        mesh=mesh,
        in_specs=(
            P(None, "lat", "lon", None),
            P(None, "lat", "lon", None),
            P(None, "lon"),
            P(),
            P(),
            P(),
        ),
        out_specs=(P(None, "lat", "lon", None), P(), P(), P()),
        check_vma=False,
    )
```

profile of v0, /device:TPU:1, one launch (start us, length us, event | category | flops | bytes accessed | tf_op | source)
XLA Modules:
  0.0 259.5 jit_solution(1139401937647588168)
XLA Ops:
  0.6 1.0 pad_maximum_fusion.3
  1.7 16.2 %collective-permute-start = (bf16[2,2,8,4,384]{4,3,2,1,0:T(4,128)(2,1)S(1)}, bf16[2,2,8,4,384]{4,3,2,1,0:T(4,128)(2,1)S(1)}, u32[]{:S(2)}, u32[]{:S(2)}) collective-permute-start(bf16[2,2,8,4,384]{4,3,2,1,0:T(4,128)(2,1)S(1)} %pad_maximum_fusion.3), channel_id=1, source_target_pairs={{1,0},{2,1},{3,2},{4,3},{5,4},{6,5},{7,6},{8,7},{9,8},{10,9},{11,1... | collective-permute-start | bytes 294920 | tf_op jit(solution)/shard_map/ppermute | solution.py:13
  17.9 1.2 slice_maximum_fusion
  19.1 0.7 convert_element_type.105
  19.8 0.8 copy.92
  20.7 0.1 fusion.31
  20.9 2.9 %collective-permute-start.1 = (bf16[2,2,4,16,384]{4,3,2,1,0:T(8,128)(2,1)S(1)}, bf16[2,2,4,16,384]{4,3,2,1,0:T(8,128)(2,1)S(1)}, u32[]{:S(2)}, u32[]{:S(2)}) collective-permute-start(bf16[2,2,4,16,384]{4,3,2,1,0:T(8,128)(2,1)S(1)} %get-tuple-element.15), channel_id=1, source_target_pairs={{32,0},{64,32},{96,64},{128,96},{160,128},{192,160},{224,192},{256... | collective-permute-start | bytes 589832 | tf_op jit(solution)/shard_map/ppermute | solution.py:13
  23.8 4.3 %collective-permute-done.1 = bf16[2,2,4,16,384]{4,3,2,1,0:T(8,128)(2,1)S(1)} collective-permute-done((bf16[2,2,4,16,384]{4,3,2,1,0:T(8,128)(2,1)S(1)}, bf16[2,2,4,16,384]{4,3,2,1,0:T(8,128)(2,1)S(1)}, u32[]{:S(2)}, u32[]{:S(2)}) %collective-permute-start.1) | collective-permute-done | bytes 196640 | tf_op jit(solution)/shard_map/ppermute | solution.py:13
  28.2 0.1 fusion.27
  28.4 0.2 multiply_reduce_fusion.3
  29.0 0.3 copy-done.3
  29.3 0.3 convolution_convert_fusion.1
  29.6 0.2 copy.93
  29.8 0.5 convolution_convert_fusion
  30.3 0.3 copy.88
  30.7 1.8 fusion.55
  32.5 2.5 convolution_convert_fusion.2
  35.0 1.2 convolution_bitcast_fusion.2
  36.2 1.3 fusion.39
  37.6 3.2 %fusion.13 = bf16[2,128,1,12,32]{1,4,3,0,2:T(8,128)(2,1)} fusion(f32[2,12,128,128]{2,3,1,0:T(8,128)S(1)} %fusion.39, bf16[2,128,3,12,32]{1,4,3,2,0:T(8,128)(2,1)} %bitcast.117, f32[2,12,128,128]{2,3,1,0:T(8,128)} %get-tuple-element.19, f32[2,12,128]{2,1,0:T(8,128)S(1)} %get-tuple-element.18), kind=kOutput, calls=%fused_computation.13 | convolution fusion | flops 27921536 | bytes 6717440 | tf_op jit(solution)/shard_map/nhqk,nkhc->nqhc/dot_general | solution.py:17
  40.8 3.3 %fusion.16 = bf16[2,128,1,12,32]{1,4,3,0,2:T(8,128)(2,1)} fusion(f32[2,12,128,128]{2,3,1,0:T(8,128)S(1)} %fusion.39, bf16[2,128,3,12,32]{1,4,3,2,0:T(8,128)(2,1)} %bitcast.118, f32[2,12,128,128]{2,3,1,0:T(8,128)} %get-tuple-element.19, f32[2,12,128]{2,1,0:T(8,128)S(1)} %get-tuple-element.18), kind=kOutput, calls=%fused_computation.14 | convolution fusion | flops 27921536 | bytes 6717440 | tf_op jit(solution)/shard_map/nhqk,nqhc->nkhc/dot_general | solution.py:17
  44.1 0.1 multiply_convert_fusion.1
  44.3 1.2 convolution_bitcast_fusion.1
  45.7 0.7 multiply_reduce_fusion.1
  46.4 0.2 multiply_convert_fusion.2
  46.7 1.9 collective-permute-start.2
  48.6 0.5 convolution_bitcast_fusion
  49.1 7.6 %collective-permute-done.2 = bf16[1,2,4,16,384]{4,3,2,1,0:T(8,128)(2,1)} collective-permute-done((bf16[1,2,4,16,384]{4,3,2,1,0:T(8,128)(2,1)S(1)}, bf16[1,2,4,16,384]{4,3,2,1,0:T(8,128)(2,1)}, u32[]{:S(2)}, u32[]{:S(2)}) %collective-permute-start.2) | collective-permute-done | bytes 98336 | tf_op jit(solution)/shard_map/ppermute | solution.py:13
  56.7 1.4 pad_maximum_fusion.4
  58.2 2.2 collective-permute-start.3
  60.4 197.4 %all-reduce.2 = (bf16[384,1152]{1,0:T(8,128)(2,1)}, bf16[384,384]{1,0:T(8,128)(2,1)}, bf16[384]{0:T(512)(128)(2,1)}) all-reduce(f32[384,1152]{1,0:T(8,128)S(1)} %convolution_bitcast_fusion, f32[384,384]{1,0:T(8,128)S(1)} %convolution_bitcast_fusion.1, f32[384]{0:T(512)S(1)} %get-tuple-element.4), channel_id=1, replica_groups=mesh['lat'=16,'lon'=32] {'lat','lon'}, use_global_device_ids=true, to_apply=%region_7.8 | all-reduce | flops 590208 | bytes 3541248 | tf_op jit(solution)/shard_map/psum | solution.py:133
  257.8 1.7 fusion.24
  (40 shorter events, 1.0 us)
Async XLA Ops:
  0.6 29.2 %copy-start = (bf16[384,1152]{1,0:T(8,128)(2,1)S(1)}, bf16[384,1152]{1,0:T(8,128)(2,1)}, u32[]{:S(2)}) copy-start(bf16[384,1152]{1,0:T(8,128)(2,1)} %param.10) | copy-start | bytes 2654212
  1.7 19.1 %collective-permute-start = (bf16[2,2,8,4,384]{4,3,2,1,0:T(4,128)(2,1)S(1)}, bf16[2,2,8,4,384]{4,3,2,1,0:T(4,128)(2,1)S(1)}, u32[]{:S(2)}, u32[]{:S(2)}) collective-permute-start(bf16[2,2,8,4,384]{4,3,2,1,0:T(4,128)(2,1)S(1)} %pad_maximum_fusion.3), channel_id=1, source_target_pairs={{1,0},{2,1},{3,2},{4,3},{5,4},{6,5},{7,6},{8,7},{9,8},{10,9},{11,1... | collective-permute-start | bytes 294920 | tf_op jit(solution)/shard_map/ppermute | solution.py:13
  20.9 7.3 %collective-permute-start.1 = (bf16[2,2,4,16,384]{4,3,2,1,0:T(8,128)(2,1)S(1)}, bf16[2,2,4,16,384]{4,3,2,1,0:T(8,128)(2,1)S(1)}, u32[]{:S(2)}, u32[]{:S(2)}) collective-permute-start(bf16[2,2,4,16,384]{4,3,2,1,0:T(8,128)(2,1)S(1)} %get-tuple-element.15), channel_id=1, source_target_pairs={{32,0},{64,32},{96,64},{128,96},{160,128},{192,160},{224,192},{256... | collective-permute-start | bytes 589832 | tf_op jit(solution)/shard_map/ppermute | solution.py:13
  28.3 1.0 copy-start.3
  30.7 4.4 %copy-start.2 = (bf16[2,128,1152]{1,2,0:T(8,128)(2,1)}, bf16[2,128,1152]{1,2,0:T(8,128)(2,1)S(1)}, u32[]{:S(2)}) copy-start(bf16[2,128,1152]{1,2,0:T(8,128)(2,1)S(1)} %copy.88) | copy-start | bytes 1769476
  32.5 2.5 copy-start.7
  44.1 1.5 copy-start.4
  44.1 1.5 copy-start.5
  44.1 1.5 copy-start.6
  46.7 10.0 %collective-permute-start.2 = (bf16[1,2,4,16,384]{4,3,2,1,0:T(8,128)(2,1)S(1)}, bf16[1,2,4,16,384]{4,3,2,1,0:T(8,128)(2,1)}, u32[]{:S(2)}, u32[]{:S(2)}) collective-permute-start(bf16[1,2,4,16,384]{4,3,2,1,0:T(8,128)(2,1)S(1)} %get-tuple-element.16), channel_id=1, source_target_pairs={{480,0},{0,32},{32,64},{64,96},{96,128},{128,160},{160,192},{192,2... | collective-permute-start | bytes 294920 | tf_op jit(solution)/shard_map/ppermute | solution.py:13
  49.1 208.7 %copy-start.1 = (bf16[2,8,16,384]{3,2,1,0:T(8,128)(2,1)S(1)}, bf16[2,8,16,384]{3,2,1,0:T(8,128)(2,1)}, u32[]{:S(2)}) copy-start(bf16[2,8,16,384]{3,2,1,0:T(8,128)(2,1)} %param.7) | copy-start | bytes 589828
  58.2 199.6 %collective-permute-start.3 = (bf16[1,2,8,4,384]{4,3,2,1,0:T(4,128)(2,1)}, bf16[1,2,8,4,384]{4,3,2,1,0:T(4,128)(2,1)}, u32[]{:S(2)}, u32[]{:S(2)}) collective-permute-start(bf16[1,2,8,4,384]{4,3,2,1,0:T(4,128)(2,1)} %pad_maximum_fusion.4), channel_id=1, source_target_pairs={{31,0},{0,1},{1,2},{2,3},{3,4},{4,5},{5,6},{6,7},{7,8},{8,9},{9,10... | collective-permute-start | bytes 147464 | tf_op jit(solution)/shard_map/ppermute | solution.py:13
where the time goes:
time: 260 us; the launch traced here: 259 us
  blocking collectives  197 us (76%)
  starting transfers between devices  23.2 us (9%)
  matrix products  16.7 us (6%)
  waiting for transfers between devices  11.9 us (5%)
  other arithmetic  7.29 us (3%)
    psum x1, blocking collectives, local(): totals = lax.psum((qkv_term, out_term, gain_product), ('lat', 'lon'))  197 us
    ppermute x4, starting transfers between devices, passed_along(): return lax.ppermute(block, axis, route)  23.2 us
    dot_general x10, matrix products, contract(): return jnp.einsum(form, left, right, preferred_element_type=jnp.float32)  14.9 us
    ppermute x4, waiting for transfers between devices, passed_along(): return lax.ppermute(block, axis, route)  11.9 us
  transfers between devices with their start and end apart: 4, of which 2 were waited for; matrix products, arithmetic and copies ran while one was open for 1% of the time, Pallas kernels for 0%

commit v1 on v0

--- a/solution.py
+++ b/solution.py
@@ -1,6 +1,7 @@
 import jax
 import jax.numpy as jnp
 from jax import lax
+from jax.sharding import Mesh
 from jax.sharding import PartitionSpec as P
 
 HEADS = 12
@@ -62,14 +63,13 @@
     )
     qkv_term = contract("ntd,nte->de", norm_output, d_packed)
     gradient_after_norm = contract("nte,de->ntd", d_packed, w_qkv)
-    gain_product = jnp.sum(gradient_after_norm * normalized_input, (0, 1))
     normalized_gradient = gradient_after_norm * gain_float32
     branch_gradient = inverse_deviation * (
         normalized_gradient
         - jnp.mean(normalized_gradient, -1, keepdims=True)
         - normalized_input * jnp.mean(normalized_gradient * normalized_input, -1, keepdims=True)
     )
-    return (branch_gradient.astype(jnp.bfloat16), qkv_term, out_term, gain_product)
+    return (branch_gradient.astype(jnp.bfloat16), qkv_term, out_term)
 
 
 def to_windows(grid):
@@ -89,7 +89,7 @@
         piece = stacked[:, :, :, :4]
     else:
         piece = stacked[:, :, :, -4:]
-    moved = passed_along(piece, "lon", step)
+    moved = passed_along(piece, LON, step)
     if step < 0:
         return jnp.concatenate([stacked[:, :, :, 4:], moved], 3)
     return jnp.concatenate([moved, stacked[:, :, :, :-4]], 3)
@@ -100,10 +100,58 @@
         piece = stacked[:, :, :4]
     else:
         piece = stacked[:, :, -4:]
-    moved = passed_along(piece, "lat", step)
+    moved = passed_along(piece, LAT, step)
     if step < 0:
         return jnp.concatenate([stacked[:, :, 4:], moved], 2)
     return jnp.concatenate([moved, stacked[:, :, :-4]], 2)
+
+
+LAT = ("zhi", "x", "core")
+LON = ("zlo", "y")
+PLANE = ("x", "y")
+RING = ("zhi", "zlo")
+
+
+def exchange(parts, axis):
+    return lax.all_to_all(parts, axis, 0, 0, tiled=False)
+
+
+def summed(parts):
+    return jnp.sum(parts.astype(jnp.float32), 0).astype(jnp.bfloat16)
+
+
+def spread(part, axis):
+    parts = jnp.broadcast_to(part[None], (lax.axis_size(axis),) + part.shape)
+    return exchange(parts, axis)
+
+
+def reduced(blocks):
+    core = lax.axis_index("core")
+    swap = [(0, 1), (1, 0)]
+    half = blocks.shape[0] // 2
+    mine = lax.dynamic_slice_in_dim(blocks, core * half, half, 0)
+    other = lax.dynamic_slice_in_dim(blocks, (1 - core) * half, half, 0).astype(jnp.bfloat16)
+    mine = (mine + lax.ppermute(other, "core", swap).astype(jnp.float32)).astype(jnp.bfloat16)
+    n_plane = lax.axis_size(PLANE)
+    mine = summed(exchange(mine.reshape(n_plane, half // n_plane, 128), PLANE))
+    n_ring = lax.axis_size(RING)
+    mine = summed(exchange(mine.reshape(n_ring, mine.shape[0] // n_ring, 128), RING))
+    mine = spread(mine, RING).reshape(-1, 128)
+    mine = spread(mine, PLANE).reshape(half, 128)
+    other = lax.ppermute(mine, "core", swap)
+    first = jnp.where(core == 0, mine, other)
+    second = jnp.where(core == 0, other, mine)
+    return jnp.concatenate([first, second], 0)
+
+
+def to_blocks(array):
+    rows, cols = array.shape
+    return array.reshape(rows, cols // 128, 128).transpose(1, 0, 2).reshape(-1, 128)
+
+
+def from_blocks(blocks, rows):
+    count = blocks.shape[0] // rows
+    return blocks.reshape(count, rows, 128).transpose(1, 0, 2).reshape(rows, count * 128)
 
 
 def local(tokens, cotangent, ocean_mask, gain, w_qkv, w_out):
@@ -111,8 +159,8 @@
     lat_w = rows // 8
     lon_w = cols // 8
     count = lat_w * lon_w
-    n_lat = lax.axis_size("lat")
-    lat_index = lax.axis_index("lat")
+    n_lat = lax.axis_size(LAT)
+    lat_index = lax.axis_index(LAT)
     stacked = edge_lat(edge_lon(jnp.stack([tokens, cotangent]), -1), -1)
     x_blocks = to_windows(stacked[0])
     g_blocks = to_windows(stacked[1])
@@ -124,34 +172,35 @@
     g_masked = g_blocks * local_ocean.astype(jnp.bfloat16)[:, None, None]
     last_window = (lat_index == n_lat - 1) & (jnp.arange(count) // lon_w == lat_w - 1)
     wrapped = last_window[:, None] & (token_row >= 4)[None, :]
-    d_blocks, qkv_term, out_term, gain_product = window_grads(
+    d_blocks, qkv_term, out_term = window_grads(
         x_blocks, g_masked, wrapped.astype(jnp.int32), gain, w_qkv, w_out
     )
     d_grid = from_windows(d_blocks, levels, lat_w, lon_w)
     d_grid = edge_lon(edge_lat(d_grid[None], 1), 1)[0]
     token_grad = (cotangent.astype(jnp.float32) + d_grid.astype(jnp.float32)).astype(jnp.bfloat16)
-    totals = lax.psum((qkv_term, out_term, gain_product), ("lat", "lon"))
-    qkv_total, out_total, gain_total = (totals[0], totals[1], totals[2])
-    return (
-        token_grad,
-        qkv_total.astype(jnp.bfloat16),
-        out_total.astype(jnp.bfloat16),
-        gain_total.astype(jnp.bfloat16),
-    )
+    blocks = jnp.concatenate([to_blocks(qkv_term), to_blocks(out_term)], 0)
+    totals = reduced(blocks)
+    qkv_rows = w_qkv.size // 128
+    qkv_total = from_blocks(totals[:qkv_rows], dim)
+    out_total = from_blocks(totals[qkv_rows:], dim)
+    along = jnp.sum(w_qkv.astype(jnp.float32) * qkv_total.astype(jnp.float32), 1)
+    gain_total = along / gain.astype(jnp.float32)
+    return token_grad, qkv_total, out_total, gain_total.astype(jnp.bfloat16)
 
 
 def solution(mesh):
+    fine = Mesh(mesh.devices.reshape(2, 4, 2, 8, 4), ("zhi", "x", "core", "zlo", "y"))
     return jax.shard_map(
         local,
-        mesh=mesh,
+        mesh=fine,
         in_specs=(
-            P(None, "lat", "lon", None),
-            P(None, "lat", "lon", None),
-            P(None, "lon"),
+            P(None, LAT, LON, None),
+            P(None, LAT, LON, None),
+            P(None, LON),
             P(),
             P(),
             P(),
         ),
-        out_specs=(P(None, "lat", "lon", None), P(), P(), P()),
+        out_specs=(P(None, LAT, LON, None), P(), P(), P()),
         check_vma=False,
     )

time: 260 us -> 177 us (0.68)
  the two profiles are of different devices: /device:TPU:1 before, /device:TPU:0 now
where the time goes in v1:
time: 177 us; the launch traced here: 176 us
  blocking collectives  62.3 us (35%)
  waiting for transfers between devices  41.8 us (24%)
  starting transfers between devices  32.1 us (18%)
  matrix products  17.7 us (10%)
  local copies, waits for them, and re-layouts  10.8 us (6%)
  other arithmetic  10.2 us (6%)
    all_to_all x3, blocking collectives, exchange(): return lax.all_to_all(parts, axis, 0, 0, tiled=False)  62.3 us
    ppermute x4, waiting for transfers between devices, passed_along(): return lax.ppermute(block, axis, route)  30.1 us
    ppermute x4, starting transfers between devices, passed_along(): return lax.ppermute(block, axis, route)  24.7 us
    dot_general x10, matrix products, contract(): return jnp.einsum(form, left, right, preferred_element_type=jnp.float32)  15.3 us
    all_to_all x1, waiting for transfers between devices, exchange(): return lax.all_to_all(parts, axis, 0, 0, tiled=False)  9.45 us
    unnamed x54, local copies, waits for them, and re-layouts  5.25 us
    all_to_all x1, starting transfers between devices, exchange(): return lax.all_to_all(parts, axis, 0, 0, tiled=False)  3.58 us
  transfers between devices with their start and end apart: 7, of which 5 were waited for; matrix products, arithmetic and copies ran while one was open for 3% of the time, Pallas kernels for 0%

profile of v1, /device:TPU:0, one launch (start us, length us, event | category | flops | bytes accessed | tf_op | source)
XLA Modules:
  0.0 176.1 jit_solution(6524235655144672382)
XLA Ops:
  0.6 1.0 pad_maximum_fusion.5
  1.7 10.2 %collective-permute-start = (bf16[2,2,8,4,384]{4,3,2,1,0:T(4,128)(2,1)S(1)}, bf16[2,2,8,4,384]{4,3,2,1,0:T(4,128)(2,1)S(1)}, u32[]{:S(2)}, u32[]{:S(2)}) collective-permute-start(bf16[2,2,8,4,384]{4,3,2,1,0:T(4,128)(2,1)S(1)} %pad_maximum_fusion.5), channel_id=1, source_target_pairs={{1,0},{2,1},{3,2},{4,3},{5,4},{6,5},{7,6},{8,7},{9,8},{10,9},{11,1... | collective-permute-start | bytes 294920 | tf_op jit(solution)/shard_map/ppermute | solution.py:14
  11.9 1.2 slice_maximum_fusion
  14.9 9.6 %collective-permute-start.1 = (bf16[2,2,4,16,384]{4,3,2,1,0:T(8,128)(2,1)S(1)}, bf16[2,2,4,16,384]{4,3,2,1,0:T(8,128)(2,1)S(1)}, u32[]{:S(2)}, u32[]{:S(2)}) collective-permute-start(bf16[2,2,4,16,384]{4,3,2,1,0:T(8,128)(2,1)S(1)} %get-tuple-element.27), channel_id=1, source_target_pairs={{32,0},{64,32},{96,64},{128,96},{160,128},{192,160},{224,192},{256... | collective-permute-start | bytes 589832 | tf_op jit(solution)/shard_map/ppermute | solution.py:14
  24.6 3.8 %collective-permute-done.1 = bf16[2,2,4,16,384]{4,3,2,1,0:T(8,128)(2,1)S(1)} collective-permute-done((bf16[2,2,4,16,384]{4,3,2,1,0:T(8,128)(2,1)S(1)}, bf16[2,2,4,16,384]{4,3,2,1,0:T(8,128)(2,1)S(1)}, u32[]{:S(2)}, u32[]{:S(2)}) %collective-permute-start.1) | collective-permute-done | bytes 196640 | tf_op jit(solution)/shard_map/ppermute | solution.py:14
  31.5 2.4 %fusion.66 = (f32[2,12,128]{2,1,0:T(8,128)}, f32[2,12,128,128]{2,3,1,0:T(8,128)}) fusion(pred[2,128,128]{1,2,0:T(8,128)(4,1)S(1)} %broadcast_compare_fusion, bf16[2,128,3,12,32]{1,4,3,2,0:T(8,128)(2,1)S(1)} %bitcast.164), kind=kOutput, calls=%fused_computation.112 | convolution fusion | flops 26738816 | bytes 2011136 | tf_op jit(solution)/shard_map/sub | solution.py:40
  33.9 1.6 fusion.49
  35.6 1.2 fusion.24
  36.8 3.3 %fusion.25 = bf16[2,128,1,12,32]{1,4,3,0,2:T(8,128)(2,1)} fusion(f32[2,12,128,128]{2,3,1,0:T(8,128)S(1)} %fusion.49, bf16[2,128,3,12,32]{1,4,3,2,0:T(8,128)(2,1)} %bitcast.166, f32[2,12,128,128]{2,3,1,0:T(8,128)} %get-tuple-element.31, f32[2,12,128]{2,1,0:T(8,128)} %get-tuple-element.30), kind=kOutput, calls=%fused_computation.28 | convolution fusion | flops 28019840 | bytes 6717440 | tf_op jit(solution)/shard_map/nhqk,nqhc->nkhc/dot_general | solution.py:18
  40.1 3.3 %fusion.28 = bf16[2,128,1,12,32]{1,4,3,0,2:T(8,128)(2,1)} fusion(f32[2,12,128,128]{2,3,1,0:T(8,128)S(1)} %fusion.49, bf16[2,128,3,12,32]{1,4,3,2,0:T(8,128)(2,1)} %bitcast.167, f32[2,12,128,128]{2,3,1,0:T(8,128)} %get-tuple-element.31, f32[2,12,128]{2,1,0:T(8,128)} %get-tuple-element.30), kind=kOutput, calls=%fused_computation.29 | convolution fusion | flops 28019840 | bytes 6717440 | tf_op jit(solution)/shard_map/nhqk,nkhc->nqhc/dot_general | solution.py:18
  43.4 2.6 %convolution_convert_fusion.2 = bf16[2,12,32,128]{3,2,1,0:T(8,128)(2,1)} fusion(bf16[2,128,3,12,32]{1,4,3,2,0:T(8,128)(2,1)} %bitcast.168, f32[2,12,128,128]{2,3,1,0:T(8,128)} %get-tuple-element.31, f32[2,12,128]{2,1,0:T(8,128)} %get-tuple-element.30), kind=kOutput, calls=%fused_computation.25 | convolution fusion | flops 26050560 | bytes 1982464 | tf_op jit(solution)/shard_map/nhqk,nkhc->nqhc/dot_general | solution.py:18
  46.2 0.9 copy.116
  48.1 1.6 fusion.67
  50.8 1.4 fusion.14
  52.2 1.9 %collective-permute-start.4 = (bf16[2304,128]{1,0:T(8,128)(2,1)}, bf16[2304,128]{1,0:T(8,128)(2,1)}, u32[]{:S(2)}, u32[]{:S(2)}) collective-permute-start(bf16[2304,128]{1,0:T(8,128)(2,1)} %fusion.14), channel_id=1, source_target_pairs={{0,32},{32,0},{1,33},{33,1},{2,34},{34,2},{3,35},{35,3},{4,36},{36... | collective-permute-start | bytes 1769480 | tf_op jit(solution)/shard_map/ppermute | solution.py:134
  54.1 2.3 %collective-permute-done.4 = bf16[2304,128]{1,0:T(8,128)(2,1)} collective-permute-done((bf16[2304,128]{1,0:T(8,128)(2,1)}, bf16[2304,128]{1,0:T(8,128)(2,1)}, u32[]{:S(2)}, u32[]{:S(2)}) %collective-permute-start.4) | collective-permute-done | bytes 589856 | tf_op jit(solution)/shard_map/ppermute | solution.py:134
  56.4 1.5 fusion.17
  57.9 24.2 %all_to_all.20 = bf16[16,144,128]{2,1,0:T(8,128)(2,1)S(1)} all-to-all(bf16[16,144,128]{2,1,0:T(8,128)(2,1)S(1)} %bitcast.157), channel_id=1, replica_groups=mesh['zhi'=2,'x'=4,'core'=2,'zlo'=8,'y'=4] {'x','y'}, dimensions={0} | all-to-all | bytes 1179648 | tf_op jit(solution)/shard_map/all_to_all | solution.py:116
  82.2 22.6 %all_to_all.21 = bf16[16,9,128]{2,1,0:T(8,128)(2,1)S(1)} all-to-all(bf16[16,9,128]{2,1,0:T(8,128)(2,1)S(1)} %reshape.219), channel_id=1, replica_groups=mesh['zhi'=2,'x'=4,'core'=2,'zlo'=8,'y'=4] {'zhi','zlo'}, dimensions={0} | all-to-all | bytes 73728 | tf_op jit(solution)/shard_map/all_to_all | solution.py:116
  104.9 15.5 %all_to_all.22 = bf16[16,9,128]{2,1,0:T(8,128)(2,1)S(1)} all-to-all(bf16[16,9,128]{2,1,0:T(8,128)(2,1)S(1)} %broadcast_in_dim.20), channel_id=1, replica_groups=mesh['zhi'=2,'x'=4,'core'=2,'zlo'=8,'y'=4] {'zhi','zlo'}, dimensions={0} | all-to-all | bytes 73728 | tf_op jit(solution)/shard_map/all_to_all | solution.py:116
  120.5 0.9 broadcast_in_dim.22
  121.3 3.6 %all-to-all-start.3 = ((bf16[16,144,128]{2,1,0:T(8,128)(2,1)}), bf16[16,144,128]{2,1,0:T(8,128)(2,1)S(1)}, u32[]{:S(2)}, u32[]{:S(2)}) async-start(bf16[16,144,128]{2,1,0:T(8,128)(2,1)} %broadcast_in_dim.22), calls=%async_computation.3 | async-start | bytes 1179648 | tf_op jit(solution)/shard_map/all_to_all | solution.py:116
  125.9 9.4 %all-to-all-done.3 = bf16[16,144,128]{2,1,0:T(8,128)(2,1)S(1)} async-done(((bf16[16,144,128]{2,1,0:T(8,128)(2,1)}), bf16[16,144,128]{2,1,0:T(8,128)(2,1)S(1)}, u32[]{:S(2)}, u32[]{:S(2)}) %all-to-all-start.3) | async-done | bytes 589856 | tf_op jit(solution)/shard_map/all_to_all | solution.py:116
  135.3 1.9 %collective-permute-start.5 = (bf16[2304,128]{1,0:T(8,128)(2,1)S(1)}, bf16[2304,128]{1,0:T(8,128)(2,1)}, u32[]{:S(2)}, u32[]{:S(2)}) collective-permute-start(bf16[2304,128]{1,0:T(8,128)(2,1)S(1)} %bitcast.156), channel_id=1, source_target_pairs={{0,32},{32,0},{1,33},{33,1},{2,34},{34,2},{3,35},{35,3},{4,36},{36... | collective-permute-start | bytes 1769480 | tf_op jit(solution)/shard_map/ppermute | solution.py:141
  137.3 2.4 %collective-permute-start.2 = (bf16[1,2,4,16,384]{4,3,2,1,0:T(8,128)(2,1)S(1)}, bf16[1,2,4,16,384]{4,3,2,1,0:T(8,128)(2,1)S(1)}, u32[]{:S(2)}, u32[]{:S(2)}) collective-permute-start(bf16[1,2,4,16,384]{4,3,2,1,0:T(8,128)(2,1)S(1)} %get-tuple-element.28), channel_id=1, source_target_pairs={{480,0},{0,32},{32,64},{64,96},{96,128},{128,160},{160,192},{192,2... | collective-permute-start | bytes 294920 | tf_op jit(solution)/shard_map/ppermute | solution.py:14
  139.7 14.9 %collective-permute-done.2 = bf16[1,2,4,16,384]{4,3,2,1,0:T(8,128)(2,1)S(1)} collective-permute-done((bf16[1,2,4,16,384]{4,3,2,1,0:T(8,128)(2,1)S(1)}, bf16[1,2,4,16,384]{4,3,2,1,0:T(8,128)(2,1)S(1)}, u32[]{:S(2)}, u32[]{:S(2)}) %collective-permute-start.2) | collective-permute-done | bytes 98336 | tf_op jit(solution)/shard_map/ppermute | solution.py:14
  154.6 2.5 %collective-permute-start.3 = (bf16[1,2,8,4,384]{4,3,2,1,0:T(4,128)(2,1)S(1)}, bf16[1,2,8,4,384]{4,3,2,1,0:T(4,128)(2,1)S(1)}, u32[]{:S(2)}, u32[]{:S(2)}) collective-permute-start(bf16[1,2,8,4,384]{4,3,2,1,0:T(4,128)(2,1)S(1)} %pad_maximum_fusion.6), channel_id=1, source_target_pairs={{31,0},{0,1},{1,2},{2,3},{3,4},{4,5},{5,6},{6,7},{7,8},{8,9},{9,10... | collective-permute-start | bytes 147464 | tf_op jit(solution)/shard_map/ppermute | solution.py:14
  158.0 11.3 %collective-permute-done.3 = bf16[1,2,8,4,384]{4,3,2,1,0:T(4,128)(2,1)S(1)} collective-permute-done((bf16[1,2,8,4,384]{4,3,2,1,0:T(4,128)(2,1)S(1)}, bf16[1,2,8,4,384]{4,3,2,1,0:T(4,128)(2,1)S(1)}, u32[]{:S(2)}, u32[]{:S(2)}) %collective-permute-start.3) | collective-permute-done | bytes 49184 | tf_op jit(solution)/shard_map/ppermute | solution.py:14
  170.1 1.1 broadcast_select_fusion.1
  171.3 1.2 copy.126
  172.5 1.5 copy.129
  174.2 0.9 copy.130
  (101 shorter events, 11.3 us)
Async XLA Ops:
  0.6 28.8 %copy-start = (bf16[384,384]{1,0:T(8,128)(2,1)S(1)}, bf16[384,384]{1,0:T(8,128)(2,1)}, u32[]{:S(2)}) copy-start(bf16[384,384]{1,0:T(8,128)(2,1)} %param.11) | copy-start | bytes 884740
  1.7 13.1 %collective-permute-start = (bf16[2,2,8,4,384]{4,3,2,1,0:T(4,128)(2,1)S(1)}, bf16[2,2,8,4,384]{4,3,2,1,0:T(4,128)(2,1)S(1)}, u32[]{:S(2)}, u32[]{:S(2)}) collective-permute-start(bf16[2,2,8,4,384]{4,3,2,1,0:T(4,128)(2,1)S(1)} %pad_maximum_fusion.5), channel_id=1, source_target_pairs={{1,0},{2,1},{3,2},{4,3},{5,4},{6,5},{7,6},{8,7},{9,8},{10,9},{11,1... | collective-permute-start | bytes 294920 | tf_op jit(solution)/shard_map/ppermute | solution.py:14
  13.8 16.8 %copy-start.14 = (f32[384]{0:T(512)}, f32[384]{0:T(512)S(1)}, u32[]{:S(2)}) copy-start(f32[384]{0:T(512)S(1)} %convert_element_type.110) | copy-start | bytes 4612
  14.8 14.6 %copy-start.21 = (bf16[2]{0:T(256)(128)(2,1)}, bf16[2]{0:T(256)(128)(2,1)S(1)}, u32[]{:S(2)}) copy-start(bf16[2]{0:T(256)(128)(2,1)S(1)} %dynamic-slice_convert_fusion) | copy-start | bytes 16
  14.9 13.5 %collective-permute-start.1 = (bf16[2,2,4,16,384]{4,3,2,1,0:T(8,128)(2,1)S(1)}, bf16[2,2,4,16,384]{4,3,2,1,0:T(8,128)(2,1)S(1)}, u32[]{:S(2)}, u32[]{:S(2)}) collective-permute-start(bf16[2,2,4,16,384]{4,3,2,1,0:T(8,128)(2,1)S(1)} %get-tuple-element.27), channel_id=1, source_target_pairs={{32,0},{64,32},{96,64},{128,96},{160,128},{192,160},{224,192},{256... | collective-permute-start | bytes 589832 | tf_op jit(solution)/shard_map/ppermute | solution.py:14
  28.6 0.6 copy-start.12
  28.7 1.9 %copy-start.16 = (f32[2,128]{1,0:T(2,128)}, f32[2,128]{1,0:T(2,128)S(1)}, u32[]{:S(2)}) copy-start(f32[2,128]{1,0:T(2,128)S(1)} %div.41) | copy-start | bytes 3076
  28.8 1.8 %copy-start.1 = (bf16[384,1152]{1,0:T(8,128)(2,1)S(1)}, bf16[384,1152]{1,0:T(8,128)(2,1)}, u32[]{:S(2)}) copy-start(bf16[384,1152]{1,0:T(8,128)(2,1)} %param.10) | copy-start | bytes 2654212
  29.3 1.9 %copy-start.18 = (f32[2,128]{1,0:T(2,128)}, f32[2,128]{1,0:T(2,128)S(1)}, u32[]{:S(2)}) copy-start(f32[2,128]{1,0:T(2,128)S(1)} %rsqrt.13) | copy-start | bytes 3076
  31.5 2.4 %copy-start.5 = (bf16[2,128,1152]{1,2,0:T(8,128)(2,1)}, bf16[2,128,1152]{1,2,0:T(8,128)(2,1)S(1)}, u32[]{:S(2)}) copy-start(bf16[2,128,1152]{1,2,0:T(8,128)(2,1)S(1)} %copy.106) | copy-start | bytes 1769476
  33.9 1.6 copy-start.7
  33.9 1.7 copy-start.23
  33.9 1.7 copy-start.24
  43.4 2.6 %copy-start.22 = (bf16[2]{0:T(256)(128)(2,1)S(1)}, bf16[2]{0:T(256)(128)(2,1)}, u32[]{:S(2)}) copy-start(bf16[2]{0:T(256)(128)(2,1)} %copy-done.21) | copy-start | bytes 16
  43.4 2.7 %copy-start.8 = (bf16[2,128,1,12,32]{1,4,3,0,2:T(8,128)(2,1)S(1)}, bf16[2,128,1,12,32]{1,4,3,0,2:T(8,128)(2,1)}, u32[]{:S(2)}) copy-start(bf16[2,128,1,12,32]{1,4,3,0,2:T(8,128)(2,1)} %fusion.24) | copy-start | bytes 589828
  43.4 2.7 %copy-start.9 = (bf16[2,128,1,12,32]{1,4,3,0,2:T(8,128)(2,1)S(1)}, bf16[2,128,1,12,32]{1,4,3,0,2:T(8,128)(2,1)}, u32[]{:S(2)}) copy-start(bf16[2,128,1,12,32]{1,4,3,0,2:T(8,128)(2,1)} %fusion.25) | copy-start | bytes 589828
  43.4 2.7 %copy-start.10 = (bf16[2,128,1,12,32]{1,4,3,0,2:T(8,128)(2,1)S(1)}, bf16[2,128,1,12,32]{1,4,3,0,2:T(8,128)(2,1)}, u32[]{:S(2)}) copy-start(bf16[2,128,1,12,32]{1,4,3,0,2:T(8,128)(2,1)} %fusion.28) | copy-start | bytes 589828
  46.0 1.1 copy-start.13
  46.0 1.1 copy-start.15
  48.1 1.6 copy-start.6
  48.1 1.6 copy-start.11
  50.0 0.8 copy-start.3
  52.2 4.2 %collective-permute-start.4 = (bf16[2304,128]{1,0:T(8,128)(2,1)}, bf16[2304,128]{1,0:T(8,128)(2,1)}, u32[]{:S(2)}, u32[]{:S(2)}) collective-permute-start(bf16[2304,128]{1,0:T(8,128)(2,1)} %fusion.14), channel_id=1, source_target_pairs={{0,32},{32,0},{1,33},{33,1},{2,34},{34,2},{3,35},{35,3},{4,36},{36... | collective-permute-start | bytes 1769480 | tf_op jit(solution)/shard_map/ppermute | solution.py:134
  82.1 42.8 %copy-start.2 = (bf16[2,128,3,12,32]{1,4,3,2,0:T(8,128)(2,1)S(1)}, bf16[2,128,3,12,32]{1,4,3,2,0:T(8,128)(2,1)}, u32[]{:S(2)}) copy-start(bf16[2,128,3,12,32]{1,4,3,2,0:T(8,128)(2,1)} %copy.116) | copy-start | bytes 1769476
  82.1 42.8 %copy-start.17 = (f32[2,128]{1,0:T(2,128)S(1)}, f32[2,128]{1,0:T(2,128)}, u32[]{:S(2)}) copy-start(f32[2,128]{1,0:T(2,128)} %copy-done.16) | copy-start | bytes 3076
  82.1 42.8 %copy-start.19 = (f32[2,128]{1,0:T(2,128)S(1)}, f32[2,128]{1,0:T(2,128)}, u32[]{:S(2)}) copy-start(f32[2,128]{1,0:T(2,128)} %copy-done.18) | copy-start | bytes 3076
  121.3 14.0 %all-to-all-start.3 = ((bf16[16,144,128]{2,1,0:T(8,128)(2,1)}), bf16[16,144,128]{2,1,0:T(8,128)(2,1)S(1)}, u32[]{:S(2)}, u32[]{:S(2)}) async-start(bf16[16,144,128]{2,1,0:T(8,128)(2,1)} %broadcast_in_dim.22), calls=%async_computation.3 | async-start | bytes 1179648 | tf_op jit(solution)/shard_map/all_to_all | solution.py:116
  125.8 43.5 %copy-start.4 = (bf16[2,8,16,384]{3,2,1,0:T(8,128)(2,1)S(1)}, bf16[2,8,16,384]{3,2,1,0:T(8,128)(2,1)}, u32[]{:S(2)}) copy-start(bf16[2,8,16,384]{3,2,1,0:T(8,128)(2,1)} %param.7) | copy-start | bytes 589828
  135.3 34.7 %collective-permute-start.5 = (bf16[2304,128]{1,0:T(8,128)(2,1)S(1)}, bf16[2304,128]{1,0:T(8,128)(2,1)}, u32[]{:S(2)}, u32[]{:S(2)}) collective-permute-start(bf16[2304,128]{1,0:T(8,128)(2,1)S(1)} %bitcast.156), channel_id=1, source_target_pairs={{0,32},{32,0},{1,33},{33,1},{2,34},{34,2},{3,35},{35,3},{4,36},{36... | collective-permute-start | bytes 1769480 | tf_op jit(solution)/shard_map/ppermute | solution.py:141
  137.3 17.3 %collective-permute-start.2 = (bf16[1,2,4,16,384]{4,3,2,1,0:T(8,128)(2,1)S(1)}, bf16[1,2,4,16,384]{4,3,2,1,0:T(8,128)(2,1)S(1)}, u32[]{:S(2)}, u32[]{:S(2)}) collective-permute-start(bf16[1,2,4,16,384]{4,3,2,1,0:T(8,128)(2,1)S(1)} %get-tuple-element.28), channel_id=1, source_target_pairs={{480,0},{0,32},{32,64},{64,96},{96,128},{128,160},{160,192},{192,2... | collective-permute-start | bytes 294920 | tf_op jit(solution)/shard_map/ppermute | solution.py:14
  154.6 14.7 %collective-permute-start.3 = (bf16[1,2,8,4,384]{4,3,2,1,0:T(4,128)(2,1)S(1)}, bf16[1,2,8,4,384]{4,3,2,1,0:T(4,128)(2,1)S(1)}, u32[]{:S(2)}, u32[]{:S(2)}) collective-permute-start(bf16[1,2,8,4,384]{4,3,2,1,0:T(4,128)(2,1)S(1)} %pad_maximum_fusion.6), channel_id=1, source_target_pairs={{31,0},{0,1},{1,2},{2,3},{3,4},{4,5},{5,6},{6,7},{7,8},{8,9},{9,10... | collective-permute-start | bytes 147464 | tf_op jit(solution)/shard_map/ppermute | solution.py:14
  174.0 1.5 copy-start.20

commit v2 on v0

v2 whole, which is shorter than its diff:
```python
import functools

import jax
import jax.numpy as jnp
import numpy as np
from jax import lax
from jax.experimental import pallas as pl
from jax.experimental.pallas import tpu as pltpu
from jax.sharding import Mesh
from jax.sharding import PartitionSpec as P

HEADS = 12
HDIM = 32
PACK = 4
LANES = 128
WIN = 128
LAT = ("zhi", "x", "core")
LON = ("zlo", "y")
PLANE = ("x", "y")
RING = ("zhi", "zlo")
F32 = jnp.float32
BF16 = jnp.bfloat16


def dot(left, right):
    return jnp.dot(left, right, preferred_element_type=F32)


def dot_nt(left, right):
    return lax.dot_general(left, right, (((1,), (1,)), ((), ())), preferred_element_type=F32)


def call(kernel, outs, *args, scalars=(), scratch=()):
    specs = [pl.BlockSpec(memory_space=pltpu.SMEM)] * len(scalars)
    specs += [pl.BlockSpec(memory_space=pltpu.VMEM)] * len(args)
    return pl.pallas_call(
        kernel,
        out_shape=[jax.ShapeDtypeStruct(s, d) for s, d in outs],
        in_specs=specs,
        out_specs=[pl.BlockSpec(memory_space=pltpu.VMEM)] * len(outs),
        scratch_shapes=scratch,
        compiler_params=pltpu.CompilerParams(vmem_limit_bytes=40 * 1024 * 1024),
    )(*scalars, *args)


def pick_matrix():
    pick = np.zeros((2 * WIN, 320), np.float32)
    for w in range(2):
        for level in range(2):
            for r in range(8):
                for c in range(8):
                    col, row, below = 4 + 8 * w + c, r % 4, r // 4
                    if col < 16:
                        source = 128 * below + level * 64 + row * 16 + col
                    else:
                        source = 256 + 32 * below + level * 16 + row * 4 + col - 16
                    pick[w * WIN + level * 64 + r * 8 + c, source] = 1
    return pick


def corner_matrix():
    corner = np.zeros((32, 128), np.float32)
    for row in range(8):
        for col in range(4):
            corner[row * 4 + col, row * 16 + col] = 1
    return corner


def send_kernel(tok, cot, corner, lat_out, lon_out, diag_out):
    pick = corner[...]
    for i, ref in enumerate((tok, cot)):
        upper = ref[:, 0:4].reshape(WIN, -1)
        lower = ref[:, 4:8].reshape(WIN, -1)
        lat_out[i * WIN : (i + 1) * WIN] = upper
        lon_out[i * 32 : (i + 1) * 32] = dot(pick, lower).astype(BF16)
        diag_out[i * 32 : (i + 1) * 32] = dot(pick, upper).astype(BF16)


def window_kernel(
    meta, tok, cot, lat, lon, diag, pick, put, gain, w_qkv, w_out,
    grads, own_back, lat_back, lon_back, diag_back,
    left, right, packed, d_att,
):
    dim = w_out.shape[0]
    scale = HDIM ** (-0.5)
    gains = gain[...].astype(F32)

    def assembled(i, ref):
        return (
            dot(pick[:, 0:128], ref[:, 4:8].reshape(WIN, dim))
            + dot(pick[:, 128:256], lat[i * WIN : (i + 1) * WIN])
            + dot(pick[:, 256:288], lon[i * 32 : (i + 1) * 32])
            + dot(pick[:, 288:320], diag[i * 32 : (i + 1) * 32])
        )

    x = assembled(0, tok)
    in_first = lax.broadcasted_iota(jnp.int32, (2 * WIN, 1), 0) < WIN
    ocean = jnp.where(in_first, meta[0], meta[1]).astype(F32)
    g = (assembled(1, cot) * ocean).astype(BF16)
    centered = x - jnp.mean(x, -1, keepdims=True)
    rstd = lax.rsqrt(jnp.mean(centered * centered, -1, keepdims=True) + 1e-5)
    xhat = centered * rstd
    normed_full = xhat * gains
    normed = normed_full.astype(BF16)
    left[0] = normed_full.T.astype(BF16)
    packed[...] = dot(normed, w_qkv[...]).astype(BF16)
    d_att[...] = dot_nt(g, w_out[...]).astype(BF16)
    for j in range(dim // LANES):
        right[9 + j] = g[:, j * LANES : (j + 1) * LANES]

    lane = lax.broadcasted_iota(jnp.int32, (1, LANES), 1)
    masks = [(lane // HDIM == h).astype(F32).astype(BF16) for h in range(PACK)]
    key_row = lax.broadcasted_iota(jnp.int32, (WIN, PACK * WIN), 0) // 8 % 8 >= 4
    query_row = lax.broadcasted_iota(jnp.int32, (WIN, PACK * WIN), 1) // 8 % 8 >= 4
    differ = (key_row != query_row).astype(jnp.int32) * meta[2] > 0

    for w in range(2):
        rows = slice(w * WIN, (w + 1) * WIN)
        for group in range(HEADS // PACK):
            cols = [slice(p * dim + group * LANES, p * dim + (group + 1) * LANES) for p in range(3)]
            query, keys, values = packed[rows, cols[0]], packed[rows, cols[1]], packed[rows, cols[2]]
            d_out = d_att[rows, cols[0]]
            query_heads = jnp.concatenate([query * m for m in masks], 0)
            d_out_heads = jnp.concatenate([d_out * m for m in masks], 0)
            scores = jnp.where(differ, -1e30, dot_nt(keys, query_heads) * scale)
            expo = jnp.exp(scores - jnp.max(scores, 0, keepdims=True))
            probs = expo / jnp.sum(expo, 0, keepdims=True)
            weights = probs.astype(BF16)
            d_probs = dot_nt(values, d_out_heads)
            inner = jnp.sum(d_probs * probs, 0, keepdims=True)
            d_scores = (probs * (d_probs - inner) * scale).astype(BF16)
            values_t = values.T
            keys_t = keys.T
            att_t, d_query_t = [], []
            for h in range(PACK):
                span = slice(h * WIN, (h + 1) * WIN)
                feats = slice(h * HDIM, (h + 1) * HDIM)
                att_t.append(dot(values_t[feats], weights[:, span]))
                d_query_t.append(dot(keys_t[feats], d_scores[:, span]))
            att_rows = slice(group * LANES, (group + 1) * LANES)
            left[1, att_rows, rows] = jnp.concatenate(att_t, 0).astype(BF16)
            right[group, rows] = jnp.concatenate(d_query_t, 0).T.astype(BF16)
            right[3 + group, rows] = dot(d_scores, query_heads).astype(BF16)
            right[6 + group, rows] = dot(weights, d_out_heads).astype(BF16)

    for j in range(12):
        half, at = j // 6, j % 6
        slot = lax.rem(half + meta[3], 2)
        term = dot(left[j // 9], right[j])
        grads[slot, at * dim : (at + 1) * dim] = term.astype(BF16)

    d_packed = jnp.concatenate([right[j] for j in range(9)], 1)
    d_normed = dot_nt(d_packed, w_qkv[...])
    d_hat = d_normed * gains
    branch = rstd * (
        d_hat
        - jnp.mean(d_hat, -1, keepdims=True)
        - xhat * jnp.mean(d_hat * xhat, -1, keepdims=True)
    )
    back = dot(put[...], branch.astype(BF16)).astype(BF16)
    own_back[...] = back[0:128]
    lat_back[...] = back[128:256]
    lon_back[...] = back[256:288]
    diag_back[...] = back[288:320]


def token_kernel(cot, own, lat, lon, diag, spread, out):
    fill = spread[...]
    lower = own[...].astype(F32) + dot(fill, lon[...])
    upper = lat[...].astype(F32) + dot(fill, diag[...])
    shape = (2, 4) + cot.shape[2:]
    out[:, 0:4] = (cot[:, 0:4].astype(F32) + upper.reshape(shape)).astype(BF16)
    out[:, 4:8] = (cot[:, 4:8].astype(F32) + lower.reshape(shape)).astype(BF16)


def result_kernel(meta, mine, other, gain, w_qkv, qkv_out, out_out, gain_out):
    dim = out_out.shape[0]

    def write(halves):
        along = jnp.zeros((dim, LANES), F32)
        for j in range(12):
            at = (j % 6) * dim
            block = halves[j // 6][at : at + dim]
            if j < 9:
                cols = slice(j * LANES, (j + 1) * LANES)
                qkv_out[:, cols] = block
                along = along + w_qkv[:, cols].astype(F32) * block.astype(F32)
            else:
                out_out[:, (j - 9) * LANES : (j - 8) * LANES] = block
        total = jnp.sum(along.T, 0, keepdims=True)
        gain_out[...] = (total / gain[...].astype(F32)).astype(BF16)

    @pl.when(meta[3] == 0)
    def _():
        write((mine, other))

    @pl.when(meta[3] != 0)
    def _():
        write((other, mine))


def exchange(parts, axis):
    return lax.all_to_all(parts, axis, 0, 0, tiled=False)


def summed(parts):
    return jnp.sum(parts.astype(F32), 0).astype(BF16)


def spread_along(part, axis):
    parts = jnp.broadcast_to(part[None], (lax.axis_size(axis),) + part.shape)
    return exchange(parts, axis)


def swapped(array):
    return lax.ppermute(array, "core", [(0, 1), (1, 0)])


def reduced(grads):
    half = grads.shape[1]
    mine = (grads[0].astype(F32) + swapped(grads[1]).astype(F32)).astype(BF16)
    mine = summed(exchange(mine.reshape(16, half // 16, LANES), PLANE))
    mine = summed(exchange(mine.reshape(16, half // 256, LANES), RING))
    mine = spread_along(mine, RING).reshape(half // 16, LANES)
    mine = spread_along(mine, PLANE).reshape(half, LANES)
    return mine, swapped(mine)


def local(tokens, cotangent, ocean_mask, gain, w_qkv, w_out):
    dim = w_out.shape[0]
    n_lat, n_lon = lax.axis_size(LAT), lax.axis_size(LON)
    lat_index, core = lax.axis_index(LAT), lax.axis_index("core")
    ocean = lax.dynamic_slice_in_dim(ocean_mask, lat_index, 1, 0).reshape(2)
    flags = jnp.stack([(lat_index == n_lat - 1).astype(jnp.int32), core.astype(jnp.int32)])
    meta = jnp.concatenate([ocean, flags])
    gain_row = gain.reshape(1, dim)
    corner = corner_matrix()
    pick = pick_matrix()
    constant = functools.partial(jnp.asarray, dtype=BF16)

    def from_next(array, axis, size):
        return lax.ppermute(array, axis, [((i + 1) % size, i) for i in range(size)])

    def to_next(array, axis, size):
        return lax.ppermute(array, axis, [(i, (i + 1) % size) for i in range(size)])

    def place_of(a, b):
        return (a % n_lat) * n_lon + b % n_lon

    pairs = [(place_of(a + 1, b + 1), place_of(a, b)) for a in range(n_lat) for b in range(n_lon)]
    send = [((2 * WIN, dim), BF16), ((64, dim), BF16), ((64, dim), BF16)]
    lat, lon, diag = call(send_kernel, send, tokens, cotangent, constant(corner))
    lat = from_next(lat, LAT, n_lat)
    diag = lax.ppermute(diag, LAT + LON, pairs)
    lon = from_next(lon, LON, n_lon)

    backs = [((n, dim), BF16) for n in (WIN, WIN, 32, 32)]
    grads, own_back, lat_back, lon_back, diag_back = call(
        window_kernel, [((2, 6 * dim, LANES), BF16)] + backs,
        tokens, cotangent, lat, lon, diag, constant(pick), constant(pick.T), gain_row, w_qkv, w_out,
        scalars=(meta,),
        scratch=[
            pltpu.VMEM((2, dim, 2 * WIN), BF16),
            pltpu.VMEM((12, 2 * WIN, LANES), BF16),
            pltpu.VMEM((2 * WIN, 3 * dim), BF16),
            pltpu.VMEM((2 * WIN, dim), BF16),
        ],
    )
    lat_back = to_next(lat_back, LAT, n_lat)
    diag_back = lax.ppermute(diag_back, LAT + LON, [(b, a) for a, b in pairs])
    lon_back = to_next(lon_back, LON, n_lon)
    mine, other = reduced(grads)
    (token_grad,) = call(
        token_kernel, [(tokens.shape, BF16)],
        cotangent, own_back, lat_back, lon_back, diag_back, constant(corner.T),
    )
    qkv_grad, out_grad, gain_grad = call(
        result_kernel, [(w_qkv.shape, BF16), (w_out.shape, BF16), ((1, dim), BF16)],
        mine, other, gain_row, w_qkv,
        scalars=(meta,),
    )
    return token_grad, qkv_grad, out_grad, gain_grad.reshape(dim)


def solution(mesh):
    fine = Mesh(mesh.devices.reshape(2, 4, 2, 8, 4), ("zhi", "x", "core", "zlo", "y"))
    tiles = P(None, LAT, LON, None)
    return jax.shard_map(
        local,
        mesh=fine,
        in_specs=(tiles, tiles, P(None, LON), P(), P(), P()),
        out_specs=(tiles, P(), P(), P()),
        check_vma=False,
    )
```

time: 260 us -> 152 us (0.58)
  the two profiles are of different devices: /device:TPU:1 before, /device:TPU:32 now
where the time goes in v2:
time: 152 us; the launch traced here: 151 us
  blocking collectives  72.7 us (48%)
  starting transfers between devices  34.6 us (23%)
  waiting for transfers between devices  24.4 us (16%)
  local copies, waits for them, and re-layouts  9.46 us (6%)
  Pallas kernels  8.43 us (6%)
    all_to_all x4, blocking collectives, exchange(): return lax.all_to_all(parts, axis, 0, 0, tiled=False)  72.7 us
    ppermute x2, starting transfers between devices, from_next(): return lax.ppermute(array, axis, [((i + 1) % size, i) for i in range(size)])  21.8 us
    ppermute x1, waiting for transfers between devices, local(): diag_back = lax.ppermute(diag_back, LAT + LON, [(b, a) for a, b in pairs])  13.4 us
    pallas_call x4, Pallas kernels, call(): pl.pallas_call(kernel, out_shape=[jax.ShapeDtypeStruct(s, d) for s, d in...  8.43 us
    unnamed x26, local copies, waits for them, and re-layouts  8.4 us
    ppermute x2, starting transfers between devices, to_next(): return lax.ppermute(array, axis, [(i, (i + 1) % size) for i in range(size)])  4.88 us
    ppermute x2, starting transfers between devices, swapped(): return lax.ppermute(array, 'core', [(0, 1), (1, 0)])  3.83 us
    ppermute x1, waiting for transfers between devices, local(): diag = lax.ppermute(diag, LAT + LON, pairs)  3.6 us
  transfers between devices with their start and end apart: 8, of which 5 were waited for; matrix products, arithmetic and copies ran while one was open for 1% of the time, Pallas kernels for 1%

profile of v2, /device:TPU:32, one launch (start us, length us, event | category | flops | bytes accessed | tf_op | source)
XLA Modules:
  0.0 151.3 jit_solution(14753661656617917733)
XLA Ops:
  0.7 0.9 copy-done.3
  1.6 0.9 copy-done.6
  2.5 0.7 copy-done.12
  3.4 16.5 %collective-permute-start = (bf16[256,384]{1,0:T(8,128)(2,1)S(1)}, bf16[256,384]{1,0:T(8,128)(2,1)S(1)}, u32[]{:S(2)}, u32[]{:S(2)}) collective-permute-start(bf16[256,384]{1,0:T(8,128)(2,1)S(1)} %get-tuple-element.15), channel_id=1, source_target_pairs={{32,0},{64,32},{96,64},{128,96},{160,128},{192,160},{224,192},{256... | collective-permute-start | bytes 589832 | tf_op jit(solution)/shard_map/ppermute | solution.py:242
  19.9 5.4 %collective-permute-start.1 = (bf16[64,384]{1,0:T(8,128)(2,1)S(1)}, bf16[64,384]{1,0:T(8,128)(2,1)S(1)}, u32[]{:S(2)}, u32[]{:S(2)}) collective-permute-start(bf16[64,384]{1,0:T(8,128)(2,1)S(1)} %get-tuple-element.16), channel_id=1, source_target_pairs={{1,0},{2,1},{3,2},{4,3},{5,4},{6,5},{7,6},{8,7},{9,8},{10,9},{11,1... | collective-permute-start | bytes 147464 | tf_op jit(solution)/shard_map/ppermute | solution.py:242
  25.2 1.9 %collective-permute-start.2 = (bf16[64,384]{1,0:T(8,128)(2,1)S(1)}, bf16[64,384]{1,0:T(8,128)(2,1)S(1)}, u32[]{:S(2)}, u32[]{:S(2)}) collective-permute-start(bf16[64,384]{1,0:T(8,128)(2,1)S(1)} %get-tuple-element.17), channel_id=1, source_target_pairs={{33,0},{34,1},{35,2},{36,3},{37,4},{38,5},{39,6},{40,7},{41,8},{42... | collective-permute-start | bytes 147464 | tf_op jit(solution)/shard_map/ppermute | solution.py:254
  27.2 0.2 dynamic-slice_reduce_fusion
  27.4 0.7 reshape.31.gain
  28.1 2.3 %collective-permute-done.1.lon = bf16[64,384]{1,0:T(8,128)(2,1)S(1)} collective-permute-done((bf16[64,384]{1,0:T(8,128)(2,1)S(1)}, bf16[64,384]{1,0:T(8,128)(2,1)S(1)}, u32[]{:S(2)}, u32[]{:S(2)}) %collective-permute-start.1) | collective-permute-done | bytes 49184 | tf_op jit(solution)/shard_map/ppermute | solution.py:242
  30.4 3.6 %collective-permute-done.2.diag = bf16[64,384]{1,0:T(8,128)(2,1)S(1)} collective-permute-done((bf16[64,384]{1,0:T(8,128)(2,1)S(1)}, bf16[64,384]{1,0:T(8,128)(2,1)S(1)}, u32[]{:S(2)}, u32[]{:S(2)}) %collective-permute-start.2) | collective-permute-done | bytes 49184 | tf_op jit(solution)/shard_map/ppermute | solution.py:254
  34.0 1.2 copy-done.1
  35.2 0.9 copy-done.4
  36.1 0.9 copy-done.7
  37.0 1.0 copy-done.8
  38.0 0.9 copy-done.9
  38.9 0.9 copy-done.10
  39.8 5.4 %shard_map.130 = (bf16[2,2304,128]{2,1,0:T(8,128)(2,1)S(1)}, bf16[128,384]{1,0:T(8,128)(2,1)S(1)}, bf16[128,384]{1,0:T(8,128)(2,1)S(1)}, bf16[32,384]{1,0:T(8,128)(2,1)S(1)}, bf16[32,384]{1,0:T(8,128)(2,1)S(1)}) custom-call(s32[4]{0:T(128)S(1)} %pad_add_fusion.meta, bf16[2,8,16,384]{3,2,1,0:T(8,128)(2,1)S(1)} %copy-done.7, ...), custom_call_target="tpu_custom_call" | custom-call | tf_op jit(solution)/shard_map/pallas_call | solution.py:36
  45.3 1.9 %collective-permute-start.6 = (bf16[2304,128]{1,0:T(8,128)(2,1)S(1)}, bf16[2304,128]{1,0:T(8,128)(2,1)S(1)}, u32[]{:S(2)}, u32[]{:S(2)}) collective-permute-start(bf16[2304,128]{1,0:T(8,128)(2,1)S(1)} %slice_bitcast_fusion), channel_id=1, source_target_pairs={{0,32},{32,0},{1,33},{33,1},{2,34},{34,2},{3,35},{35,3},{4,36},{36... | collective-permute-start | bytes 1769480 | tf_op jit(solution)/shard_map/ppermute | solution.py:216
  47.2 2.0 %collective-permute-done.6 = bf16[2304,128]{1,0:T(8,128)(2,1)S(1)} collective-permute-done((bf16[2304,128]{1,0:T(8,128)(2,1)S(1)}, bf16[2304,128]{1,0:T(8,128)(2,1)S(1)}, u32[]{:S(2)}, u32[]{:S(2)}) %collective-permute-start.6) | collective-permute-done | bytes 589856 | tf_op jit(solution)/shard_map/ppermute | solution.py:216
  49.4 15.4 %all_to_all.20 = bf16[16,144,128]{2,1,0:T(8,128)(2,1)S(1)} all-to-all(bf16[16,144,128]{2,1,0:T(8,128)(2,1)S(1)} %bitcast.11), channel_id=1, replica_groups=mesh['zhi'=2,'x'=4,'core'=2,'zlo'=8,'y'=4] {'x','y'}, dimensions={0} | all-to-all | bytes 1179648 | tf_op jit(solution)/shard_map/all_to_all | solution.py:203
  64.9 27.9 %all_to_all.21 = bf16[16,9,128]{2,1,0:T(8,128)(2,1)S(1)} all-to-all(bf16[16,9,128]{2,1,0:T(8,128)(2,1)S(1)} %reshape.33), channel_id=1, replica_groups=mesh['zhi'=2,'x'=4,'core'=2,'zlo'=8,'y'=4] {'zhi','zlo'}, dimensions={0} | all-to-all | bytes 73728 | tf_op jit(solution)/shard_map/all_to_all | solution.py:203
  92.8 15.6 %all_to_all.22 = bf16[16,9,128]{2,1,0:T(8,128)(2,1)S(1)} all-to-all(bf16[16,9,128]{2,1,0:T(8,128)(2,1)S(1)} %broadcast_in_dim.6), channel_id=1, replica_groups=mesh['zhi'=2,'x'=4,'core'=2,'zlo'=8,'y'=4] {'zhi','zlo'}, dimensions={0} | all-to-all | bytes 73728 | tf_op jit(solution)/shard_map/all_to_all | solution.py:203
  108.5 13.8 %all_to_all.23 = bf16[16,144,128]{2,1,0:T(8,128)(2,1)S(1)} all-to-all(bf16[16,144,128]{2,1,0:T(8,128)(2,1)S(1)} %broadcast_in_dim.15), channel_id=1, replica_groups=mesh['zhi'=2,'x'=4,'core'=2,'zlo'=8,'y'=4] {'x','y'}, dimensions={0} | all-to-all | bytes 1179648 | tf_op jit(solution)/shard_map/all_to_all | solution.py:203
  122.4 1.9 %collective-permute-start.7 = (bf16[2304,128]{1,0:T(8,128)(2,1)S(1)}, bf16[2304,128]{1,0:T(8,128)(2,1)S(1)}, u32[]{:S(2)}, u32[]{:S(2)}) collective-permute-start(bf16[2304,128]{1,0:T(8,128)(2,1)S(1)} %bitcast.9), channel_id=1, source_target_pairs={{0,32},{32,0},{1,33},{33,1},{2,34},{34,2},{3,35},{35,3},{4,36},{36... | collective-permute-start | bytes 1769480 | tf_op jit(solution)/shard_map/ppermute | solution.py:216
  124.3 2.4 %collective-permute-start.3 = (bf16[128,384]{1,0:T(8,128)(2,1)S(1)}, bf16[128,384]{1,0:T(8,128)(2,1)S(1)}, u32[]{:S(2)}, u32[]{:S(2)}) collective-permute-start(bf16[128,384]{1,0:T(8,128)(2,1)S(1)} %get-tuple-element.19), channel_id=1, source_target_pairs={{0,32},{32,64},{64,96},{96,128},{128,160},{160,192},{192,224},{224... | collective-permute-start | bytes 294920 | tf_op jit(solution)/shard_map/ppermute | solution.py:245
  126.7 2.5 %collective-permute-start.4 = (bf16[32,384]{1,0:T(8,128)(2,1)S(1)}, bf16[32,384]{1,0:T(8,128)(2,1)S(1)}, u32[]{:S(2)}, u32[]{:S(2)}) collective-permute-start(bf16[32,384]{1,0:T(8,128)(2,1)S(1)} %get-tuple-element.20), channel_id=1, source_target_pairs={{0,1},{1,2},{2,3},{3,4},{4,5},{5,6},{6,7},{7,8},{8,9},{9,10},{10,1... | collective-permute-start | bytes 73736 | tf_op jit(solution)/shard_map/ppermute | solution.py:245
  129.2 2.2 %collective-permute-start.5 = (bf16[32,384]{1,0:T(8,128)(2,1)S(1)}, bf16[32,384]{1,0:T(8,128)(2,1)S(1)}, u32[]{:S(2)}, u32[]{:S(2)}) collective-permute-start(bf16[32,384]{1,0:T(8,128)(2,1)S(1)} %get-tuple-element.21), channel_id=1, source_target_pairs={{0,33},{1,34},{2,35},{3,36},{4,37},{5,38},{6,39},{7,40},{8,41},{9,... | collective-permute-start | bytes 73736 | tf_op jit(solution)/shard_map/ppermute | solution.py:270
  131.3 3.2 %collective-permute-done.4.lon = bf16[32,384]{1,0:T(8,128)(2,1)S(1)} collective-permute-done((bf16[32,384]{1,0:T(8,128)(2,1)S(1)}, bf16[32,384]{1,0:T(8,128)(2,1)S(1)}, u32[]{:S(2)}, u32[]{:S(2)}) %collective-permute-start.4) | collective-permute-done | bytes 24608 | tf_op jit(solution)/shard_map/ppermute | solution.py:245
  134.5 13.4 %collective-permute-done.5.diag = bf16[32,384]{1,0:T(8,128)(2,1)S(1)} collective-permute-done((bf16[32,384]{1,0:T(8,128)(2,1)S(1)}, bf16[32,384]{1,0:T(8,128)(2,1)S(1)}, u32[]{:S(2)}, u32[]{:S(2)}) %collective-permute-start.5) | collective-permute-done | bytes 24608 | tf_op jit(solution)/shard_map/ppermute | solution.py:270
  147.9 0.9 shard_map.131
  148.8 1.9 %shard_map.132 = (bf16[384,1152]{1,0:T(8,128)(2,1)}, bf16[384,384]{1,0:T(8,128)(2,1)}, bf16[1,384]{1,0:T(2,128)(2,1)S(1)}) custom-call(s32[4]{0:T(128)S(1)} %pad_add_fusion.meta, bf16[2304,128]{1,0:T(8,128)(2,1)S(1)} %bitcast.10, bf16[2304,128]{1,0:T(8,128)(2,1)S(1)} %collective-permute-done.7.other, bf16[1,384]{1,0:T(2,128)(2,1)S(1)} %reshape.31.gain, ...), custom_call_target="tpu_custom_call" | custom-call | tf_op jit(solution)/shard_map/pallas_call | solution.py:36
  150.8 0.6 reduce.3
  (30 shorter events, 0.8 us)
Async XLA Ops:
  0.6 26.5 %copy-start = (s32[16,2]{0,1:T(2,128)S(1)}, s32[16,2]{0,1:T(2,128)}, u32[]{:S(2)}) copy-start(s32[16,2]{0,1:T(2,128)} %param.12) | copy-start | bytes 388
  0.6 0.9 copy-start.3
  1.6 0.9 copy-start.6
  2.5 0.7 copy-start.12
  3.4 30.6 %collective-permute-start = (bf16[256,384]{1,0:T(8,128)(2,1)S(1)}, bf16[256,384]{1,0:T(8,128)(2,1)S(1)}, u32[]{:S(2)}, u32[]{:S(2)}) collective-permute-start(bf16[256,384]{1,0:T(8,128)(2,1)S(1)} %get-tuple-element.15), channel_id=1, source_target_pairs={{32,0},{64,32},{96,64},{128,96},{160,128},{192,160},{224,192},{256... | collective-permute-start | bytes 589832 | tf_op jit(solution)/shard_map/ppermute | solution.py:242
  19.9 10.5 %collective-permute-start.1 = (bf16[64,384]{1,0:T(8,128)(2,1)S(1)}, bf16[64,384]{1,0:T(8,128)(2,1)S(1)}, u32[]{:S(2)}, u32[]{:S(2)}) collective-permute-start(bf16[64,384]{1,0:T(8,128)(2,1)S(1)} %get-tuple-element.16), channel_id=1, source_target_pairs={{1,0},{2,1},{3,2},{4,3},{5,4},{6,5},{7,6},{8,7},{9,8},{10,9},{11,1... | collective-permute-start | bytes 147464 | tf_op jit(solution)/shard_map/ppermute | solution.py:242
  25.2 8.8 %collective-permute-start.2 = (bf16[64,384]{1,0:T(8,128)(2,1)S(1)}, bf16[64,384]{1,0:T(8,128)(2,1)S(1)}, u32[]{:S(2)}, u32[]{:S(2)}) collective-permute-start(bf16[64,384]{1,0:T(8,128)(2,1)S(1)} %get-tuple-element.17), channel_id=1, source_target_pairs={{33,0},{34,1},{35,2},{36,3},{37,4},{38,5},{39,6},{40,7},{41,8},{42... | collective-permute-start | bytes 147464 | tf_op jit(solution)/shard_map/ppermute | solution.py:254
  34.0 1.2 copy-start.1
  35.2 0.9 copy-start.4
  36.1 0.9 copy-start.7
  37.0 1.0 copy-start.8
  38.0 0.9 copy-start.9
  38.9 0.9 copy-start.10
  45.3 3.9 %collective-permute-start.6 = (bf16[2304,128]{1,0:T(8,128)(2,1)S(1)}, bf16[2304,128]{1,0:T(8,128)(2,1)S(1)}, u32[]{:S(2)}, u32[]{:S(2)}) collective-permute-start(bf16[2304,128]{1,0:T(8,128)(2,1)S(1)} %slice_bitcast_fusion), channel_id=1, source_target_pairs={{0,32},{32,0},{1,33},{33,1},{2,34},{34,2},{3,35},{35,3},{4,36},{36... | collective-permute-start | bytes 1769480 | tf_op jit(solution)/shard_map/ppermute | solution.py:216
  64.9 83.1 %copy-start.5 = (bf16[2,8,16,384]{3,2,1,0:T(8,128)(2,1)S(1)}, bf16[2,8,16,384]{3,2,1,0:T(8,128)(2,1)}, u32[]{:S(2)}) copy-start(bf16[2,8,16,384]{3,2,1,0:T(8,128)(2,1)} %cot.5) | copy-start | bytes 589828
  64.9 83.1 %copy-start.11 = (bf16[128,32]{1,0:T(8,128)(2,1)S(1)}, bf16[128,32]{1,0:T(8,128)(2,1)}, u32[]{:S(2)}) copy-start(bf16[128,32]{1,0:T(8,128)(2,1)} %constant.41.clone.spread) | copy-start | bytes 24580
  108.4 40.4 %copy-start.2 = (bf16[384,1152]{1,0:T(8,128)(2,1)S(1)}, bf16[384,1152]{1,0:T(8,128)(2,1)}, u32[]{:S(2)}) copy-start(bf16[384,1152]{1,0:T(8,128)(2,1)} %w_qkv.3) | copy-start | bytes 2654212
  122.4 26.4 %collective-permute-start.7 = (bf16[2304,128]{1,0:T(8,128)(2,1)S(1)}, bf16[2304,128]{1,0:T(8,128)(2,1)S(1)}, u32[]{:S(2)}, u32[]{:S(2)}) collective-permute-start(bf16[2304,128]{1,0:T(8,128)(2,1)S(1)} %bitcast.9), channel_id=1, source_target_pairs={{0,32},{32,0},{1,33},{33,1},{2,34},{34,2},{3,35},{35,3},{4,36},{36... | collective-permute-start | bytes 1769480 | tf_op jit(solution)/shard_map/ppermute | solution.py:216
  124.3 23.7 %collective-permute-start.3 = (bf16[128,384]{1,0:T(8,128)(2,1)S(1)}, bf16[128,384]{1,0:T(8,128)(2,1)S(1)}, u32[]{:S(2)}, u32[]{:S(2)}) collective-permute-start(bf16[128,384]{1,0:T(8,128)(2,1)S(1)} %get-tuple-element.19), channel_id=1, source_target_pairs={{0,32},{32,64},{64,96},{96,128},{128,160},{160,192},{192,224},{224... | collective-permute-start | bytes 294920 | tf_op jit(solution)/shard_map/ppermute | solution.py:245
  126.7 7.8 %collective-permute-start.4 = (bf16[32,384]{1,0:T(8,128)(2,1)S(1)}, bf16[32,384]{1,0:T(8,128)(2,1)S(1)}, u32[]{:S(2)}, u32[]{:S(2)}) collective-permute-start(bf16[32,384]{1,0:T(8,128)(2,1)S(1)} %get-tuple-element.20), channel_id=1, source_target_pairs={{0,1},{1,2},{2,3},{3,4},{4,5},{5,6},{6,7},{7,8},{8,9},{9,10},{10,1... | collective-permute-start | bytes 73736 | tf_op jit(solution)/shard_map/ppermute | solution.py:245
  129.2 18.8 %collective-permute-start.5 = (bf16[32,384]{1,0:T(8,128)(2,1)S(1)}, bf16[32,384]{1,0:T(8,128)(2,1)S(1)}, u32[]{:S(2)}, u32[]{:S(2)}) collective-permute-start(bf16[32,384]{1,0:T(8,128)(2,1)S(1)} %get-tuple-element.21), channel_id=1, source_target_pairs={{0,33},{1,34},{2,35},{3,36},{4,37},{5,38},{6,39},{7,40},{8,41},{9,... | collective-permute-start | bytes 73736 | tf_op jit(solution)/shard_map/ppermute | solution.py:270

commit v3 on v2

--- a/solution.py
+++ b/solution.py
@@ -30,17 +30,46 @@
     return lax.dot_general(left, right, (((1,), (1,)), ((), ())), preferred_element_type=F32)
 
 
-def call(kernel, outs, *args, scalars=(), scratch=()):
-    specs = [pl.BlockSpec(memory_space=pltpu.SMEM)] * len(scalars)
-    specs += [pl.BlockSpec(memory_space=pltpu.VMEM)] * len(args)
+class Fetch:
+    def __init__(self, ref, spot, sem):
+        self.spot, self.copy = spot, pltpu.make_async_copy(ref, spot, sem)
+
+    def get(self):
+        self.copy.wait()
+        return self.spot
+
+
+def call(kernel, outs, *args, scalars=(), far=(), scratch=()):
+    n_scalars, n_far, n_args, n_outs = len(scalars), len(far), len(args), len(outs)
+
+    def body(*refs):
+        head, rest = refs[:n_scalars], refs[n_scalars:]
+        sources, rest = rest[:n_far], rest[n_far:]
+        near, rest = rest[:n_args], rest[n_args:]
+        results, rest = rest[:n_outs], rest[n_outs:]
+        if not n_far:
+            return kernel(*head, *near, *results, *rest)
+        spots, sems, own = rest[:n_far], rest[n_far], rest[n_far + 1 :]
+        fetches = [Fetch(sources[i], spots[i], sems.at[i]) for i in range(n_far)]
+        for fetch in fetches:
+            fetch.copy.start()
+        kernel(*head, *fetches, *near, *results, *own)
+
+    specs = [pl.BlockSpec(memory_space=pltpu.SMEM)] * n_scalars
+    specs += [pl.BlockSpec(memory_space=pl.ANY)] * n_far
+    specs += [pl.BlockSpec(memory_space=pltpu.VMEM)] * n_args
+    spots = [pltpu.VMEM(a.shape, a.dtype) for a in far]
+    if far:
+        spots.append(pltpu.SemaphoreType.DMA((n_far,)))
     return pl.pallas_call(
-        kernel,
+        body,
         out_shape=[jax.ShapeDtypeStruct(s, d) for s, d in outs],
         in_specs=specs,
-        out_specs=[pl.BlockSpec(memory_space=pltpu.VMEM)] * len(outs),
-        scratch_shapes=scratch,
+        out_specs=[pl.BlockSpec(memory_space=pltpu.VMEM)] * n_outs,
+        scratch_shapes=spots + list(scratch),
         compiler_params=pltpu.CompilerParams(vmem_limit_bytes=40 * 1024 * 1024),
-    )(*scalars, *args)
+        name=kernel.__name__,
+    )(*scalars, *far, *args)
 
 
 def pick_matrix():
@@ -53,7 +82,7 @@
                     if col < 16:
                         source = 128 * below + level * 64 + row * 16 + col
                     else:
-                        source = 256 + 32 * below + level * 16 + row * 4 + col - 16
+                        source = 288 - 32 * below + level * 16 + row * 4 + col - 16
                     pick[w * WIN + level * 64 + r * 8 + c, source] = 1
     return pick
 
@@ -66,36 +95,44 @@
     return corner
 
 
-def send_kernel(tok, cot, corner, lat_out, lon_out, diag_out):
-    pick = corner[...]
-    for i, ref in enumerate((tok, cot)):
+def columns_kernel(tok, cot, corner, lon_out, upper_out):
+    refs = [tok.get(), cot.get()]
+    pick = corner.get()[...]
+    for i, ref in enumerate(refs):
         upper = ref[:, 0:4].reshape(WIN, -1)
         lower = ref[:, 4:8].reshape(WIN, -1)
-        lat_out[i * WIN : (i + 1) * WIN] = upper
-        lon_out[i * 32 : (i + 1) * 32] = dot(pick, lower).astype(BF16)
-        diag_out[i * 32 : (i + 1) * 32] = dot(pick, upper).astype(BF16)
+        upper_out[i * WIN : (i + 1) * WIN] = upper
+        lon_out[i * 32 : (i + 1) * 32] = dot(pick, upper).astype(BF16)
+        lon_out[64 + i * 32 : 64 + (i + 1) * 32] = dot(pick, lower).astype(BF16)
+
+
+def rows_kernel(upper, lon, lat_out):
+    for i in range(2):
+        lat_out[i * 160 : i * 160 + WIN] = upper[i * WIN : (i + 1) * WIN]
+        lat_out[i * 160 + WIN : (i + 1) * 160] = lon[i * 32 : (i + 1) * 32]
 
 
 def window_kernel(
-    meta, tok, cot, lat, lon, diag, pick, put, gain, w_qkv, w_out,
-    grads, own_back, lat_back, lon_back, diag_back,
+    meta, tok, pick, w_qkv, cot, w_out, put, lat, lon, gain,
+    grads, own_back, lat_back, side_back,
     left, right, packed, d_att,
 ):
-    dim = w_out.shape[0]
+    dim = lat.shape[1]
     scale = HDIM ** (-0.5)
-    gains = gain[...].astype(F32)
+    gains = gain[...].reshape(1, dim).astype(F32)
 
     def assembled(i, ref):
         return (
             dot(pick[:, 0:128], ref[:, 4:8].reshape(WIN, dim))
-            + dot(pick[:, 128:256], lat[i * WIN : (i + 1) * WIN])
-            + dot(pick[:, 256:288], lon[i * 32 : (i + 1) * 32])
-            + dot(pick[:, 288:320], diag[i * 32 : (i + 1) * 32])
+            + dot(pick[:, 128:288], lat[i * 160 : (i + 1) * 160])
+            + dot(pick[:, 288:320], lon[64 + i * 32 : 64 + (i + 1) * 32])
         )
 
+    tok, pick = tok.get(), pick.get()
     x = assembled(0, tok)
     in_first = lax.broadcasted_iota(jnp.int32, (2 * WIN, 1), 0) < WIN
     ocean = jnp.where(in_first, meta[0], meta[1]).astype(F32)
+    w_qkv, cot, w_out, put = w_qkv.get(), cot.get(), w_out.get(), put.get()
     g = (assembled(1, cot) * ocean).astype(BF16)
     centered = x - jnp.mean(x, -1, keepdims=True)
     rstd = lax.rsqrt(jnp.mean(centered * centered, -1, keepdims=True) + 1e-5)
@@ -160,21 +197,26 @@
     back = dot(put[...], branch.astype(BF16)).astype(BF16)
     own_back[...] = back[0:128]
     lat_back[...] = back[128:256]
-    lon_back[...] = back[256:288]
-    diag_back[...] = back[288:320]
-
-
-def token_kernel(cot, own, lat, lon, diag, spread, out):
-    fill = spread[...]
-    lower = own[...].astype(F32) + dot(fill, lon[...])
-    upper = lat[...].astype(F32) + dot(fill, diag[...])
+    side_back[...] = back[256:320]
+
+
+def join_kernel(spread, lat_back, side, out):
+    fill = spread.get()[...]
+    out[...] = (lat_back[...].astype(F32) + dot(fill, side[0:32])).astype(BF16)
+
+
+def token_kernel(cot, spread, own, lat, side, out):
+    cot, fill = cot.get(), spread.get()[...]
+    lower = own[...].astype(F32) + dot(fill, side[32:64])
+    upper = lat[...].astype(F32)
     shape = (2, 4) + cot.shape[2:]
     out[:, 0:4] = (cot[:, 0:4].astype(F32) + upper.reshape(shape)).astype(BF16)
     out[:, 4:8] = (cot[:, 4:8].astype(F32) + lower.reshape(shape)).astype(BF16)
 
 
-def result_kernel(meta, mine, other, gain, w_qkv, qkv_out, out_out, gain_out):
+def result_kernel(meta, w_qkv, mine, other, gain, qkv_out, out_out, gain_out):
     dim = out_out.shape[0]
+    w_qkv = w_qkv.get()
 
     def write(halves):
         along = jnp.zeros((dim, LANES), F32)
@@ -188,7 +230,8 @@
             else:
                 out_out[:, (j - 9) * LANES : (j - 8) * LANES] = block
         total = jnp.sum(along.T, 0, keepdims=True)
-        gain_out[...] = (total / gain[...].astype(F32)).astype(BF16)
+        gains = gain[...].reshape(1, dim).astype(F32)
+        gain_out[...] = (total / gains).astype(BF16).reshape(dim)
 
     @pl.when(meta[3] == 0)
     def _():
@@ -216,14 +259,8 @@
     return lax.ppermute(array, "core", [(0, 1), (1, 0)])
 
 
-def reduced(grads):
-    half = grads.shape[1]
-    mine = (grads[0].astype(F32) + swapped(grads[1]).astype(F32)).astype(BF16)
-    mine = summed(exchange(mine.reshape(16, half // 16, LANES), PLANE))
-    mine = summed(exchange(mine.reshape(16, half // 256, LANES), RING))
-    mine = spread_along(mine, RING).reshape(half // 16, LANES)
-    mine = spread_along(mine, PLANE).reshape(half, LANES)
-    return mine, swapped(mine)
+def tied(*arrays):
+    return lax.optimization_barrier(arrays)
 
 
 def local(tokens, cotangent, ocean_mask, gain, w_qkv, w_out):
@@ -233,9 +270,7 @@
     ocean = lax.dynamic_slice_in_dim(ocean_mask, lat_index, 1, 0).reshape(2)
     flags = jnp.stack([(lat_index == n_lat - 1).astype(jnp.int32), core.astype(jnp.int32)])
     meta = jnp.concatenate([ocean, flags])
-    gain_row = gain.reshape(1, dim)
-    corner = corner_matrix()
-    pick = pick_matrix()
+    corner, pick = corner_matrix(), pick_matrix()
     constant = functools.partial(jnp.asarray, dtype=BF16)
 
     def from_next(array, axis, size):
@@ -244,21 +279,21 @@
     def to_next(array, axis, size):
         return lax.ppermute(array, axis, [(i, (i + 1) % size) for i in range(size)])
 
-    def place_of(a, b):
-        return (a % n_lat) * n_lon + b % n_lon
-
-    pairs = [(place_of(a + 1, b + 1), place_of(a, b)) for a in range(n_lat) for b in range(n_lon)]
-    send = [((2 * WIN, dim), BF16), ((64, dim), BF16), ((64, dim), BF16)]
-    lat, lon, diag = call(send_kernel, send, tokens, cotangent, constant(corner))
+    lon, upper = call(
+        columns_kernel, [((2 * 64, dim), BF16), ((2 * WIN, dim), BF16)],
+        far=(tokens, cotangent, constant(corner)),
+    )
+    lon = from_next(lon, LON, n_lon)
+    (lat,) = call(rows_kernel, [((2 * 160, dim), BF16)], upper, lon)
     lat = from_next(lat, LAT, n_lat)
-    diag = lax.ppermute(diag, LAT + LON, pairs)
-    lon = from_next(lon, LON, n_lon)
-
-    backs = [((n, dim), BF16) for n in (WIN, WIN, 32, 32)]
-    grads, own_back, lat_back, lon_back, diag_back = call(
-        window_kernel, [((2, 6 * dim, LANES), BF16)] + backs,
-        tokens, cotangent, lat, lon, diag, constant(pick), constant(pick.T), gain_row, w_qkv, w_out,
+
+    half = 6 * dim
+    grads, own_back, lat_back, side_back = call(
+        window_kernel,
+        [((2, half, LANES), BF16), ((WIN, dim), BF16), ((WIN, dim), BF16), ((64, dim), BF16)],
+        lat, lon, gain,
         scalars=(meta,),
+        far=(tokens, constant(pick), w_qkv, cotangent, w_out, constant(pick.T)),
         scratch=[
             pltpu.VMEM((2, dim, 2 * WIN), BF16),
             pltpu.VMEM((12, 2 * WIN, LANES), BF16),
@@ -266,20 +301,29 @@
             pltpu.VMEM((2 * WIN, dim), BF16),
         ],
     )
-    lat_back = to_next(lat_back, LAT, n_lat)
-    diag_back = lax.ppermute(diag_back, LAT + LON, [(b, a) for a, b in pairs])
-    lon_back = to_next(lon_back, LON, n_lon)
-    mine, other = reduced(grads)
+
+    side = to_next(side_back, LON, n_lon)
+    mine = (grads[0].astype(F32) + swapped(grads[1]).astype(F32)).astype(BF16)
+    mine = summed(exchange(mine.reshape(16, half // 16, LANES), PLANE))
+    mine, side = tied(mine, side)
+    (rows_back,) = call(join_kernel, [((WIN, dim), BF16)], lat_back, side, far=(constant(corner.T),))
+    rows_back = to_next(rows_back, LAT, n_lat)
+    mine = summed(exchange(mine.reshape(16, half // 256, LANES), RING))
+    mine = spread_along(mine, RING).reshape(half // 16, LANES)
+    mine, rows_back = tied(mine, rows_back)
+    mine = spread_along(mine, PLANE).reshape(half, LANES)
+    other = swapped(mine)
     (token_grad,) = call(
         token_kernel, [(tokens.shape, BF16)],
-        cotangent, own_back, lat_back, lon_back, diag_back, constant(corner.T),
+        own_back, rows_back, side,
+        far=(cotangent, constant(corner.T)),
     )
     qkv_grad, out_grad, gain_grad = call(
-        result_kernel, [(w_qkv.shape, BF16), (w_out.shape, BF16), ((1, dim), BF16)],
-        mine, other, gain_row, w_qkv,
-        scalars=(meta,),
-    )
-    return token_grad, qkv_grad, out_grad, gain_grad.reshape(dim)
+        result_kernel, [(w_qkv.shape, BF16), (w_out.shape, BF16), ((dim,), BF16)],
+        mine, other, gain,
+        scalars=(meta,), far=(w_qkv,),
+    )
+    return token_grad, qkv_grad, out_grad, gain_grad
 
 
 def solution(mesh):

time: 152 us -> 148 us (0.974)
  the two profiles are of different devices: /device:TPU:32 before, /device:TPU:1 now
where the time goes in v3:
time: 148 us
  starting transfers between devices  57.9 us (39%)
  blocking collectives  43.8 us (30%)
  waiting for transfers between devices  23.8 us (16%)
  Pallas kernels  11 us (7%)
  local copies, waits for them, and re-layouts  8.98 us (6%)
    all_to_all x2, blocking collectives, exchange(): return lax.all_to_all(parts, axis, 0, 0, tiled=False)  43.8 us
    ppermute x2, starting transfers between devices, from_next(): return lax.ppermute(array, axis, [((i + 1) % size, i) for i in range(size)])  19.6 us
    all_to_all x2, starting transfers between devices, exchange(): return lax.all_to_all(parts, axis, 0, 0, tiled=False)  15 us
    ppermute x2, starting transfers between devices, swapped(): return lax.ppermute(array, 'core', [(0, 1), (1, 0)])  13.5 us
    all_to_all x2, waiting for transfers between devices, exchange(): return lax.all_to_all(parts, axis, 0, 0, tiled=False)  12.3 us
    pallas_call x6, Pallas kernels, call(): pl.pallas_call(body, out_shape=[jax.ShapeDtypeStruct(s, d) for s, d in ou...  11 us
    ppermute x2, starting transfers between devices, to_next(): return lax.ppermute(array, axis, [(i, (i + 1) % size) for i in range(size)])  9.77 us
    unnamed x28, local copies, waits for them, and re-layouts  7.98 us
  transfers between devices with their start and end apart: 8, of which 7 were waited for; matrix products, arithmetic and copies ran while one was open for 0% of the time, Pallas kernels for 1%

profile of v3, /device:TPU:1, one launch (start us, length us, event | category | flops | bytes accessed | tf_op | source)
XLA Modules:
  0.0 147.5 jit_solution(3890733584719656476)
XLA Ops:
  0.7 1.0 copy-done.2
  1.7 0.9 copy-done.5
  2.6 0.7 copy-done.11
  3.3 0.7 columns_kernel.1
  4.0 16.2 %collective-permute-start = (bf16[128,384]{1,0:T(8,128)(2,1)S(1)}, bf16[128,384]{1,0:T(8,128)(2,1)S(1)}, u32[]{:S(2)}, u32[]{:S(2)}) collective-permute-start(bf16[128,384]{1,0:T(8,128)(2,1)S(1)} %get-tuple-element.18), channel_id=1, source_target_pairs={{1,0},{2,1},{3,2},{4,3},{5,4},{6,5},{7,6},{8,7},{9,8},{10,9},{11,1... | collective-permute-start | bytes 294920 | tf_op jit(solution)/shard_map/ppermute | solution.py:277
  20.2 1.6 %collective-permute-done.refs_1_.refs_8_ = bf16[128,384]{1,0:T(8,128)(2,1)S(1)} collective-permute-done((bf16[128,384]{1,0:T(8,128)(2,1)S(1)}, bf16[128,384]{1,0:T(8,128)(2,1)S(1)}, u32[]{:S(2)}, u32[]{:S(2)}) %collective-permute-start) | collective-permute-done | bytes 98336 | tf_op jit(solution)/shard_map/ppermute | solution.py:277
  21.8 3.4 %collective-permute-start.1 = (bf16[320,384]{1,0:T(8,128)(2,1)S(1)}, bf16[320,384]{1,0:T(8,128)(2,1)S(1)}, u32[]{:S(2)}, u32[]{:S(2)}) collective-permute-start(bf16[320,384]{1,0:T(8,128)(2,1)S(1)} %rows_kernel.1), channel_id=1, source_target_pairs={{32,0},{64,32},{96,64},{128,96},{160,128},{192,160},{224,192},{256... | collective-permute-start | bytes 737288 | tf_op jit(solution)/shard_map/ppermute | solution.py:277
  25.5 4.7 %collective-permute-done.1.refs_7_ = bf16[320,384]{1,0:T(8,128)(2,1)S(1)} collective-permute-done((bf16[320,384]{1,0:T(8,128)(2,1)S(1)}, bf16[320,384]{1,0:T(8,128)(2,1)S(1)}, u32[]{:S(2)}, u32[]{:S(2)}) %collective-permute-start.1) | collective-permute-done | bytes 245792 | tf_op jit(solution)/shard_map/ppermute | solution.py:277
  30.2 0.9 copy-done.3
  31.1 0.9 copy-done.6
  32.1 1.0 copy-done.7
  33.0 0.9 copy-done.8
  34.0 0.9 copy-done.9
  34.9 0.7 copy-done.12
  35.6 6.8 %window_kernel.1 = (bf16[2,2304,128]{2,1,0:T(8,128)(2,1)S(1)}, bf16[128,384]{1,0:T(8,128)(2,1)S(1)}, bf16[128,384]{1,0:T(8,128)(2,1)S(1)}, bf16[64,384]{1,0:T(8,128)(2,1)S(1)}) custom-call(s32[4]{0:T(128)S(1)} %pad_add_fusion.refs_0_, bf16[2,8,16,384]{3,2,1,0:T(8,128)(2,1)S(1)} %copy-done.6, bf16[256,320]{1,0:T(8,128)(2,1)S(1)} %copy-done.8, ...), custom_call_target="tpu_custom_call" | custom-call | tf_op jit(solution)/shard_map/window_kernel/pallas_call | solution.py:64
  42.4 11.2 %collective-permute-start.2 = (bf16[2304,128]{1,0:T(8,128)(2,1)S(1)}, bf16[2304,128]{1,0:T(8,128)(2,1)S(1)}, u32[]{:S(2)}, u32[]{:S(2)}) collective-permute-start(bf16[2304,128]{1,0:T(8,128)(2,1)S(1)} %slice_bitcast_fusion), channel_id=1, source_target_pairs={{0,32},{32,0},{1,33},{33,1},{2,34},{34,2},{3,35},{35,3},{4,36},{36... | collective-permute-start | bytes 1769480 | tf_op jit(solution)/shard_map/ppermute | solution.py:259
  53.6 1.6 %collective-permute-done.2 = bf16[2304,128]{1,0:T(8,128)(2,1)S(1)} collective-permute-done((bf16[2304,128]{1,0:T(8,128)(2,1)S(1)}, bf16[2304,128]{1,0:T(8,128)(2,1)S(1)}, u32[]{:S(2)}, u32[]{:S(2)}) %collective-permute-start.2) | collective-permute-done | bytes 589856 | tf_op jit(solution)/shard_map/ppermute | solution.py:259
  55.2 1.0 fusion
  56.2 11.5 %all-to-all-start = ((bf16[16,144,128]{2,1,0:T(8,128)(2,1)}), bf16[16,144,128]{2,1,0:T(8,128)(2,1)S(1)}, u32[]{:S(2)}, u32[]{:S(2)}) async-start(bf16[16,144,128]{2,1,0:T(8,128)(2,1)} %bitcast.4), calls=%async_computation | async-start | bytes 1179648 | tf_op jit(solution)/shard_map/all_to_all | solution.py:246
  67.7 3.3 %collective-permute-start.3 = (bf16[64,384]{1,0:T(8,128)(2,1)S(1)}, bf16[64,384]{1,0:T(8,128)(2,1)S(1)}, u32[]{:S(2)}, u32[]{:S(2)}) collective-permute-start(bf16[64,384]{1,0:T(8,128)(2,1)S(1)} %get-tuple-element.21), channel_id=1, source_target_pairs={{0,1},{1,2},{2,3},{3,4},{4,5},{5,6},{6,7},{7,8},{8,9},{9,10},{10,1... | collective-permute-start | bytes 147464 | tf_op jit(solution)/shard_map/ppermute | solution.py:280
  71.0 7.5 %all-to-all-done = bf16[16,144,128]{2,1,0:T(8,128)(2,1)S(1)} async-done(((bf16[16,144,128]{2,1,0:T(8,128)(2,1)}), bf16[16,144,128]{2,1,0:T(8,128)(2,1)S(1)}, u32[]{:S(2)}, u32[]{:S(2)}) %all-to-all-start) | async-done | bytes 589856 | tf_op jit(solution)/shard_map/all_to_all | solution.py:246
  78.5 3.2 %collective-permute-done.3.refs_2_.refs_4_ = bf16[64,384]{1,0:T(8,128)(2,1)S(1)} collective-permute-done((bf16[64,384]{1,0:T(8,128)(2,1)S(1)}, bf16[64,384]{1,0:T(8,128)(2,1)S(1)}, u32[]{:S(2)}, u32[]{:S(2)}) %collective-permute-start.3) | collective-permute-done | bytes 49184 | tf_op jit(solution)/shard_map/ppermute | solution.py:280
  81.7 19.2 %all_to_all.20 = bf16[16,9,128]{2,1,0:T(8,128)(2,1)S(1)} all-to-all(bf16[16,9,128]{2,1,0:T(8,128)(2,1)S(1)} %reshape.29), channel_id=1, replica_groups=mesh['zhi'=2,'x'=4,'core'=2,'zlo'=8,'y'=4] {'zhi','zlo'}, dimensions={0} | all-to-all | bytes 73728 | tf_op jit(solution)/shard_map/all_to_all | solution.py:246
  100.9 0.6 broadcast_in_dim.4
  101.6 3.5 %all-to-all-start.2 = ((bf16[16,9,128]{2,1,0:T(8,128)(2,1)}), bf16[16,9,128]{2,1,0:T(8,128)(2,1)S(1)}, u32[]{:S(2)}, u32[]{:S(2)}) async-start(bf16[16,9,128]{2,1,0:T(8,128)(2,1)} %broadcast_in_dim.4), calls=%async_computation.2 | async-start | bytes 131072 | tf_op jit(solution)/shard_map/all_to_all | solution.py:246
  105.3 6.5 %collective-permute-start.4 = (bf16[128,384]{1,0:T(8,128)(2,1)S(1)}, bf16[128,384]{1,0:T(8,128)(2,1)S(1)}, u32[]{:S(2)}, u32[]{:S(2)}) collective-permute-start(bf16[128,384]{1,0:T(8,128)(2,1)S(1)} %join_kernel.1), channel_id=1, source_target_pairs={{0,32},{32,64},{64,96},{96,128},{128,160},{160,192},{192,224},{224... | collective-permute-start | bytes 294920 | tf_op jit(solution)/shard_map/ppermute | solution.py:280
  111.8 4.9 %all-to-all-done.2 = bf16[16,9,128]{2,1,0:T(8,128)(2,1)S(1)} async-done(((bf16[16,9,128]{2,1,0:T(8,128)(2,1)}), bf16[16,9,128]{2,1,0:T(8,128)(2,1)S(1)}, u32[]{:S(2)}, u32[]{:S(2)}) %all-to-all-start.2) | async-done | bytes 36896 | tf_op jit(solution)/shard_map/all_to_all | solution.py:246
  116.8 24.7 %all_to_all.21 = bf16[16,144,128]{2,1,0:T(8,128)(2,1)S(1)} all-to-all(bf16[16,144,128]{2,1,0:T(8,128)(2,1)S(1)} %broadcast_in_dim.5), channel_id=1, replica_groups=mesh['zhi'=2,'x'=4,'core'=2,'zlo'=8,'y'=4] {'x','y'}, dimensions={0} | all-to-all | bytes 1179648 | tf_op jit(solution)/shard_map/all_to_all | solution.py:246
  141.5 2.3 %collective-permute-start.5 = (bf16[2304,128]{1,0:T(8,128)(2,1)S(1)}, bf16[2304,128]{1,0:T(8,128)(2,1)S(1)}, u32[]{:S(2)}, u32[]{:S(2)}) collective-permute-start(bf16[2304,128]{1,0:T(8,128)(2,1)S(1)} %bitcast.9), channel_id=1, source_target_pairs={{0,32},{32,0},{1,33},{33,1},{2,34},{34,2},{3,35},{35,3},{4,36},{36... | collective-permute-start | bytes 1769480 | tf_op jit(solution)/shard_map/ppermute | solution.py:259
  143.8 1.1 token_kernel.1
  144.9 0.4 collective-permute-done.5.refs_3_
  145.4 2.2 %result_kernel.1 = (bf16[384,1152]{1,0:T(8,128)(2,1)}, bf16[384,384]{1,0:T(8,128)(2,1)}, bf16[384]{0:T(512)(128)(2,1)}) custom-call(s32[4]{0:T(128)S(1)} %pad_add_fusion.refs_0_, bf16[384,1152]{1,0:T(8,128)(2,1)S(1)} %copy-done.1, bf16[2304,128]{1,0:T(8,128)(2,1)S(1)} %bitcast.10, bf16[2304,128]{1,0:T(8,128)(2,1)S(1)} %collective-permute-done.5.refs_3_, ...), custom_call_target="tpu_custom_call" | custom-call | tf_op jit(solution)/shard_map/result_kernel/pallas_call | solution.py:64
  (30 shorter events, 0.8 us)
Async XLA Ops:
  0.6 24.6 %copy-start = (s32[16,2]{0,1:T(2,128)S(1)}, s32[16,2]{0,1:T(2,128)}, u32[]{:S(2)}) copy-start(s32[16,2]{0,1:T(2,128)} %param.13) | copy-start | bytes 388
  0.6 29.6 %copy-start.1 = (bf16[384,1152]{1,0:T(8,128)(2,1)S(1)}, bf16[384,1152]{1,0:T(8,128)(2,1)}, u32[]{:S(2)}) copy-start(bf16[384,1152]{1,0:T(8,128)(2,1)} %refs_1_.6) | copy-start | bytes 2654212
  0.7 1.0 copy-start.2
  1.7 0.9 copy-start.5
  2.6 0.7 copy-start.11
  4.0 17.8 %collective-permute-start = (bf16[128,384]{1,0:T(8,128)(2,1)S(1)}, bf16[128,384]{1,0:T(8,128)(2,1)S(1)}, u32[]{:S(2)}, u32[]{:S(2)}) collective-permute-start(bf16[128,384]{1,0:T(8,128)(2,1)S(1)} %get-tuple-element.18), channel_id=1, source_target_pairs={{1,0},{2,1},{3,2},{4,3},{5,4},{6,5},{7,6},{8,7},{9,8},{10,9},{11,1... | collective-permute-start | bytes 294920 | tf_op jit(solution)/shard_map/ppermute | solution.py:277
  21.8 8.4 %collective-permute-start.1 = (bf16[320,384]{1,0:T(8,128)(2,1)S(1)}, bf16[320,384]{1,0:T(8,128)(2,1)S(1)}, u32[]{:S(2)}, u32[]{:S(2)}) collective-permute-start(bf16[320,384]{1,0:T(8,128)(2,1)S(1)} %rows_kernel.1), channel_id=1, source_target_pairs={{32,0},{64,32},{96,64},{128,96},{160,128},{192,160},{224,192},{256... | collective-permute-start | bytes 737288 | tf_op jit(solution)/shard_map/ppermute | solution.py:277
  30.2 0.9 copy-start.3
  31.1 0.9 copy-start.6
  32.1 1.0 copy-start.7
  33.0 0.9 copy-start.8
  34.0 0.9 copy-start.9
  34.9 0.7 copy-start.12
  42.4 12.8 %collective-permute-start.2 = (bf16[2304,128]{1,0:T(8,128)(2,1)S(1)}, bf16[2304,128]{1,0:T(8,128)(2,1)S(1)}, u32[]{:S(2)}, u32[]{:S(2)}) collective-permute-start(bf16[2304,128]{1,0:T(8,128)(2,1)S(1)} %slice_bitcast_fusion), channel_id=1, source_target_pairs={{0,32},{32,0},{1,33},{33,1},{2,34},{34,2},{3,35},{35,3},{4,36},{36... | collective-permute-start | bytes 1769480 | tf_op jit(solution)/shard_map/ppermute | solution.py:259
  56.2 48.9 %copy-start.10 = (bf16[128,32]{1,0:T(8,128)(2,1)S(1)}, bf16[128,32]{1,0:T(8,128)(2,1)}, u32[]{:S(2)}) copy-start(bf16[128,32]{1,0:T(8,128)(2,1)} %constant.41.clone.refs_0_.refs_1_) | copy-start | bytes 24580
  56.2 22.3 %all-to-all-start = ((bf16[16,144,128]{2,1,0:T(8,128)(2,1)}), bf16[16,144,128]{2,1,0:T(8,128)(2,1)S(1)}, u32[]{:S(2)}, u32[]{:S(2)}) async-start(bf16[16,144,128]{2,1,0:T(8,128)(2,1)} %bitcast.4), calls=%async_computation | async-start | bytes 1179648 | tf_op jit(solution)/shard_map/all_to_all | solution.py:246
  67.7 14.0 %collective-permute-start.3 = (bf16[64,384]{1,0:T(8,128)(2,1)S(1)}, bf16[64,384]{1,0:T(8,128)(2,1)S(1)}, u32[]{:S(2)}, u32[]{:S(2)}) collective-permute-start(bf16[64,384]{1,0:T(8,128)(2,1)S(1)} %get-tuple-element.21), channel_id=1, source_target_pairs={{0,1},{1,2},{2,3},{3,4},{4,5},{5,6},{6,7},{7,8},{8,9},{9,10},{10,1... | collective-permute-start | bytes 147464 | tf_op jit(solution)/shard_map/ppermute | solution.py:280
  100.9 42.9 %copy-start.4 = (bf16[2,8,16,384]{3,2,1,0:T(8,128)(2,1)S(1)}, bf16[2,8,16,384]{3,2,1,0:T(8,128)(2,1)}, u32[]{:S(2)}) copy-start(bf16[2,8,16,384]{3,2,1,0:T(8,128)(2,1)} %refs_0_.4) | copy-start | bytes 589828
  101.6 15.1 %all-to-all-start.2 = ((bf16[16,9,128]{2,1,0:T(8,128)(2,1)}), bf16[16,9,128]{2,1,0:T(8,128)(2,1)S(1)}, u32[]{:S(2)}, u32[]{:S(2)}) async-start(bf16[16,9,128]{2,1,0:T(8,128)(2,1)} %broadcast_in_dim.4), calls=%async_computation.2 | async-start | bytes 131072 | tf_op jit(solution)/shard_map/all_to_all | solution.py:246
  105.3 11.4 %collective-permute-start.4 = (bf16[128,384]{1,0:T(8,128)(2,1)S(1)}, bf16[128,384]{1,0:T(8,128)(2,1)S(1)}, u32[]{:S(2)}, u32[]{:S(2)}) collective-permute-start(bf16[128,384]{1,0:T(8,128)(2,1)S(1)} %join_kernel.1), channel_id=1, source_target_pairs={{0,32},{32,64},{64,96},{96,128},{128,160},{160,192},{192,224},{224... | collective-permute-start | bytes 294920 | tf_op jit(solution)/shard_map/ppermute | solution.py:280
  116.7 28.7 %copy-start.13 = (bf16[384]{0:T(512)(128)(2,1)S(1)}, bf16[384]{0:T(512)(128)(2,1)}, u32[]{:S(2)}) copy-start(bf16[384]{0:T(512)(128)(2,1)} %refs_4_.3) | copy-start | bytes 2308
  141.5 3.9 %collective-permute-start.5 = (bf16[2304,128]{1,0:T(8,128)(2,1)S(1)}, bf16[2304,128]{1,0:T(8,128)(2,1)S(1)}, u32[]{:S(2)}, u32[]{:S(2)}) collective-permute-start(bf16[2304,128]{1,0:T(8,128)(2,1)S(1)} %bitcast.9), channel_id=1, source_target_pairs={{0,32},{32,0},{1,33},{33,1},{2,34},{34,2},{3,35},{35,3},{4,36},{36... | collective-permute-start | bytes 1769480 | tf_op jit(solution)/shard_map/ppermute | solution.py:259

commit v4 on v3

--- a/solution.py
+++ b/solution.py
@@ -20,6 +20,7 @@
 RING = ("zhi", "zlo")
 F32 = jnp.float32
 BF16 = jnp.bfloat16
+LONG = 3 * 10**10
 
 
 def dot(left, right):
@@ -39,7 +40,7 @@
         return self.spot
 
 
-def call(kernel, outs, *args, scalars=(), far=(), scratch=()):
+def call(kernel, outs, *args, scalars=(), far=(), scratch=(), limit=40, flops=0):
     n_scalars, n_far, n_args, n_outs = len(scalars), len(far), len(args), len(outs)
 
     def body(*refs):
@@ -56,7 +57,7 @@
         kernel(*head, *fetches, *near, *results, *own)
 
     specs = [pl.BlockSpec(memory_space=pltpu.SMEM)] * n_scalars
-    specs += [pl.BlockSpec(memory_space=pl.ANY)] * n_far
+    specs += [pl.BlockSpec(memory_space=pltpu.HBM)] * n_far
     specs += [pl.BlockSpec(memory_space=pltpu.VMEM)] * n_args
     spots = [pltpu.VMEM(a.shape, a.dtype) for a in far]
     if far:
@@ -67,8 +68,9 @@
         in_specs=specs,
         out_specs=[pl.BlockSpec(memory_space=pltpu.VMEM)] * n_outs,
         scratch_shapes=spots + list(scratch),
-        compiler_params=pltpu.CompilerParams(vmem_limit_bytes=40 * 1024 * 1024),
+        compiler_params=pltpu.CompilerParams(vmem_limit_bytes=limit * 1024 * 1024),
         name=kernel.__name__,
+        cost_estimate=pl.CostEstimate(flops=flops, bytes_accessed=0, transcendentals=0) if flops else None,
     )(*scalars, *far, *args)
 
 
@@ -95,44 +97,46 @@
     return corner
 
 
-def columns_kernel(tok, cot, corner, lon_out, upper_out):
+def send_kernel(tok, cot, corner, lat_out, diag_out, lon_out):
     refs = [tok.get(), cot.get()]
     pick = corner.get()[...]
     for i, ref in enumerate(refs):
         upper = ref[:, 0:4].reshape(WIN, -1)
         lower = ref[:, 4:8].reshape(WIN, -1)
-        upper_out[i * WIN : (i + 1) * WIN] = upper
-        lon_out[i * 32 : (i + 1) * 32] = dot(pick, upper).astype(BF16)
-        lon_out[64 + i * 32 : 64 + (i + 1) * 32] = dot(pick, lower).astype(BF16)
-
-
-def rows_kernel(upper, lon, lat_out):
-    for i in range(2):
-        lat_out[i * 160 : i * 160 + WIN] = upper[i * WIN : (i + 1) * WIN]
-        lat_out[i * 160 + WIN : (i + 1) * 160] = lon[i * 32 : (i + 1) * 32]
+        lat_out[i * WIN : (i + 1) * WIN] = upper
+        diag_out[i * 32 : (i + 1) * 32] = dot(pick, upper).astype(BF16)
+        lon_out[i * 32 : (i + 1) * 32] = dot(pick, lower).astype(BF16)
+
+
+def stage_kernel(*refs):
+    half = len(refs) // 2
+    for fetch, out in zip(refs[:half], refs[half:]):
+        out[...] = fetch.get()[...]
 
 
 def window_kernel(
-    meta, tok, pick, w_qkv, cot, w_out, put, lat, lon, gain,
+    place, ocean_mask, tok, pick, w_qkv, cot, w_out, put, lat, diag, lon, gain,
     grads, own_back, lat_back, side_back,
     left, right, packed, d_att,
 ):
     dim = lat.shape[1]
+    lat_index = place[0]
+    core = lax.rem(lat_index, 2)
+    last_band = (lat_index == ocean_mask.shape[1] - 1).astype(jnp.int32)
     scale = HDIM ** (-0.5)
     gains = gain[...].reshape(1, dim).astype(F32)
 
     def assembled(i, ref):
         return (
             dot(pick[:, 0:128], ref[:, 4:8].reshape(WIN, dim))
-            + dot(pick[:, 128:288], lat[i * 160 : (i + 1) * 160])
-            + dot(pick[:, 288:320], lon[64 + i * 32 : 64 + (i + 1) * 32])
+            + dot(pick[:, 128:256], lat[i * WIN : (i + 1) * WIN])
+            + dot(pick[:, 256:288], diag[i * 32 : (i + 1) * 32])
+            + dot(pick[:, 288:320], lon[i * 32 : (i + 1) * 32])
         )
 
-    tok, pick = tok.get(), pick.get()
     x = assembled(0, tok)
     in_first = lax.broadcasted_iota(jnp.int32, (2 * WIN, 1), 0) < WIN
-    ocean = jnp.where(in_first, meta[0], meta[1]).astype(F32)
-    w_qkv, cot, w_out, put = w_qkv.get(), cot.get(), w_out.get(), put.get()
+    ocean = jnp.where(in_first, ocean_mask[0, lat_index], ocean_mask[1, lat_index]).astype(F32)
     g = (assembled(1, cot) * ocean).astype(BF16)
     centered = x - jnp.mean(x, -1, keepdims=True)
     rstd = lax.rsqrt(jnp.mean(centered * centered, -1, keepdims=True) + 1e-5)
@@ -149,7 +153,7 @@
     masks = [(lane // HDIM == h).astype(F32).astype(BF16) for h in range(PACK)]
     key_row = lax.broadcasted_iota(jnp.int32, (WIN, PACK * WIN), 0) // 8 % 8 >= 4
     query_row = lax.broadcasted_iota(jnp.int32, (WIN, PACK * WIN), 1) // 8 % 8 >= 4
-    differ = (key_row != query_row).astype(jnp.int32) * meta[2] > 0
+    differ = (key_row != query_row).astype(jnp.int32) * last_band > 0
 
     for w in range(2):
         rows = slice(w * WIN, (w + 1) * WIN)
@@ -182,7 +186,7 @@
 
     for j in range(12):
         half, at = j // 6, j % 6
-        slot = lax.rem(half + meta[3], 2)
+        slot = lax.rem(half + core, 2)
         term = dot(left[j // 9], right[j])
         grads[slot, at * dim : (at + 1) * dim] = term.astype(BF16)
 
@@ -214,7 +218,7 @@
     out[:, 4:8] = (cot[:, 4:8].astype(F32) + lower.reshape(shape)).astype(BF16)
 
 
-def result_kernel(meta, w_qkv, mine, other, gain, qkv_out, out_out, gain_out):
+def result_kernel(place, w_qkv, mine, other, gain, qkv_out, out_out, gain_out):
     dim = out_out.shape[0]
     w_qkv = w_qkv.get()
 
@@ -233,11 +237,13 @@
         gains = gain[...].reshape(1, dim).astype(F32)
         gain_out[...] = (total / gains).astype(BF16).reshape(dim)
 
-    @pl.when(meta[3] == 0)
+    core = lax.rem(place[0], 2)
+
+    @pl.when(core == 0)
     def _():
         write((mine, other))
 
-    @pl.when(meta[3] != 0)
+    @pl.when(core != 0)
     def _():
         write((other, mine))
 
@@ -266,10 +272,7 @@
 def local(tokens, cotangent, ocean_mask, gain, w_qkv, w_out):
     dim = w_out.shape[0]
     n_lat, n_lon = lax.axis_size(LAT), lax.axis_size(LON)
-    lat_index, core = lax.axis_index(LAT), lax.axis_index("core")
-    ocean = lax.dynamic_slice_in_dim(ocean_mask, lat_index, 1, 0).reshape(2)
-    flags = jnp.stack([(lat_index == n_lat - 1).astype(jnp.int32), core.astype(jnp.int32)])
-    meta = jnp.concatenate([ocean, flags])
+    place = lax.axis_index(LAT).astype(jnp.int32).reshape(1)
     corner, pick = corner_matrix(), pick_matrix()
     constant = functools.partial(jnp.asarray, dtype=BF16)
 
@@ -279,21 +282,25 @@
     def to_next(array, axis, size):
         return lax.ppermute(array, axis, [(i, (i + 1) % size) for i in range(size)])
 
-    lon, upper = call(
-        columns_kernel, [((2 * 64, dim), BF16), ((2 * WIN, dim), BF16)],
-        far=(tokens, cotangent, constant(corner)),
-    )
+    def place_of(a, b):
+        return (a % n_lat) * n_lon + b % n_lon
+
+    pairs = [(place_of(a + 1, b + 1), place_of(a, b)) for a in range(n_lat) for b in range(n_lon)]
+    lat, diag, lon = call(
+        send_kernel, [((2 * WIN, dim), BF16), ((64, dim), BF16), ((64, dim), BF16)],
+        far=(tokens, cotangent, constant(corner)), limit=60,
+    )
+    lat = from_next(lat, LAT, n_lat)
+    diag = lax.ppermute(diag, LAT + LON, pairs)
     lon = from_next(lon, LON, n_lon)
-    (lat,) = call(rows_kernel, [((2 * 160, dim), BF16)], upper, lon)
-    lat = from_next(lat, LAT, n_lat)
-
+    near = (tokens, constant(pick), w_qkv, cotangent, w_out, constant(pick.T))
+    near = call(stage_kernel, [(a.shape, BF16) for a in near], far=near)
     half = 6 * dim
     grads, own_back, lat_back, side_back = call(
         window_kernel,
         [((2, half, LANES), BF16), ((WIN, dim), BF16), ((WIN, dim), BF16), ((64, dim), BF16)],
-        lat, lon, gain,
-        scalars=(meta,),
-        far=(tokens, constant(pick), w_qkv, cotangent, w_out, constant(pick.T)),
+        *near, lat, diag, lon, gain,
+        scalars=(place, ocean_mask.T),
         scratch=[
             pltpu.VMEM((2, dim, 2 * WIN), BF16),
             pltpu.VMEM((12, 2 * WIN, LANES), BF16),
@@ -305,23 +312,25 @@
     side = to_next(side_back, LON, n_lon)
     mine = (grads[0].astype(F32) + swapped(grads[1]).astype(F32)).astype(BF16)
     mine = summed(exchange(mine.reshape(16, half // 16, LANES), PLANE))
-    mine, side = tied(mine, side)
-    (rows_back,) = call(join_kernel, [((WIN, dim), BF16)], lat_back, side, far=(constant(corner.T),))
+    mine = summed(exchange(mine.reshape(16, half // 256, LANES), RING))
+    (rows_back,) = call(
+        join_kernel, [((WIN, dim), BF16)], lat_back, side, far=(constant(corner.T),), flops=LONG
+    )
+    mine, rows_back = tied(mine, rows_back)
     rows_back = to_next(rows_back, LAT, n_lat)
-    mine = summed(exchange(mine.reshape(16, half // 256, LANES), RING))
     mine = spread_along(mine, RING).reshape(half // 16, LANES)
-    mine, rows_back = tied(mine, rows_back)
     mine = spread_along(mine, PLANE).reshape(half, LANES)
-    other = swapped(mine)
     (token_grad,) = call(
         token_kernel, [(tokens.shape, BF16)],
         own_back, rows_back, side,
-        far=(cotangent, constant(corner.T)),
-    )
+        far=(cotangent, constant(corner.T)), flops=LONG,
+    )
+    mine, token_grad = tied(mine, token_grad)
+    other = swapped(mine)
     qkv_grad, out_grad, gain_grad = call(
         result_kernel, [(w_qkv.shape, BF16), (w_out.shape, BF16), ((dim,), BF16)],
         mine, other, gain,
-        scalars=(meta,), far=(w_qkv,),
+        scalars=(place,), far=(w_qkv,),
     )
     return token_grad, qkv_grad, out_grad, gain_grad
 

time: 148 us -> 132 us (0.89)
  blocking collectives: 43.8 us -> 0 us
  waiting for transfers between devices: 23.8 us -> 39.1 us
  starting transfers between devices: 57.9 us -> 70.1 us
    all_to_all x2 -> x0, blocking collectives: 43.8 us -> none  [exchange(): return lax.all_to_all(parts, axis, 0, 0, tiled=False)]
    all_to_all x2 -> x4, waiting for transfers between devices: 12.3 us -> 35.8 us  [exchange(): return lax.all_to_all(parts, axis, 0, 0, tiled=False)]
    ppermute x0 -> x1, starting transfers between devices: none -> 17.8 us  [local(): diag = lax.ppermute(diag, LAT + LON, pairs)]
    all_to_all x2 -> x4, starting transfers between devices: 15 us -> 26.7 us  [exchange(): return lax.all_to_all(parts, axis, 0, 0, tiled=False)]
    ppermute x2, starting transfers between devices: 19.6 us -> 11.2 us  [from_next(): return lax.ppermute(array, axis, [((i + 1) % size, i) for i in range(size)])]
    ppermute x2, starting transfers between devices: 13.5 us -> 5.96 us  [swapped(): return lax.ppermute(array, 'core', [(0, 1), (1, 0)])]
    ppermute x2, waiting for transfers between devices: 6.29 us -> 0.01 us  [from_next(): return lax.ppermute(array, axis, [((i + 1) % size, i) for i in range(size)])]
    ppermute x2, waiting for transfers between devices: 3.18 us -> 0.01 us  [to_next(): return lax.ppermute(array, axis, [(i, (i + 1) % size) for i in range(size)])]
  transfers between devices with their start and end apart: 8 -> 11, of which waited for: 7 -> 6; matrix products, arithmetic and copies ran while one was open for 0% -> 1% of each run, Pallas kernels for 1% -> 2%
where the time goes in v4:
time: 132 us; the launch traced here: 131 us
  starting transfers between devices  70.1 us (53%)
  waiting for transfers between devices  39.1 us (30%)
  Pallas kernels  11.7 us (9%)
  local copies, waits for them, and re-layouts  8.1 us (6%)
    all_to_all x4, waiting for transfers between devices, exchange(): return lax.all_to_all(parts, axis, 0, 0, tiled=False)  35.8 us
    all_to_all x4, starting transfers between devices, exchange(): return lax.all_to_all(parts, axis, 0, 0, tiled=False)  26.7 us
    ppermute x1, starting transfers between devices, local(): diag = lax.ppermute(diag, LAT + LON, pairs)  17.8 us
    pallas_call x6, Pallas kernels, call(): pl.pallas_call(body, out_shape=[jax.ShapeDtypeStruct(s, d) for s, d in ou...  11.7 us
    ppermute x2, starting transfers between devices, from_next(): return lax.ppermute(array, axis, [((i + 1) % size, i) for i in range(size)])  11.2 us
    ppermute x2, starting transfers between devices, to_next(): return lax.ppermute(array, axis, [(i, (i + 1) % size) for i in range(size)])  8.53 us
    ppermute x2, starting transfers between devices, swapped(): return lax.ppermute(array, 'core', [(0, 1), (1, 0)])  5.96 us
    unnamed x22, local copies, waits for them, and re-layouts  5.84 us
  transfers between devices with their start and end apart: 11, of which 6 were waited for; matrix products, arithmetic and copies ran while one was open for 1% of the time, Pallas kernels for 2%

profile of v4, /device:TPU:1, one launch (start us, length us, event | category | flops | bytes accessed | tf_op | source)
XLA Modules:
  0.0 130.9 jit_solution(12444764481375807795)
XLA Ops:
  0.7 1.9 %send_kernel.1 = (bf16[256,384]{1,0:T(8,128)(2,1)}, bf16[64,384]{1,0:T(8,128)(2,1)}, bf16[64,384]{1,0:T(8,128)(2,1)}) custom-call(bf16[2,8,16,384]{3,2,1,0:T(8,128)(2,1)} %refs_0_.5, bf16[2,8,16,384]{3,2,1,0:T(8,128)(2,1)} %refs_0_.6, bf16[32,128]{1,0:T(8,128)(2,1)} %constant.32.clone.refs_2_), custom_call_target="tpu_custom_call" | custom-call | tf_op jit(solution)/shard_map/send_kernel/pallas_call | solution.py:65
  2.5 8.8 %collective-permute-start = (bf16[256,384]{1,0:T(8,128)(2,1)}, bf16[256,384]{1,0:T(8,128)(2,1)S(1)}, u32[]{:S(2)}, u32[]{:S(2)}) collective-permute-start(bf16[256,384]{1,0:T(8,128)(2,1)} %get-tuple-element.30), channel_id=1, source_target_pairs={{32,0},{64,32},{96,64},{128,96},{160,128},{192,160},{224,192},{256... | collective-permute-start | bytes 589832 | tf_op jit(solution)/shard_map/ppermute | solution.py:280
  11.3 17.8 %collective-permute-start.1 = (bf16[64,384]{1,0:T(8,128)(2,1)}, bf16[64,384]{1,0:T(8,128)(2,1)S(1)}, u32[]{:S(2)}, u32[]{:S(2)}) collective-permute-start(bf16[64,384]{1,0:T(8,128)(2,1)} %get-tuple-element.31), channel_id=1, source_target_pairs={{33,0},{34,1},{35,2},{36,3},{37,4},{38,5},{39,6},{40,7},{41,8},{42... | collective-permute-start | bytes 147464 | tf_op jit(solution)/shard_map/ppermute | solution.py:294
  29.1 2.4 %collective-permute-start.2 = (bf16[64,384]{1,0:T(8,128)(2,1)}, bf16[64,384]{1,0:T(8,128)(2,1)S(1)}, u32[]{:S(2)}, u32[]{:S(2)}) collective-permute-start(bf16[64,384]{1,0:T(8,128)(2,1)} %get-tuple-element.32), channel_id=1, source_target_pairs={{1,0},{2,1},{3,2},{4,3},{5,4},{6,5},{7,6},{8,7},{9,8},{10,9},{11,1... | collective-permute-start | bytes 147464 | tf_op jit(solution)/shard_map/ppermute | solution.py:280
  31.5 1.2 copy-done
  32.7 0.9 copy-done.2
  33.6 0.9 copy-done.3
  34.5 1.0 copy-done.5
  35.5 0.9 copy-done.6
  36.4 0.9 copy-done.7
  37.3 1.4 %stage_kernel.1 = (bf16[2,8,16,384]{3,2,1,0:T(8,128)(2,1)S(1)}, bf16[256,320]{1,0:T(8,128)(2,1)S(1)}, bf16[384,1152]{1,0:T(8,128)(2,1)S(1)}, bf16[2,8,16,384]{3,...) custom-call(bf16[2,8,16,384]{3,2,1,0:T(8,128)(2,1)S(1)} %copy-done.2, ...), custom_call_target="tpu_custom_call" | custom-call | tf_op jit(solution)/shard_map/stage_kernel/pallas_call | solution.py:65
  38.8 5.4 %window_kernel.1 = (bf16[2,2304,128]{2,1,0:T(8,128)(2,1)S(1)}, bf16[128,384]{1,0:T(8,128)(2,1)S(1)}, bf16[128,384]{1,0:T(8,128)(2,1)S(1)}, bf16[64,384]{1,0:T(8,128)(2,1)S(1)}) custom-call(s32[1]{0:T(128)} %bitcast.refs_0_, s32[2,16]{1,0:T(2,128)S(1)} %bitcast.11, bf16[2,8,16,384]{3,2,1,0:T(8,128)(2,1)S(1)} %get-tuple-element.24.refs_2_, ...), custom_call_target="tpu_custom_call" | custom-call | tf_op jit(solution)/shard_map/window_kernel/pallas_call | solution.py:65
  44.3 2.7 %collective-permute-start.3 = (bf16[2304,128]{1,0:T(8,128)(2,1)S(1)}, bf16[2304,128]{1,0:T(8,128)(2,1)S(1)}, u32[]{:S(2)}, u32[]{:S(2)}) collective-permute-start(bf16[2304,128]{1,0:T(8,128)(2,1)S(1)} %slice_bitcast_fusion), channel_id=1, source_target_pairs={{0,32},{32,0},{1,33},{33,1},{2,34},{34,2},{3,35},{35,3},{4,36},{36... | collective-permute-start | bytes 1769480 | tf_op jit(solution)/shard_map/ppermute | solution.py:265
  47.0 1.6 %collective-permute-done.3 = bf16[2304,128]{1,0:T(8,128)(2,1)S(1)} collective-permute-done((bf16[2304,128]{1,0:T(8,128)(2,1)S(1)}, bf16[2304,128]{1,0:T(8,128)(2,1)S(1)}, u32[]{:S(2)}, u32[]{:S(2)}) %collective-permute-start.3) | collective-permute-done | bytes 589856 | tf_op jit(solution)/shard_map/ppermute | solution.py:265
  48.6 1.0 fusion
  49.6 3.7 %all-to-all-start = ((bf16[16,144,128]{2,1,0:T(8,128)(2,1)}), bf16[16,144,128]{2,1,0:T(8,128)(2,1)S(1)}, u32[]{:S(2)}, u32[]{:S(2)}) async-start(bf16[16,144,128]{2,1,0:T(8,128)(2,1)} %bitcast.4), calls=%async_computation | async-start | bytes 1179648 | tf_op jit(solution)/shard_map/all_to_all | solution.py:252
  53.3 3.1 %collective-permute-start.4 = (bf16[64,384]{1,0:T(8,128)(2,1)S(1)}, bf16[64,384]{1,0:T(8,128)(2,1)S(1)}, u32[]{:S(2)}, u32[]{:S(2)}) collective-permute-start(bf16[64,384]{1,0:T(8,128)(2,1)S(1)} %get-tuple-element.35), channel_id=1, source_target_pairs={{0,1},{1,2},{2,3},{3,4},{4,5},{5,6},{6,7},{7,8},{8,9},{9,10},{10,1... | collective-permute-start | bytes 147464 | tf_op jit(solution)/shard_map/ppermute | solution.py:283
  56.4 7.5 %all-to-all-done = bf16[16,144,128]{2,1,0:T(8,128)(2,1)S(1)} async-done(((bf16[16,144,128]{2,1,0:T(8,128)(2,1)}), bf16[16,144,128]{2,1,0:T(8,128)(2,1)S(1)}, u32[]{:S(2)}, u32[]{:S(2)}) %all-to-all-start) | async-done | bytes 589856 | tf_op jit(solution)/shard_map/all_to_all | solution.py:252
  64.1 0.7 reshape.26
  64.7 11.1 %all-to-all-start.1 = ((bf16[16,9,128]{2,1,0:T(8,128)(2,1)}), bf16[16,9,128]{2,1,0:T(8,128)(2,1)S(1)}, u32[]{:S(2)}, u32[]{:S(2)}) async-start(bf16[16,9,128]{2,1,0:T(8,128)(2,1)} %reshape.26), calls=%async_computation.1 | async-start | bytes 131072 | tf_op jit(solution)/shard_map/all_to_all | solution.py:252
  76.0 11.4 %all-to-all-done.1 = bf16[16,9,128]{2,1,0:T(8,128)(2,1)S(1)} async-done(((bf16[16,9,128]{2,1,0:T(8,128)(2,1)}), bf16[16,9,128]{2,1,0:T(8,128)(2,1)S(1)}, u32[]{:S(2)}, u32[]{:S(2)}) %all-to-all-start.1) | async-done | bytes 36896 | tf_op jit(solution)/shard_map/all_to_all | solution.py:252
  87.5 0.6 broadcast_in_dim.6
  88.1 3.5 %all-to-all-start.2 = ((bf16[16,9,128]{2,1,0:T(8,128)(2,1)}), bf16[16,9,128]{2,1,0:T(8,128)(2,1)S(1)}, u32[]{:S(2)}, u32[]{:S(2)}) async-start(bf16[16,9,128]{2,1,0:T(8,128)(2,1)} %broadcast_in_dim.6), calls=%async_computation.2 | async-start | bytes 131072 | tf_op jit(solution)/shard_map/all_to_all | solution.py:252
  91.6 5.4 %collective-permute-start.5 = (bf16[128,384]{1,0:T(8,128)(2,1)S(1)}, bf16[128,384]{1,0:T(8,128)(2,1)S(1)}, u32[]{:S(2)}, u32[]{:S(2)}) collective-permute-start(bf16[128,384]{1,0:T(8,128)(2,1)S(1)} %join_kernel.1), channel_id=1, source_target_pairs={{0,32},{32,64},{64,96},{96,128},{128,160},{160,192},{192,224},{224... | collective-permute-start | bytes 294920 | tf_op jit(solution)/shard_map/ppermute | solution.py:283
  97.0 6.2 %all-to-all-done.2 = bf16[16,9,128]{2,1,0:T(8,128)(2,1)S(1)} async-done(((bf16[16,9,128]{2,1,0:T(8,128)(2,1)}), bf16[16,9,128]{2,1,0:T(8,128)(2,1)S(1)}, u32[]{:S(2)}, u32[]{:S(2)}) %all-to-all-start.2) | async-done | bytes 36896 | tf_op jit(solution)/shard_map/all_to_all | solution.py:252
  103.3 0.9 broadcast_in_dim.15
  104.2 8.4 %all-to-all-start.3 = ((bf16[16,144,128]{2,1,0:T(8,128)(2,1)}), bf16[16,144,128]{2,1,0:T(8,128)(2,1)S(1)}, u32[]{:S(2)}, u32[]{:S(2)}) async-start(bf16[16,144,128]{2,1,0:T(8,128)(2,1)} %broadcast_in_dim.15), calls=%async_computation.3 | async-start | bytes 1179648 | tf_op jit(solution)/shard_map/all_to_all | solution.py:252
  112.6 1.1 token_kernel.1
  113.8 10.7 %all-to-all-done.3 = bf16[16,144,128]{2,1,0:T(8,128)(2,1)S(1)} async-done(((bf16[16,144,128]{2,1,0:T(8,128)(2,1)}), bf16[16,144,128]{2,1,0:T(8,128)(2,1)S(1)}, u32[]{:S(2)}, u32[]{:S(2)}) %all-to-all-start.3) | async-done | bytes 589856 | tf_op jit(solution)/shard_map/all_to_all | solution.py:252
  124.5 3.3 %collective-permute-start.6 = (bf16[2304,128]{1,0:T(8,128)(2,1)S(1)}, bf16[2304,128]{1,0:T(8,128)(2,1)S(1)}, u32[]{:S(2)}, u32[]{:S(2)}) collective-permute-start(bf16[2304,128]{1,0:T(8,128)(2,1)S(1)} %bitcast.9), channel_id=1, source_target_pairs={{0,32},{32,0},{1,33},{33,1},{2,34},{34,2},{3,35},{35,3},{4,36},{36... | collective-permute-start | bytes 1769480 | tf_op jit(solution)/shard_map/ppermute | solution.py:265
  127.7 1.6 %collective-permute-done.6.refs_3_ = bf16[2304,128]{1,0:T(8,128)(2,1)S(1)} collective-permute-done((bf16[2304,128]{1,0:T(8,128)(2,1)S(1)}, bf16[2304,128]{1,0:T(8,128)(2,1)S(1)}, u32[]{:S(2)}, u32[]{:S(2)}) %collective-permute-start.6) | collective-permute-done | bytes 589856 | tf_op jit(solution)/shard_map/ppermute | solution.py:265
  129.3 1.6 %result_kernel.1 = (bf16[384,1152]{1,0:T(8,128)(2,1)}, bf16[384,384]{1,0:T(8,128)(2,1)}, bf16[384]{0:T(512)(128)(2,1)}) custom-call(s32[1]{0:T(128)} %bitcast.refs_0_, bf16[384,1152]{1,0:T(8,128)(2,1)S(1)} %copy-done.1, bf16[2304,128]{1,0:T(8,128)(2,1)S(1)} %bitcast.10, bf16[2304,128]{1,0:T(8,128)(2,1)S(1)} %collective-permute-done.6.refs_3_, ...), custom_call_target="tpu_custom_call" | custom-call | tf_op jit(solution)/shard_map/result_kernel/pallas_call | solution.py:65
  (26 shorter events, 0.4 us)
Async XLA Ops:
  0.6 38.1 %copy-start.8 = (bf16[384]{0:T(512)(128)(2,1)S(1)}, bf16[384]{0:T(512)(128)(2,1)}, u32[]{:S(2)}) copy-start(bf16[384]{0:T(512)(128)(2,1)} %refs_4_.3) | copy-start | bytes 2308
  0.6 38.1 %copy-start.9 = (s32[16,2]{0,1:T(2,128)S(1)}, s32[16,2]{0,1:T(2,128)}, u32[]{:S(2)}) copy-start(s32[16,2]{0,1:T(2,128)} %param.13) | copy-start | bytes 388
  2.5 36.2 %collective-permute-start = (bf16[256,384]{1,0:T(8,128)(2,1)}, bf16[256,384]{1,0:T(8,128)(2,1)S(1)}, u32[]{:S(2)}, u32[]{:S(2)}) collective-permute-start(bf16[256,384]{1,0:T(8,128)(2,1)} %get-tuple-element.30), channel_id=1, source_target_pairs={{32,0},{64,32},{96,64},{128,96},{160,128},{192,160},{224,192},{256... | collective-permute-start | bytes 589832 | tf_op jit(solution)/shard_map/ppermute | solution.py:280
  11.3 27.4 %collective-permute-start.1 = (bf16[64,384]{1,0:T(8,128)(2,1)}, bf16[64,384]{1,0:T(8,128)(2,1)S(1)}, u32[]{:S(2)}, u32[]{:S(2)}) collective-permute-start(bf16[64,384]{1,0:T(8,128)(2,1)} %get-tuple-element.31), channel_id=1, source_target_pairs={{33,0},{34,1},{35,2},{36,3},{37,4},{38,5},{39,6},{40,7},{41,8},{42... | collective-permute-start | bytes 147464 | tf_op jit(solution)/shard_map/ppermute | solution.py:294
  29.1 9.6 %collective-permute-start.2 = (bf16[64,384]{1,0:T(8,128)(2,1)}, bf16[64,384]{1,0:T(8,128)(2,1)S(1)}, u32[]{:S(2)}, u32[]{:S(2)}) collective-permute-start(bf16[64,384]{1,0:T(8,128)(2,1)} %get-tuple-element.32), channel_id=1, source_target_pairs={{1,0},{2,1},{3,2},{4,3},{5,4},{6,5},{7,6},{8,7},{9,8},{10,9},{11,1... | collective-permute-start | bytes 147464 | tf_op jit(solution)/shard_map/ppermute | solution.py:280
  31.5 1.2 copy-start
  32.7 0.9 copy-start.2
  33.6 0.9 copy-start.3
  34.5 1.0 copy-start.5
  35.5 0.9 copy-start.6
  36.4 0.9 copy-start.7
  44.3 4.3 %collective-permute-start.3 = (bf16[2304,128]{1,0:T(8,128)(2,1)S(1)}, bf16[2304,128]{1,0:T(8,128)(2,1)S(1)}, u32[]{:S(2)}, u32[]{:S(2)}) collective-permute-start(bf16[2304,128]{1,0:T(8,128)(2,1)S(1)} %slice_bitcast_fusion), channel_id=1, source_target_pairs={{0,32},{32,0},{1,33},{33,1},{2,34},{34,2},{3,35},{35,3},{4,36},{36... | collective-permute-start | bytes 1769480 | tf_op jit(solution)/shard_map/ppermute | solution.py:265
  49.5 26.3 %copy-start.10 = (bf16[128,32]{1,0:T(8,128)(2,1)S(1)}, bf16[128,32]{1,0:T(8,128)(2,1)}, u32[]{:S(2)}) copy-start(bf16[128,32]{1,0:T(8,128)(2,1)} %constant.35.clone.refs_0_.refs_1_) | copy-start | bytes 24580
  49.6 14.4 %all-to-all-start = ((bf16[16,144,128]{2,1,0:T(8,128)(2,1)}), bf16[16,144,128]{2,1,0:T(8,128)(2,1)S(1)}, u32[]{:S(2)}, u32[]{:S(2)}) async-start(bf16[16,144,128]{2,1,0:T(8,128)(2,1)} %bitcast.4), calls=%async_computation | async-start | bytes 1179648 | tf_op jit(solution)/shard_map/all_to_all | solution.py:252
  53.3 22.5 %collective-permute-start.4 = (bf16[64,384]{1,0:T(8,128)(2,1)S(1)}, bf16[64,384]{1,0:T(8,128)(2,1)S(1)}, u32[]{:S(2)}, u32[]{:S(2)}) collective-permute-start(bf16[64,384]{1,0:T(8,128)(2,1)S(1)} %get-tuple-element.35), channel_id=1, source_target_pairs={{0,1},{1,2},{2,3},{3,4},{4,5},{5,6},{6,7},{7,8},{8,9},{9,10},{10,1... | collective-permute-start | bytes 147464 | tf_op jit(solution)/shard_map/ppermute | solution.py:283
  64.7 22.8 %all-to-all-start.1 = ((bf16[16,9,128]{2,1,0:T(8,128)(2,1)}), bf16[16,9,128]{2,1,0:T(8,128)(2,1)S(1)}, u32[]{:S(2)}, u32[]{:S(2)}) async-start(bf16[16,9,128]{2,1,0:T(8,128)(2,1)} %reshape.26), calls=%async_computation.1 | async-start | bytes 131072 | tf_op jit(solution)/shard_map/all_to_all | solution.py:252
  76.0 36.6 %copy-start.4 = (bf16[2,8,16,384]{3,2,1,0:T(8,128)(2,1)S(1)}, bf16[2,8,16,384]{3,2,1,0:T(8,128)(2,1)}, u32[]{:S(2)}) copy-start(bf16[2,8,16,384]{3,2,1,0:T(8,128)(2,1)} %refs_0_.6) | copy-start | bytes 589828
  88.1 15.1 %all-to-all-start.2 = ((bf16[16,9,128]{2,1,0:T(8,128)(2,1)}), bf16[16,9,128]{2,1,0:T(8,128)(2,1)S(1)}, u32[]{:S(2)}, u32[]{:S(2)}) async-start(bf16[16,9,128]{2,1,0:T(8,128)(2,1)} %broadcast_in_dim.6), calls=%async_computation.2 | async-start | bytes 131072 | tf_op jit(solution)/shard_map/all_to_all | solution.py:252
  91.6 20.9 %collective-permute-start.5 = (bf16[128,384]{1,0:T(8,128)(2,1)S(1)}, bf16[128,384]{1,0:T(8,128)(2,1)S(1)}, u32[]{:S(2)}, u32[]{:S(2)}) collective-permute-start(bf16[128,384]{1,0:T(8,128)(2,1)S(1)} %join_kernel.1), channel_id=1, source_target_pairs={{0,32},{32,64},{64,96},{96,128},{128,160},{160,192},{192,224},{224... | collective-permute-start | bytes 294920 | tf_op jit(solution)/shard_map/ppermute | solution.py:283
  104.2 20.3 %all-to-all-start.3 = ((bf16[16,144,128]{2,1,0:T(8,128)(2,1)}), bf16[16,144,128]{2,1,0:T(8,128)(2,1)S(1)}, u32[]{:S(2)}, u32[]{:S(2)}) async-start(bf16[16,144,128]{2,1,0:T(8,128)(2,1)} %broadcast_in_dim.15), calls=%async_computation.3 | async-start | bytes 1179648 | tf_op jit(solution)/shard_map/all_to_all | solution.py:252
  112.6 16.7 %copy-start.1 = (bf16[384,1152]{1,0:T(8,128)(2,1)S(1)}, bf16[384,1152]{1,0:T(8,128)(2,1)}, u32[]{:S(2)}) copy-start(bf16[384,1152]{1,0:T(8,128)(2,1)} %refs_1_.5) | copy-start | bytes 2654212
  124.5 4.9 %collective-permute-start.6 = (bf16[2304,128]{1,0:T(8,128)(2,1)S(1)}, bf16[2304,128]{1,0:T(8,128)(2,1)S(1)}, u32[]{:S(2)}, u32[]{:S(2)}) collective-permute-start(bf16[2304,128]{1,0:T(8,128)(2,1)S(1)} %bitcast.9), channel_id=1, source_target_pairs={{0,32},{32,0},{1,33},{33,1},{2,34},{34,2},{3,35},{35,3},{4,36},{36... | collective-permute-start | bytes 1769480 | tf_op jit(solution)/shard_map/ppermute | solution.py:265

commit v5 on v4

--- a/solution.py
+++ b/solution.py
@@ -74,38 +74,66 @@
     )(*scalars, *far, *args)
 
 
-def pick_matrix():
-    pick = np.zeros((2 * WIN, 320), np.float32)
+PICK = (slice(0, 128), slice(128, 224), slice(256, 288), slice(384, 416))
+PUT = 256
+EDGE_PICK = (slice(256, 384), slice(384, 416))
+EDGE_PUT = 384
+
+
+def constants():
+    pick = np.zeros((2 * WIN, 512), np.float32)
+    back = np.zeros((288, 2 * WIN), np.float32)
+    edge = np.zeros((WIN, 256), np.float32)
+    edge_back = np.zeros((160, WIN), np.float32)
     for w in range(2):
         for level in range(2):
             for r in range(8):
                 for c in range(8):
                     col, row, below = 4 + 8 * w + c, r % 4, r // 4
-                    if col < 16:
-                        source = 128 * below + level * 64 + row * 16 + col
+                    token = w * WIN + level * 64 + r * 8 + c
+                    corner = level * 16 + row * 4 + col - 16
+                    grid = level * 64 + row * 16 + col
+                    if col >= 16:
+                        pick[token, (256 if below else 384) + corner] = 1
+                        back[(224 if below else 256) + corner, token] = 1
+                    elif below:
+                        inner = level * 48 + row * 12 + col - 4
+                        pick[token, 128 + inner] = 1
+                        back[128 + inner, token] = 1
                     else:
-                        source = 288 - 32 * below + level * 16 + row * 4 + col - 16
-                    pick[w * WIN + level * 64 + r * 8 + c, source] = 1
-    return pick
-
-
-def corner_matrix():
-    corner = np.zeros((32, 128), np.float32)
+                        pick[token, grid] = 1
+                        back[grid, token] = 1
+                    if r < 4:
+                        token = w * 64 + level * 32 + r * 8 + c
+                        edge[token, 128 + corner if col >= 16 else grid] = 1
+                        edge_back[128 + corner if col >= 16 else grid, token] = 1
+    packed = np.zeros((544, 512), np.float32)
+    packed[0:256] = pick
+    packed[256:544, 0:256] = back
+    packed[256:384, 256:512] = edge
+    packed[384:544, 256:384] = edge_back
+    return packed
+
+
+def columns_matrix():
+    columns = np.zeros((128, 128), np.float32)
     for row in range(8):
-        for col in range(4):
-            corner[row * 4 + col, row * 16 + col] = 1
-    return corner
-
-
-def send_kernel(tok, cot, corner, lat_out, diag_out, lon_out):
+        for col in range(16):
+            at = row * 4 + col if col < 4 else 32 + row * 12 + col - 4
+            columns[at, row * 16 + col] = 1
+    return columns
+
+
+def send_kernel(tok, cot, columns, lat_out, diag_out, lon_out):
     refs = [tok.get(), cot.get()]
-    pick = corner.get()[...]
+    pick = columns.get()[...]
     for i, ref in enumerate(refs):
-        upper = ref[:, 0:4].reshape(WIN, -1)
-        lower = ref[:, 4:8].reshape(WIN, -1)
-        lat_out[i * WIN : (i + 1) * WIN] = upper
-        diag_out[i * 32 : (i + 1) * 32] = dot(pick, upper).astype(BF16)
-        lon_out[i * 32 : (i + 1) * 32] = dot(pick, lower).astype(BF16)
+        upper = dot(pick, ref[:, 0:4].reshape(WIN, -1)).astype(BF16)
+        lower = dot(pick[0:32], ref[:, 4:8].reshape(WIN, -1)).astype(BF16)
+        lat_out[i * 96 : (i + 1) * 96] = upper[32:128]
+        diag_out[i * 32 : (i + 1) * 32] = upper[0:32]
+        lon_out[i * 32 : (i + 1) * 32] = lower
+        lon_out[64 + i * 32 : 64 + (i + 1) * 32] = upper[0:32]
 
 
 def stage_kernel(*refs):
@@ -115,8 +143,8 @@
 
 
 def window_kernel(
-    place, ocean_mask, tok, pick, w_qkv, cot, w_out, put, lat, diag, lon, gain,
-    grads, own_back, lat_back, side_back,
+    place, ocean_mask, tok, const, w_qkv, cot, w_out, lat, diag, lon, gain,
+    grads, own_back, lat_back, side_back, edge_back,
     left, right, packed, d_att,
 ):
     dim = lat.shape[1]
@@ -125,38 +153,26 @@
     last_band = (lat_index == ocean_mask.shape[1] - 1).astype(jnp.int32)
     scale = HDIM ** (-0.5)
     gains = gain[...].reshape(1, dim).astype(F32)
-
-    def assembled(i, ref):
-        return (
-            dot(pick[:, 0:128], ref[:, 4:8].reshape(WIN, dim))
-            + dot(pick[:, 128:256], lat[i * WIN : (i + 1) * WIN])
-            + dot(pick[:, 256:288], diag[i * 32 : (i + 1) * 32])
-            + dot(pick[:, 288:320], lon[i * 32 : (i + 1) * 32])
-        )
-
-    x = assembled(0, tok)
-    in_first = lax.broadcasted_iota(jnp.int32, (2 * WIN, 1), 0) < WIN
-    ocean = jnp.where(in_first, ocean_mask[0, lat_index], ocean_mask[1, lat_index]).astype(F32)
-    g = (assembled(1, cot) * ocean).astype(BF16)
-    centered = x - jnp.mean(x, -1, keepdims=True)
-    rstd = lax.rsqrt(jnp.mean(centered * centered, -1, keepdims=True) + 1e-5)
-    xhat = centered * rstd
-    normed_full = xhat * gains
-    normed = normed_full.astype(BF16)
-    left[0] = normed_full.T.astype(BF16)
-    packed[...] = dot(normed, w_qkv[...]).astype(BF16)
-    d_att[...] = dot_nt(g, w_out[...]).astype(BF16)
-    for j in range(dim // LANES):
-        right[9 + j] = g[:, j * LANES : (j + 1) * LANES]
-
     lane = lax.broadcasted_iota(jnp.int32, (1, LANES), 1)
     masks = [(lane // HDIM == h).astype(F32).astype(BF16) for h in range(PACK)]
-    key_row = lax.broadcasted_iota(jnp.int32, (WIN, PACK * WIN), 0) // 8 % 8 >= 4
-    query_row = lax.broadcasted_iota(jnp.int32, (WIN, PACK * WIN), 1) // 8 % 8 >= 4
-    differ = (key_row != query_row).astype(jnp.int32) * last_band > 0
-
-    for w in range(2):
-        rows = slice(w * WIN, (w + 1) * WIN)
+    key_at = lax.broadcasted_iota(jnp.int32, (WIN, PACK * WIN), 0)
+    query_at = lax.broadcasted_iota(jnp.int32, (WIN, PACK * WIN), 1) % WIN
+
+    def project(x, g, first):
+        rows = slice(first, first + x.shape[0])
+        centered = x - jnp.mean(x, -1, keepdims=True)
+        rstd = lax.rsqrt(jnp.mean(centered * centered, -1, keepdims=True) + 1e-5)
+        xhat = centered * rstd
+        normed = xhat * gains
+        left[0, :, rows] = normed.T.astype(BF16)
+        packed[rows] = dot(normed.astype(BF16), w_qkv[...]).astype(BF16)
+        d_att[rows] = dot_nt(g, w_out[...]).astype(BF16)
+        for j in range(dim // LANES):
+            right[9 + j, rows] = g[:, j * LANES : (j + 1) * LANES]
+        return xhat, rstd
+
+    def attend(first, differ):
+        rows = slice(first, first + WIN)
         for group in range(HEADS // PACK):
             cols = [slice(p * dim + group * LANES, p * dim + (group + 1) * LANES) for p in range(3)]
             query, keys, values = packed[rows, cols[0]], packed[rows, cols[1]], packed[rows, cols[2]]
@@ -184,35 +200,83 @@
             right[3 + group, rows] = dot(d_scores, query_heads).astype(BF16)
             right[6 + group, rows] = dot(weights, d_out_heads).astype(BF16)
 
-    for j in range(12):
-        half, at = j // 6, j % 6
-        slot = lax.rem(half + core, 2)
-        term = dot(left[j // 9], right[j])
-        grads[slot, at * dim : (at + 1) * dim] = term.astype(BF16)
-
-    d_packed = jnp.concatenate([right[j] for j in range(9)], 1)
-    d_normed = dot_nt(d_packed, w_qkv[...])
-    d_hat = d_normed * gains
-    branch = rstd * (
-        d_hat
-        - jnp.mean(d_hat, -1, keepdims=True)
-        - xhat * jnp.mean(d_hat * xhat, -1, keepdims=True)
-    )
-    back = dot(put[...], branch.astype(BF16)).astype(BF16)
+    def branch(first, xhat, rstd):
+        rows = slice(first, first + xhat.shape[0])
+        d_packed = jnp.concatenate([right[j, rows] for j in range(9)], 1)
+        d_normed = dot_nt(d_packed, w_qkv[...])
+        d_hat = d_normed * gains
+        d_branch = rstd * (
+            d_hat
+            - jnp.mean(d_hat, -1, keepdims=True)
+            - xhat * jnp.mean(d_hat * xhat, -1, keepdims=True)
+        )
+        return d_branch.astype(BF16)
+
+    def emit(count):
+        for j in range(12):
+            half, at = j // 6, j % 6
+            slot = lax.rem(half + core, 2)
+            term = dot(left[j // 9, :, 0:count], right[j, 0:count])
+            grads[slot, at * dim : (at + 1) * dim] = term.astype(BF16)
+
+    def assembled(i, ref):
+        return (
+            dot(const[0:256, PICK[0]], ref[:, 4:8].reshape(WIN, dim))
+            + dot(const[0:256, PICK[1]], lat[i * 96 : (i + 1) * 96])
+            + dot(const[0:256, PICK[2]], diag[i * 32 : (i + 1) * 32])
+            + dot(const[0:256, PICK[3]], lon[i * 32 : (i + 1) * 32])
+        )
+
+    def ocean(band, rows, size):
+        first = lax.broadcasted_iota(jnp.int32, (rows, 1), 0) < size
+        return jnp.where(first, ocean_mask[0, band], ocean_mask[1, band]).astype(F32)
+
+    g = (assembled(1, cot) * ocean(lat_index, 2 * WIN, WIN)).astype(BF16)
+    xhat, rstd = project(assembled(0, tok), g, 0)
+    lower_differs = ((key_at // 8 % 8 >= 4) != (query_at // 8 % 8 >= 4)).astype(jnp.int32)
+    for w in range(2):
+        attend(w * WIN, lower_differs * last_band > 0)
+
+    @pl.when(lat_index == 0)
+    def _():
+        def edge(i, ref):
+            return dot(const[256:384, EDGE_PICK[0]], ref[:, 0:4].reshape(WIN, dim)) + dot(
+                const[256:384, EDGE_PICK[1]], lon[64 + i * 32 : 64 + (i + 1) * 32]
+            )
+
+        last = ocean_mask.shape[1] - 1
+        edge_g = (edge(1, cot) * ocean(last, WIN, 64)).astype(BF16)
+        edge_xhat, edge_rstd = project(edge(0, tok), edge_g, 2 * WIN)
+        attend(2 * WIN, key_at // 64 != query_at // 64)
+        edge_branch = branch(2 * WIN, edge_xhat, edge_rstd)
+        edge_back[...] = dot(const[EDGE_PUT : EDGE_PUT + 160, 256:384], edge_branch).astype(BF16)
+        emit(3 * WIN)
+
+    @pl.when(lat_index != 0)
+    def _():
+        edge_back[...] = jnp.zeros_like(edge_back)
+        emit(2 * WIN)
+
+    back = dot(const[PUT : PUT + 288, 0:256], branch(0, xhat, rstd)).astype(BF16)
     own_back[...] = back[0:128]
-    lat_back[...] = back[128:256]
-    side_back[...] = back[256:320]
-
-
-def join_kernel(spread, lat_back, side, out):
-    fill = spread.get()[...]
-    out[...] = (lat_back[...].astype(F32) + dot(fill, side[0:32])).astype(BF16)
-
-
-def token_kernel(cot, spread, own, lat, side, out):
+    lat_back[...] = back[128:224]
+    side_back[0:64] = back[224:288]
+    side_back[64:96] = edge_back[128:160]
+
+
+def join_kernel(lat_back, side, out):
+    out[0:96] = lat_back[...]
+    out[96:128] = side[0:32]
+
+
+def token_kernel(cot, spread, own, edge, lat, side, out):
     cot, fill = cot.get(), spread.get()[...]
-    lower = own[...].astype(F32) + dot(fill, side[32:64])
-    upper = lat[...].astype(F32)
+    lower = own[...].astype(F32) + dot(fill[:, 0:32], side[32:64])
+    upper = (
+        edge[0:128].astype(F32)
+        + dot(fill[:, 0:32], lat[96:128] + side[64:96])
+        + dot(fill[:, 128:224], lat[0:96])
+    )
     shape = (2, 4) + cot.shape[2:]
     out[:, 0:4] = (cot[:, 0:4].astype(F32) + upper.reshape(shape)).astype(BF16)
     out[:, 4:8] = (cot[:, 4:8].astype(F32) + lower.reshape(shape)).astype(BF16)
@@ -273,57 +337,59 @@
     dim = w_out.shape[0]
     n_lat, n_lon = lax.axis_size(LAT), lax.axis_size(LON)
     place = lax.axis_index(LAT).astype(jnp.int32).reshape(1)
-    corner, pick = corner_matrix(), pick_matrix()
     constant = functools.partial(jnp.asarray, dtype=BF16)
-
-    def from_next(array, axis, size):
-        return lax.ppermute(array, axis, [((i + 1) % size, i) for i in range(size)])
-
-    def to_next(array, axis, size):
-        return lax.ppermute(array, axis, [(i, (i + 1) % size) for i in range(size)])
+    columns = columns_matrix()
+    spread = np.zeros((128, 256), np.float32)
+    spread[:, 0:32], spread[:, 128:224] = columns[0:32].T, columns[32:128].T
 
     def place_of(a, b):
-        return (a % n_lat) * n_lon + b % n_lon
-
-    pairs = [(place_of(a + 1, b + 1), place_of(a, b)) for a in range(n_lat) for b in range(n_lon)]
+        return a * n_lon + b % n_lon
+
+    south = [(a, a + 1) for a in range(n_lat - 1)]
+    diagonal = [(place_of(a, b), place_of(a + 1, b + 1)) for a in range(n_lat - 1) for b in range(n_lon)]
+    east = [(b, (b + 1) % n_lon) for b in range(n_lon)]
+
+    def back(pairs):
+        return [(target, source) for source, target in pairs]
+
     lat, diag, lon = call(
-        send_kernel, [((2 * WIN, dim), BF16), ((64, dim), BF16), ((64, dim), BF16)],
-        far=(tokens, cotangent, constant(corner)), limit=60,
-    )
-    lat = from_next(lat, LAT, n_lat)
-    diag = lax.ppermute(diag, LAT + LON, pairs)
-    lon = from_next(lon, LON, n_lon)
-    near = (tokens, constant(pick), w_qkv, cotangent, w_out, constant(pick.T))
+        send_kernel, [((192, dim), BF16), ((64, dim), BF16), ((128, dim), BF16)],
+        far=(tokens, cotangent, constant(columns)), limit=60,
+    )
+    lat = lax.ppermute(lat, LAT, back(south))
+    diag = lax.ppermute(diag, LAT + LON, back(diagonal))
+    lon = lax.ppermute(lon, LON, back(east))
+    near = (tokens, constant(constants()), w_qkv, cotangent, w_out)
     near = call(stage_kernel, [(a.shape, BF16) for a in near], far=near)
     half = 6 * dim
-    grads, own_back, lat_back, side_back = call(
-        window_kernel,
-        [((2, half, LANES), BF16), ((WIN, dim), BF16), ((WIN, dim), BF16), ((64, dim), BF16)],
+    shapes = [(2, half, LANES), (WIN, dim), (96, dim), (96, dim), (160, dim)]
+    grads, own_back, lat_back, side_back, edge_back = call(
+        window_kernel, [(shape, BF16) for shape in shapes],
         *near, lat, diag, lon, gain,
         scalars=(place, ocean_mask.T),
         scratch=[
-            pltpu.VMEM((2, dim, 2 * WIN), BF16),
-            pltpu.VMEM((12, 2 * WIN, LANES), BF16),
-            pltpu.VMEM((2 * WIN, 3 * dim), BF16),
-            pltpu.VMEM((2 * WIN, dim), BF16),
+            pltpu.VMEM((2, dim, 3 * WIN), BF16),
+            pltpu.VMEM((12, 3 * WIN, LANES), BF16),
+            pltpu.VMEM((3 * WIN, 3 * dim), BF16),
+            pltpu.VMEM((3 * WIN, dim), BF16),
         ],
     )
 
-    side = to_next(side_back, LON, n_lon)
+    side = lax.ppermute(side_back, LON, east)
     mine = (grads[0].astype(F32) + swapped(grads[1]).astype(F32)).astype(BF16)
     mine = summed(exchange(mine.reshape(16, half // 16, LANES), PLANE))
     mine = summed(exchange(mine.reshape(16, half // 256, LANES), RING))
     (rows_back,) = call(
-        join_kernel, [((WIN, dim), BF16)], lat_back, side, far=(constant(corner.T),), flops=LONG
+        join_kernel, [((WIN, dim), BF16)], lat_back, side, flops=LONG
     )
     mine, rows_back = tied(mine, rows_back)
-    rows_back = to_next(rows_back, LAT, n_lat)
+    rows_back = lax.ppermute(rows_back, LAT, south)
     mine = spread_along(mine, RING).reshape(half // 16, LANES)
     mine = spread_along(mine, PLANE).reshape(half, LANES)
     (token_grad,) = call(
         token_kernel, [(tokens.shape, BF16)],
-        own_back, rows_back, side,
-        far=(cotangent, constant(corner.T)), flops=LONG,
+        own_back, edge_back, rows_back, side,
+        far=(cotangent, constant(spread)), flops=LONG,
     )
     mine, token_grad = tied(mine, token_grad)
     other = swapped(mine)

time: 132 us -> 127 us (0.962)
  starting transfers between devices: 70.1 us -> 63.9 us
  waiting for transfers between devices: 39.1 us -> 41.3 us
    ppermute x5, starting transfers between devices: 37.5 us -> 29.7 us  [the longest x1 9.95 us: local(): lon = lax.ppermute(lon, LON, back(east))]
    ppermute x5, waiting for transfers between devices: 0.01 us -> 2.42 us  [the longest x1 2.41 us: local(): diag = lax.ppermute(diag, LAT + LON, back(diagonal))]
    all_to_all x4, starting transfers between devices: 26.7 us -> 28.4 us  [exchange(): return lax.all_to_all(parts, axis, 0, 0, tiled=False)]
    unnamed x22 -> x20, local copies, waits for them, and re-layouts: 5.84 us -> 5.06 us
  transfers between devices with their start and end apart: 11 -> 11, of which waited for: 6 -> 7; matrix products, arithmetic and copies ran while one was open for 1% -> 1% of each run, Pallas kernels for 2% -> 2%
where the time goes in v5:
time: 127 us; the launch traced here: 126 us
  starting transfers between devices  63.9 us (50%)
  waiting for transfers between devices  41.3 us (33%)
  Pallas kernels  11.9 us (9%)
  local copies, waits for them, and re-layouts  7.32 us (6%)
    all_to_all x4, waiting for transfers between devices, exchange(): return lax.all_to_all(parts, axis, 0, 0, tiled=False)  35.6 us
    all_to_all x4, starting transfers between devices, exchange(): return lax.all_to_all(parts, axis, 0, 0, tiled=False)  28.4 us
    pallas_call x6, Pallas kernels, call(): pl.pallas_call(body, out_shape=[jax.ShapeDtypeStruct(s, d) for s, d in ou...  11.9 us
    ppermute x1, starting transfers between devices, local(): lon = lax.ppermute(lon, LON, back(east))  9.95 us
    ppermute x1, starting transfers between devices, local(): lat = lax.ppermute(lat, LAT, back(south))  8.79 us
    ppermute x2, starting transfers between devices, swapped(): return lax.ppermute(array, 'core', [(0, 1), (1, 0)])  5.79 us
    ppermute x1, starting transfers between devices, local(): rows_back = lax.ppermute(rows_back, LAT, south)  5.78 us
    unnamed x20, local copies, waits for them, and re-layouts  5.06 us
  transfers between devices with their start and end apart: 11, of which 7 were waited for; matrix products, arithmetic and copies ran while one was open for 1% of the time, Pallas kernels for 2%

profile of v5, /device:TPU:1, one launch (start us, length us, event | category | flops | bytes accessed | tf_op | source)
XLA Modules:
  0.0 126.3 jit_solution(1024990003558173969)
XLA Ops:
  0.6 2.0 %send_kernel.1 = (bf16[192,384]{1,0:T(8,128)(2,1)}, bf16[64,384]{1,0:T(8,128)(2,1)}, bf16[128,384]{1,0:T(8,128)(2,1)}) custom-call(bf16[2,8,16,384]{3,2,1,0:T(8,128)(2,1)} %refs_0_.4, bf16[2,8,16,384]{3,2,1,0:T(8,128)(2,1)} %refs_0_.5, bf16[128,128]{1,0:T(8,128)(2,1)} %constant.30.clone.refs_2_), custom_call_target="tpu_custom_call" | custom-call | tf_op jit(solution)/shard_map/send_kernel/pallas_call | solution.py:65
  2.6 8.8 %collective-permute-start = (bf16[192,384]{1,0:T(8,128)(2,1)}, bf16[192,384]{1,0:T(8,128)(2,1)S(1)}, u32[]{:S(2)}, u32[]{:S(2)}) collective-permute-start(bf16[192,384]{1,0:T(8,128)(2,1)} %get-tuple-element.29), channel_id=1, source_target_pairs={{32,0},{64,32},{96,64},{128,96},{160,128},{192,160},{224,192},{256... | collective-permute-start | bytes 442376 | tf_op jit(solution)/shard_map/ppermute | solution.py:359
  11.4 10.0 %collective-permute-start.2 = (bf16[128,384]{1,0:T(8,128)(2,1)}, bf16[128,384]{1,0:T(8,128)(2,1)S(1)}, u32[]{:S(2)}, u32[]{:S(2)}) collective-permute-start(bf16[128,384]{1,0:T(8,128)(2,1)} %get-tuple-element.31), channel_id=1, source_target_pairs={{1,0},{2,1},{3,2},{4,3},{5,4},{6,5},{7,6},{8,7},{9,8},{10,9},{11,1... | collective-permute-start | bytes 294920 | tf_op jit(solution)/shard_map/ppermute | solution.py:361
  21.4 1.9 %collective-permute-start.1 = (bf16[64,384]{1,0:T(8,128)(2,1)}, bf16[64,384]{1,0:T(8,128)(2,1)S(1)}, u32[]{:S(2)}, u32[]{:S(2)}) collective-permute-start(bf16[64,384]{1,0:T(8,128)(2,1)} %get-tuple-element.30), channel_id=1, source_target_pairs={{33,0},{34,1},{35,2},{36,3},{37,4},{38,5},{39,6},{40,7},{41,8},{42... | collective-permute-start | bytes 147464 | tf_op jit(solution)/shard_map/ppermute | solution.py:360
  23.3 1.2 copy-done
  24.5 0.9 copy-done.2
  25.4 0.9 copy-done.3
  26.3 1.1 copy-done.5
  27.4 1.0 copy-done.6
  28.4 1.0 stage_kernel.1
  29.4 2.4 %collective-permute-done.1.refs_8_ = bf16[64,384]{1,0:T(8,128)(2,1)S(1)} collective-permute-done((bf16[64,384]{1,0:T(8,128)(2,1)}, bf16[64,384]{1,0:T(8,128)(2,1)S(1)}, u32[]{:S(2)}, u32[]{:S(2)}) %collective-permute-start.1) | collective-permute-done | bytes 49184 | tf_op jit(solution)/shard_map/ppermute | solution.py:360
  31.8 6.0 %window_kernel.1 = (bf16[2,2304,128]{2,1,0:T(8,128)(2,1)S(1)}, bf16[128,384]{1,0:T(8,128)(2,1)S(1)}, bf16[96,384]{1,0:T(8,128)(2,1)S(1)}, bf16[96,384]{1,0:T(8,128)(2,1)S(1)}, bf16[160,384]{1,0:T(8,128)(2,1)S(1)}) custom-call(s32[1]{0:T(128)} %bitcast.refs_0_, s32[2,16]{1,0:T(2,128)S(1)} %bitcast.11, bf16[2,8,16,384]{3,2,1,0:T(8,128)(2,1)S(1)} %get-tuple-element.24.refs_2_, ...), custom_call_target="tpu_custom_call" | custom-call | tf_op jit(solution)/shard_map/window_kernel/pallas_call | solution.py:65
  37.9 2.8 %collective-permute-start.3 = (bf16[2304,128]{1,0:T(8,128)(2,1)S(1)}, bf16[2304,128]{1,0:T(8,128)(2,1)S(1)}, u32[]{:S(2)}, u32[]{:S(2)}) collective-permute-start(bf16[2304,128]{1,0:T(8,128)(2,1)S(1)} %slice_bitcast_fusion), channel_id=1, source_target_pairs={{0,32},{32,0},{1,33},{33,1},{2,34},{34,2},{3,35},{35,3},{4,36},{36... | collective-permute-start | bytes 1769480 | tf_op jit(solution)/shard_map/ppermute | solution.py:329
  40.7 1.6 %collective-permute-done.3 = bf16[2304,128]{1,0:T(8,128)(2,1)S(1)} collective-permute-done((bf16[2304,128]{1,0:T(8,128)(2,1)S(1)}, bf16[2304,128]{1,0:T(8,128)(2,1)S(1)}, u32[]{:S(2)}, u32[]{:S(2)}) %collective-permute-start.3) | collective-permute-done | bytes 589856 | tf_op jit(solution)/shard_map/ppermute | solution.py:329
  42.3 1.0 fusion
  43.3 10.3 %all-to-all-start = ((bf16[16,144,128]{2,1,0:T(8,128)(2,1)}), bf16[16,144,128]{2,1,0:T(8,128)(2,1)S(1)}, u32[]{:S(2)}, u32[]{:S(2)}) async-start(bf16[16,144,128]{2,1,0:T(8,128)(2,1)} %bitcast.4), calls=%async_computation | async-start | bytes 1179648 | tf_op jit(solution)/shard_map/all_to_all | solution.py:316
  53.6 3.3 %collective-permute-start.4 = (bf16[96,384]{1,0:T(8,128)(2,1)S(1)}, bf16[96,384]{1,0:T(8,128)(2,1)S(1)}, u32[]{:S(2)}, u32[]{:S(2)}) collective-permute-start(bf16[96,384]{1,0:T(8,128)(2,1)S(1)} %get-tuple-element.34), channel_id=1, source_target_pairs={{0,1},{1,2},{2,3},{3,4},{4,5},{5,6},{6,7},{7,8},{8,9},{9,10},{10,1... | collective-permute-start | bytes 221192 | tf_op jit(solution)/shard_map/ppermute | solution.py:378
  56.8 7.5 %all-to-all-done = bf16[16,144,128]{2,1,0:T(8,128)(2,1)S(1)} async-done(((bf16[16,144,128]{2,1,0:T(8,128)(2,1)}), bf16[16,144,128]{2,1,0:T(8,128)(2,1)S(1)}, u32[]{:S(2)}, u32[]{:S(2)}) %all-to-all-start) | async-done | bytes 589856 | tf_op jit(solution)/shard_map/all_to_all | solution.py:316
  64.4 0.7 reshape.26
  65.1 6.5 %all-to-all-start.1 = ((bf16[16,9,128]{2,1,0:T(8,128)(2,1)}), bf16[16,9,128]{2,1,0:T(8,128)(2,1)S(1)}, u32[]{:S(2)}, u32[]{:S(2)}) async-start(bf16[16,9,128]{2,1,0:T(8,128)(2,1)} %reshape.26), calls=%async_computation.1 | async-start | bytes 131072 | tf_op jit(solution)/shard_map/all_to_all | solution.py:316
  71.7 11.5 %all-to-all-done.1 = bf16[16,9,128]{2,1,0:T(8,128)(2,1)S(1)} async-done(((bf16[16,9,128]{2,1,0:T(8,128)(2,1)}), bf16[16,9,128]{2,1,0:T(8,128)(2,1)S(1)}, u32[]{:S(2)}, u32[]{:S(2)}) %all-to-all-start.1) | async-done | bytes 36896 | tf_op jit(solution)/shard_map/all_to_all | solution.py:316
  83.2 0.6 broadcast_in_dim.6
  83.9 3.5 %all-to-all-start.2 = ((bf16[16,9,128]{2,1,0:T(8,128)(2,1)}), bf16[16,9,128]{2,1,0:T(8,128)(2,1)S(1)}, u32[]{:S(2)}, u32[]{:S(2)}) async-start(bf16[16,9,128]{2,1,0:T(8,128)(2,1)} %broadcast_in_dim.6), calls=%async_computation.2 | async-start | bytes 131072 | tf_op jit(solution)/shard_map/all_to_all | solution.py:316
  87.4 5.8 %collective-permute-start.5 = (bf16[128,384]{1,0:T(8,128)(2,1)S(1)}, bf16[128,384]{1,0:T(8,128)(2,1)S(1)}, u32[]{:S(2)}, u32[]{:S(2)}) collective-permute-start(bf16[128,384]{1,0:T(8,128)(2,1)S(1)} %join_kernel.1), channel_id=1, source_target_pairs={{0,32},{32,64},{64,96},{96,128},{128,160},{160,192},{192,224},{224... | collective-permute-start | bytes 294920 | tf_op jit(solution)/shard_map/ppermute | solution.py:386
  93.2 5.8 %all-to-all-done.2 = bf16[16,9,128]{2,1,0:T(8,128)(2,1)S(1)} async-done(((bf16[16,9,128]{2,1,0:T(8,128)(2,1)}), bf16[16,9,128]{2,1,0:T(8,128)(2,1)S(1)}, u32[]{:S(2)}, u32[]{:S(2)}) %all-to-all-start.2) | async-done | bytes 36896 | tf_op jit(solution)/shard_map/all_to_all | solution.py:316
  99.0 0.9 broadcast_in_dim.15
  99.9 8.1 %all-to-all-start.3 = ((bf16[16,144,128]{2,1,0:T(8,128)(2,1)}), bf16[16,144,128]{2,1,0:T(8,128)(2,1)S(1)}, u32[]{:S(2)}, u32[]{:S(2)}) async-start(bf16[16,144,128]{2,1,0:T(8,128)(2,1)} %broadcast_in_dim.15), calls=%async_computation.3 | async-start | bytes 1179648 | tf_op jit(solution)/shard_map/all_to_all | solution.py:316
  108.0 1.3 token_kernel.1
  109.3 10.8 %all-to-all-done.3 = bf16[16,144,128]{2,1,0:T(8,128)(2,1)S(1)} async-done(((bf16[16,144,128]{2,1,0:T(8,128)(2,1)}), bf16[16,144,128]{2,1,0:T(8,128)(2,1)S(1)}, u32[]{:S(2)}, u32[]{:S(2)}) %all-to-all-start.3) | async-done | bytes 589856 | tf_op jit(solution)/shard_map/all_to_all | solution.py:316
  120.1 3.0 %collective-permute-start.6 = (bf16[2304,128]{1,0:T(8,128)(2,1)S(1)}, bf16[2304,128]{1,0:T(8,128)(2,1)S(1)}, u32[]{:S(2)}, u32[]{:S(2)}) collective-permute-start(bf16[2304,128]{1,0:T(8,128)(2,1)S(1)} %bitcast.9), channel_id=1, source_target_pairs={{0,32},{32,0},{1,33},{33,1},{2,34},{34,2},{3,35},{35,3},{4,36},{36... | collective-permute-start | bytes 1769480 | tf_op jit(solution)/shard_map/ppermute | solution.py:329
  123.1 1.6 %collective-permute-done.6.refs_3_ = bf16[2304,128]{1,0:T(8,128)(2,1)S(1)} collective-permute-done((bf16[2304,128]{1,0:T(8,128)(2,1)S(1)}, bf16[2304,128]{1,0:T(8,128)(2,1)S(1)}, u32[]{:S(2)}, u32[]{:S(2)}) %collective-permute-start.6) | collective-permute-done | bytes 589856 | tf_op jit(solution)/shard_map/ppermute | solution.py:329
  124.7 1.6 %result_kernel.1 = (bf16[384,1152]{1,0:T(8,128)(2,1)}, bf16[384,384]{1,0:T(8,128)(2,1)}, bf16[384]{0:T(512)(128)(2,1)}) custom-call(s32[1]{0:T(128)} %bitcast.refs_0_, bf16[384,1152]{1,0:T(8,128)(2,1)S(1)} %copy-done.1, bf16[2304,128]{1,0:T(8,128)(2,1)S(1)} %bitcast.10, bf16[2304,128]{1,0:T(8,128)(2,1)S(1)} %collective-permute-done.6.refs_3_, ...), custom_call_target="tpu_custom_call" | custom-call | tf_op jit(solution)/shard_map/result_kernel/pallas_call | solution.py:65
  (24 shorter events, 0.2 us)
Async XLA Ops:
  2.6 29.2 %copy-start.7 = (bf16[384]{0:T(512)(128)(2,1)S(1)}, bf16[384]{0:T(512)(128)(2,1)}, u32[]{:S(2)}) copy-start(bf16[384]{0:T(512)(128)(2,1)} %refs_4_.3) | copy-start | bytes 2308
  2.6 29.2 %copy-start.8 = (s32[16,2]{0,1:T(2,128)S(1)}, s32[16,2]{0,1:T(2,128)}, u32[]{:S(2)}) copy-start(s32[16,2]{0,1:T(2,128)} %param.11) | copy-start | bytes 388
  2.6 29.2 %collective-permute-start = (bf16[192,384]{1,0:T(8,128)(2,1)}, bf16[192,384]{1,0:T(8,128)(2,1)S(1)}, u32[]{:S(2)}, u32[]{:S(2)}) collective-permute-start(bf16[192,384]{1,0:T(8,128)(2,1)} %get-tuple-element.29), channel_id=1, source_target_pairs={{32,0},{64,32},{96,64},{128,96},{160,128},{192,160},{224,192},{256... | collective-permute-start | bytes 442376 | tf_op jit(solution)/shard_map/ppermute | solution.py:359
  11.4 20.4 %collective-permute-start.2 = (bf16[128,384]{1,0:T(8,128)(2,1)}, bf16[128,384]{1,0:T(8,128)(2,1)S(1)}, u32[]{:S(2)}, u32[]{:S(2)}) collective-permute-start(bf16[128,384]{1,0:T(8,128)(2,1)} %get-tuple-element.31), channel_id=1, source_target_pairs={{1,0},{2,1},{3,2},{4,3},{5,4},{6,5},{7,6},{8,7},{9,8},{10,9},{11,1... | collective-permute-start | bytes 294920 | tf_op jit(solution)/shard_map/ppermute | solution.py:361
  21.4 10.4 %collective-permute-start.1 = (bf16[64,384]{1,0:T(8,128)(2,1)}, bf16[64,384]{1,0:T(8,128)(2,1)S(1)}, u32[]{:S(2)}, u32[]{:S(2)}) collective-permute-start(bf16[64,384]{1,0:T(8,128)(2,1)} %get-tuple-element.30), channel_id=1, source_target_pairs={{33,0},{34,1},{35,2},{36,3},{37,4},{38,5},{39,6},{40,7},{41,8},{42... | collective-permute-start | bytes 147464 | tf_op jit(solution)/shard_map/ppermute | solution.py:360
  23.3 1.2 copy-start
  24.5 0.9 copy-start.2
  25.4 0.9 copy-start.3
  26.3 1.1 copy-start.5
  27.4 1.0 copy-start.6
  37.9 4.4 %collective-permute-start.3 = (bf16[2304,128]{1,0:T(8,128)(2,1)S(1)}, bf16[2304,128]{1,0:T(8,128)(2,1)S(1)}, u32[]{:S(2)}, u32[]{:S(2)}) collective-permute-start(bf16[2304,128]{1,0:T(8,128)(2,1)S(1)} %slice_bitcast_fusion), channel_id=1, source_target_pairs={{0,32},{32,0},{1,33},{33,1},{2,34},{34,2},{3,35},{35,3},{4,36},{36... | collective-permute-start | bytes 1769480 | tf_op jit(solution)/shard_map/ppermute | solution.py:329
  43.3 21.0 %all-to-all-start = ((bf16[16,144,128]{2,1,0:T(8,128)(2,1)}), bf16[16,144,128]{2,1,0:T(8,128)(2,1)S(1)}, u32[]{:S(2)}, u32[]{:S(2)}) async-start(bf16[16,144,128]{2,1,0:T(8,128)(2,1)} %bitcast.4), calls=%async_computation | async-start | bytes 1179648 | tf_op jit(solution)/shard_map/all_to_all | solution.py:316
  53.6 18.0 %collective-permute-start.4 = (bf16[96,384]{1,0:T(8,128)(2,1)S(1)}, bf16[96,384]{1,0:T(8,128)(2,1)S(1)}, u32[]{:S(2)}, u32[]{:S(2)}) collective-permute-start(bf16[96,384]{1,0:T(8,128)(2,1)S(1)} %get-tuple-element.34), channel_id=1, source_target_pairs={{0,1},{1,2},{2,3},{3,4},{4,5},{5,6},{6,7},{7,8},{8,9},{9,10},{10,1... | collective-permute-start | bytes 221192 | tf_op jit(solution)/shard_map/ppermute | solution.py:378
  65.1 18.1 %all-to-all-start.1 = ((bf16[16,9,128]{2,1,0:T(8,128)(2,1)}), bf16[16,9,128]{2,1,0:T(8,128)(2,1)S(1)}, u32[]{:S(2)}, u32[]{:S(2)}) async-start(bf16[16,9,128]{2,1,0:T(8,128)(2,1)} %reshape.26), calls=%async_computation.1 | async-start | bytes 131072 | tf_op jit(solution)/shard_map/all_to_all | solution.py:316
  71.6 36.3 %copy-start.4 = (bf16[2,8,16,384]{3,2,1,0:T(8,128)(2,1)S(1)}, bf16[2,8,16,384]{3,2,1,0:T(8,128)(2,1)}, u32[]{:S(2)}) copy-start(bf16[2,8,16,384]{3,2,1,0:T(8,128)(2,1)} %refs_0_.5) | copy-start | bytes 589828
  71.6 36.3 %copy-start.9 = (bf16[128,256]{1,0:T(8,128)(2,1)S(1)}, bf16[128,256]{1,0:T(8,128)(2,1)}, u32[]{:S(2)}) copy-start(bf16[128,256]{1,0:T(8,128)(2,1)} %constant.32.clone.refs_1_) | copy-start | bytes 196612
  83.9 15.1 %all-to-all-start.2 = ((bf16[16,9,128]{2,1,0:T(8,128)(2,1)}), bf16[16,9,128]{2,1,0:T(8,128)(2,1)S(1)}, u32[]{:S(2)}, u32[]{:S(2)}) async-start(bf16[16,9,128]{2,1,0:T(8,128)(2,1)} %broadcast_in_dim.6), calls=%async_computation.2 | async-start | bytes 131072 | tf_op jit(solution)/shard_map/all_to_all | solution.py:316
  87.4 20.6 %collective-permute-start.5 = (bf16[128,384]{1,0:T(8,128)(2,1)S(1)}, bf16[128,384]{1,0:T(8,128)(2,1)S(1)}, u32[]{:S(2)}, u32[]{:S(2)}) collective-permute-start(bf16[128,384]{1,0:T(8,128)(2,1)S(1)} %join_kernel.1), channel_id=1, source_target_pairs={{0,32},{32,64},{64,96},{96,128},{128,160},{160,192},{192,224},{224... | collective-permute-start | bytes 294920 | tf_op jit(solution)/shard_map/ppermute | solution.py:386
  99.9 20.2 %all-to-all-start.3 = ((bf16[16,144,128]{2,1,0:T(8,128)(2,1)}), bf16[16,144,128]{2,1,0:T(8,128)(2,1)S(1)}, u32[]{:S(2)}, u32[]{:S(2)}) async-start(bf16[16,144,128]{2,1,0:T(8,128)(2,1)} %broadcast_in_dim.15), calls=%async_computation.3 | async-start | bytes 1179648 | tf_op jit(solution)/shard_map/all_to_all | solution.py:316
  108.0 16.7 %copy-start.1 = (bf16[384,1152]{1,0:T(8,128)(2,1)S(1)}, bf16[384,1152]{1,0:T(8,128)(2,1)}, u32[]{:S(2)}) copy-start(bf16[384,1152]{1,0:T(8,128)(2,1)} %refs_1_.5) | copy-start | bytes 2654212
  120.1 4.6 %collective-permute-start.6 = (bf16[2304,128]{1,0:T(8,128)(2,1)S(1)}, bf16[2304,128]{1,0:T(8,128)(2,1)S(1)}, u32[]{:S(2)}, u32[]{:S(2)}) collective-permute-start(bf16[2304,128]{1,0:T(8,128)(2,1)S(1)} %bitcast.9), channel_id=1, source_target_pairs={{0,32},{32,0},{1,33},{33,1},{2,34},{34,2},{3,35},{35,3},{4,36},{36... | collective-permute-start | bytes 1769480 | tf_op jit(solution)/shard_map/ppermute | solution.py:329

commit v6 on v5

--- a/solution.py
+++ b/solution.py
@@ -40,13 +40,14 @@
         return self.spot
 
 
-def call(kernel, outs, *args, scalars=(), far=(), scratch=(), limit=40, flops=0):
+def call(kernel, outs, *args, scalars=(), far=(), scratch=(), limit=40, flops=0, spaces=None, after=()):
+    n_after = len(after)
     n_scalars, n_far, n_args, n_outs = len(scalars), len(far), len(args), len(outs)
 
     def body(*refs):
         head, rest = refs[:n_scalars], refs[n_scalars:]
         sources, rest = rest[:n_far], rest[n_far:]
-        near, rest = rest[:n_args], rest[n_args:]
+        near, rest = rest[:n_args], rest[n_args + n_after :]
         results, rest = rest[:n_outs], rest[n_outs:]
         if not n_far:
             return kernel(*head, *near, *results, *rest)
@@ -59,6 +60,7 @@
     specs = [pl.BlockSpec(memory_space=pltpu.SMEM)] * n_scalars
     specs += [pl.BlockSpec(memory_space=pltpu.HBM)] * n_far
     specs += [pl.BlockSpec(memory_space=pltpu.VMEM)] * n_args
+    specs += [pl.BlockSpec(memory_space=pl.ANY)] * n_after
     spots = [pltpu.VMEM(a.shape, a.dtype) for a in far]
     if far:
         spots.append(pltpu.SemaphoreType.DMA((n_far,)))
@@ -66,12 +68,12 @@
         body,
         out_shape=[jax.ShapeDtypeStruct(s, d) for s, d in outs],
         in_specs=specs,
-        out_specs=[pl.BlockSpec(memory_space=pltpu.VMEM)] * n_outs,
+        out_specs=[pl.BlockSpec(memory_space=space) for space in spaces or [pltpu.VMEM] * n_outs],
         scratch_shapes=spots + list(scratch),
         compiler_params=pltpu.CompilerParams(vmem_limit_bytes=limit * 1024 * 1024),
         name=kernel.__name__,
         cost_estimate=pl.CostEstimate(flops=flops, bytes_accessed=0, transcendentals=0) if flops else None,
-    )(*scalars, *far, *args)
+    )(*scalars, *far, *args, *after)
 
 
 PICK = (slice(0, 128), slice(128, 224), slice(256, 288), slice(384, 416))
@@ -136,16 +138,28 @@
         lon_out[64 + i * 32 : 64 + (i + 1) * 32] = upper[0:32]
 
 
-def stage_kernel(*refs):
-    half = len(refs) // 2
-    for fetch, out in zip(refs[:half], refs[half:]):
-        out[...] = fetch.get()[...]
+def pause_kernel(place, out):
+    out[0] = place[0]
+
+
+def normalized(x):
+    centered = x - jnp.mean(x, -1, keepdims=True)
+    rstd = lax.rsqrt(jnp.mean(centered * centered, -1, keepdims=True) + 1e-5)
+    return centered * rstd, rstd
+
+
+def half_sums(left, right, out, half, count):
+    dim = left.shape[1]
+    for at in range(6):
+        j = half * 6 + at
+        term = dot(left[j // 9, :, 0:count], right[j, 0:count])
+        out[at * dim : (at + 1) * dim] = term.astype(BF16)
 
 
 def window_kernel(
     place, ocean_mask, tok, const, w_qkv, cot, w_out, lat, diag, lon, gain,
-    grads, own_back, lat_back, side_back, edge_back,
-    left, right, packed, d_att,
+    other, left, right, windows,
+    packed, d_att,
 ):
     dim = lat.shape[1]
     lat_index = place[0]
@@ -160,16 +174,13 @@
 
     def project(x, g, first):
         rows = slice(first, first + x.shape[0])
-        centered = x - jnp.mean(x, -1, keepdims=True)
-        rstd = lax.rsqrt(jnp.mean(centered * centered, -1, keepdims=True) + 1e-5)
-        xhat = centered * rstd
-        normed = xhat * gains
+        windows[rows] = x.astype(BF16)
+        normed = normalized(x)[0] * gains
         left[0, :, rows] = normed.T.astype(BF16)
         packed[rows] = dot(normed.astype(BF16), w_qkv[...]).astype(BF16)
         d_att[rows] = dot_nt(g, w_out[...]).astype(BF16)
         for j in range(dim // LANES):
             right[9 + j, rows] = g[:, j * LANES : (j + 1) * LANES]
-        return xhat, rstd
 
     def attend(first, differ):
         rows = slice(first, first + WIN)
@@ -200,8 +211,51 @@
             right[3 + group, rows] = dot(d_scores, query_heads).astype(BF16)
             right[6 + group, rows] = dot(weights, d_out_heads).astype(BF16)
 
-    def branch(first, xhat, rstd):
-        rows = slice(first, first + xhat.shape[0])
+    def assembled(i, ref):
+        return (
+            dot(const[0:256, PICK[0]], ref[:, 4:8].reshape(WIN, dim))
+            + dot(const[0:256, PICK[1]], lat[i * 96 : (i + 1) * 96])
+            + dot(const[0:256, PICK[2]], diag[i * 32 : (i + 1) * 32])
+            + dot(const[0:256, PICK[3]], lon[i * 32 : (i + 1) * 32])
+        )
+
+    def ocean(band, rows, size):
+        first = lax.broadcasted_iota(jnp.int32, (rows, 1), 0) < size
+        return jnp.where(first, ocean_mask[0, band], ocean_mask[1, band]).astype(F32)
+
+    g = (assembled(1, cot) * ocean(lat_index, 2 * WIN, WIN)).astype(BF16)
+    project(assembled(0, tok), g, 0)
+    lower_differs = ((key_at // 8 % 8 >= 4) != (query_at // 8 % 8 >= 4)).astype(jnp.int32)
+    for w in range(2):
+        attend(w * WIN, lower_differs * last_band > 0)
+
+    @pl.when(lat_index == 0)
+    def _():
+        def edge(i, ref):
+            return dot(const[256:384, EDGE_PICK[0]], ref[:, 0:4].reshape(WIN, dim)) + dot(
+                const[256:384, EDGE_PICK[1]], lon[64 + i * 32 : 64 + (i + 1) * 32]
+            )
+
+        last = ocean_mask.shape[1] - 1
+        edge_g = (edge(1, cot) * ocean(last, WIN, 64)).astype(BF16)
+        project(edge(0, tok), edge_g, 2 * WIN)
+        attend(2 * WIN, key_at // 64 != query_at // 64)
+        half_sums(left, right, other, 1 - core, 3 * WIN)
+
+    @pl.when(lat_index != 0)
+    def _():
+        half_sums(left, right, other, 1 - core, 2 * WIN)
+
+
+def branch_kernel(place, left, right, windows, const, w_qkv, gain, mine, own_back, lat_back, side_back, edge_back):
+    dim = windows.shape[1]
+    lat_index = place[0]
+    core = lax.rem(lat_index, 2)
+    gains = gain[...].reshape(1, dim).astype(F32)
+
+    def branch(first, count):
+        rows = slice(first, first + count)
+        xhat, rstd = normalized(windows[rows].astype(F32))
         d_packed = jnp.concatenate([right[j, rows] for j in range(9)], 1)
         d_normed = dot_nt(d_packed, w_qkv[...])
         d_hat = d_normed * gains
@@ -212,56 +266,25 @@
         )
         return d_branch.astype(BF16)
 
-    def emit(count):
-        for j in range(12):
-            half, at = j // 6, j % 6
-            slot = lax.rem(half + core, 2)
-            term = dot(left[j // 9, :, 0:count], right[j, 0:count])
-            grads[slot, at * dim : (at + 1) * dim] = term.astype(BF16)
-
-    def assembled(i, ref):
-        return (
-            dot(const[0:256, PICK[0]], ref[:, 4:8].reshape(WIN, dim))
-            + dot(const[0:256, PICK[1]], lat[i * 96 : (i + 1) * 96])
-            + dot(const[0:256, PICK[2]], diag[i * 32 : (i + 1) * 32])
-            + dot(const[0:256, PICK[3]], lon[i * 32 : (i + 1) * 32])
-        )
-
-    def ocean(band, rows, size):
-        first = lax.broadcasted_iota(jnp.int32, (rows, 1), 0) < size
-        return jnp.where(first, ocean_mask[0, band], ocean_mask[1, band]).astype(F32)
-
-    g = (assembled(1, cot) * ocean(lat_index, 2 * WIN, WIN)).astype(BF16)
-    xhat, rstd = project(assembled(0, tok), g, 0)
-    lower_differs = ((key_at // 8 % 8 >= 4) != (query_at // 8 % 8 >= 4)).astype(jnp.int32)
-    for w in range(2):
-        attend(w * WIN, lower_differs * last_band > 0)
-
     @pl.when(lat_index == 0)
     def _():
-        def edge(i, ref):
-            return dot(const[256:384, EDGE_PICK[0]], ref[:, 0:4].reshape(WIN, dim)) + dot(
-                const[256:384, EDGE_PICK[1]], lon[64 + i * 32 : 64 + (i + 1) * 32]
-            )
-
-        last = ocean_mask.shape[1] - 1
-        edge_g = (edge(1, cot) * ocean(last, WIN, 64)).astype(BF16)
-        edge_xhat, edge_rstd = project(edge(0, tok), edge_g, 2 * WIN)
-        attend(2 * WIN, key_at // 64 != query_at // 64)
-        edge_branch = branch(2 * WIN, edge_xhat, edge_rstd)
-        edge_back[...] = dot(const[EDGE_PUT : EDGE_PUT + 160, 256:384], edge_branch).astype(BF16)
-        emit(3 * WIN)
+        half_sums(left, right, mine, core, 3 * WIN)
+        edge_back[...] = dot(const[EDGE_PUT : EDGE_PUT + 160, 256:384], branch(2 * WIN, WIN)).astype(BF16)
 
     @pl.when(lat_index != 0)
     def _():
+        half_sums(left, right, mine, core, 2 * WIN)
         edge_back[...] = jnp.zeros_like(edge_back)
-        emit(2 * WIN)
-
-    back = dot(const[PUT : PUT + 288, 0:256], branch(0, xhat, rstd)).astype(BF16)
+
+    back = dot(const[PUT : PUT + 288, 0:256], branch(0, 2 * WIN)).astype(BF16)
     own_back[...] = back[0:128]
     lat_back[...] = back[128:224]
     side_back[0:64] = back[224:288]
     side_back[64:96] = edge_back[128:160]
+
+
+def add_kernel(mine, received, out):
+    out[...] = (mine[...].astype(F32) + received[...].astype(F32)).astype(BF16)
 
 
 def join_kernel(lat_back, side, out):
@@ -360,23 +383,24 @@
     diag = lax.ppermute(diag, LAT + LON, back(diagonal))
     lon = lax.ppermute(lon, LON, back(east))
     near = (tokens, constant(constants()), w_qkv, cotangent, w_out)
-    near = call(stage_kernel, [(a.shape, BF16) for a in near], far=near)
+    (pause,) = call(pause_kernel, [((1,), jnp.int32)], scalars=(place,), limit=8, flops=LONG, spaces=[pltpu.SMEM])
     half = 6 * dim
-    shapes = [(2, half, LANES), (WIN, dim), (96, dim), (96, dim), (160, dim)]
-    grads, own_back, lat_back, side_back, edge_back = call(
+    shapes = [(half, LANES), (2, dim, 3 * WIN), (12, 3 * WIN, LANES), (3 * WIN, dim)]
+    other, left, right, windows = call(
         window_kernel, [(shape, BF16) for shape in shapes],
         *near, lat, diag, lon, gain,
-        scalars=(place, ocean_mask.T),
-        scratch=[
-            pltpu.VMEM((2, dim, 3 * WIN), BF16),
-            pltpu.VMEM((12, 3 * WIN, LANES), BF16),
-            pltpu.VMEM((3 * WIN, 3 * dim), BF16),
-            pltpu.VMEM((3 * WIN, dim), BF16),
-        ],
+        scalars=(place, ocean_mask.T), after=(pause,),
+        scratch=[pltpu.VMEM((3 * WIN, 3 * dim), BF16), pltpu.VMEM((3 * WIN, dim), BF16)],
+    )
+    shapes = [(half, LANES), (WIN, dim), (96, dim), (96, dim), (160, dim)]
+    mine, own_back, lat_back, side_back, edge_back = call(
+        branch_kernel, [(shape, BF16) for shape in shapes],
+        left, right, windows, near[1], w_qkv, gain,
+        scalars=(place,), flops=LONG,
     )
 
     side = lax.ppermute(side_back, LON, east)
-    mine = (grads[0].astype(F32) + swapped(grads[1]).astype(F32)).astype(BF16)
+    (mine,) = call(add_kernel, [((half, LANES), BF16)], mine, swapped(other))
     mine = summed(exchange(mine.reshape(16, half // 16, LANES), PLANE))
     mine = summed(exchange(mine.reshape(16, half // 256, LANES), RING))
     (rows_back,) = call(

time: 127 us -> 125 us (0.984)
  local copies, waits for them, and re-layouts: 7.32 us -> 2.27 us
  waiting for transfers between devices: 41.3 us -> 42.8 us
  Pallas kernels: 11.9 us -> 13.2 us
    ppermute x1, starting transfers between devices: 1.92 us -> 16.7 us  [local(): diag = lax.ppermute(diag, LAT + LON, back(diagonal))]
    ppermute x1, starting transfers between devices: 9.95 us -> 2.37 us  [local(): lon = lax.ppermute(lon, LON, back(east))]
    ppermute x1, starting transfers between devices: 8.79 us -> 1.92 us  [local(): lat = lax.ppermute(lat, LAT, back(south))]
    unnamed x20 -> x16, local copies, waits for them, and re-layouts: 5.06 us -> 0.05 us
    ppermute x1, waiting for transfers between devices: 2.41 us -> 0.01 us  [local(): diag = lax.ppermute(diag, LAT + LON, back(diagonal))]
    all_to_all x4, starting transfers between devices: 28.4 us -> 30.7 us  [exchange(): return lax.all_to_all(parts, axis, 0, 0, tiled=False)]
    ppermute x1, waiting for transfers between devices: 0.01 us -> 2.17 us  [local(): lat = lax.ppermute(lat, LAT, back(south))]
    ppermute x1, waiting for transfers between devices: 0.01 us -> 1.94 us  [local(): lon = lax.ppermute(lon, LON, back(east))]
  transfers between devices with their start and end apart: 11 -> 11, of which waited for: 7 -> 8; matrix products, arithmetic and copies ran while one was open for 1% -> 1% of each run, Pallas kernels for 2% -> 2%
where the time goes in v6:
time: 125 us; the launch traced here: 124 us
  starting transfers between devices  65 us (52%)
  waiting for transfers between devices  42.8 us (34%)
  Pallas kernels  13.2 us (11%)
  local copies, waits for them, and re-layouts  2.27 us (2%)
    all_to_all x4, waiting for transfers between devices, exchange(): return lax.all_to_all(parts, axis, 0, 0, tiled=False)  36.6 us
    all_to_all x4, starting transfers between devices, exchange(): return lax.all_to_all(parts, axis, 0, 0, tiled=False)  30.7 us
    ppermute x1, starting transfers between devices, local(): diag = lax.ppermute(diag, LAT + LON, back(diagonal))  16.7 us
    pallas_call x8, Pallas kernels, call(): pl.pallas_call(body, out_shape=[jax.ShapeDtypeStruct(s, d) for s, d in ou...  13.2 us
    ppermute x1, starting transfers between devices, local(): rows_back = lax.ppermute(rows_back, LAT, south)  5.03 us
    ppermute x2, starting transfers between devices, swapped(): return lax.ppermute(array, 'core', [(0, 1), (1, 0)])  4.99 us
    ppermute x1, starting transfers between devices, local(): side = lax.ppermute(side_back, LON, east)  3.26 us
  transfers between devices with their start and end apart: 11, of which 8 were waited for; matrix products, arithmetic and copies ran while one was open for 1% of the time, Pallas kernels for 2%

profile of v6, /device:TPU:1, one launch (start us, length us, event | category | flops | bytes accessed | tf_op | source)
XLA Modules:
  0.0 124.3 jit_solution(8285391152112459548)
XLA Ops:
  0.6 2.0 %send_kernel.1 = (bf16[192,384]{1,0:T(8,128)(2,1)}, bf16[64,384]{1,0:T(8,128)(2,1)}, bf16[128,384]{1,0:T(8,128)(2,1)}) custom-call(bf16[2,8,16,384]{3,2,1,0:T(8,128)(2,1)} %refs_2_.2, bf16[2,8,16,384]{3,2,1,0:T(8,128)(2,1)} %refs_0_.3, bf16[128,128]{1,0:T(8,128)(2,1)} %constant.30.clone.refs_2_), custom_call_target="tpu_custom_call" | custom-call | tf_op jit(solution)/shard_map/send_kernel/pallas_call | solution.py:67
  2.6 16.7 %collective-permute-start.1 = (bf16[64,384]{1,0:T(8,128)(2,1)}, bf16[64,384]{1,0:T(8,128)(2,1)S(1)}, u32[]{:S(2)}, u32[]{:S(2)}) collective-permute-start(bf16[64,384]{1,0:T(8,128)(2,1)} %get-tuple-element.24), channel_id=1, source_target_pairs={{33,0},{34,1},{35,2},{36,3},{37,4},{38,5},{39,6},{40,7},{41,8},{42... | collective-permute-start | bytes 147464 | tf_op jit(solution)/shard_map/ppermute | solution.py:383
  19.3 2.4 %collective-permute-start.2 = (bf16[128,384]{1,0:T(8,128)(2,1)}, bf16[128,384]{1,0:T(8,128)(2,1)S(1)}, u32[]{:S(2)}, u32[]{:S(2)}) collective-permute-start(bf16[128,384]{1,0:T(8,128)(2,1)} %get-tuple-element.25), channel_id=1, source_target_pairs={{1,0},{2,1},{3,2},{4,3},{5,4},{6,5},{7,6},{8,7},{9,8},{10,9},{11,1... | collective-permute-start | bytes 294920 | tf_op jit(solution)/shard_map/ppermute | solution.py:384
  21.7 1.9 %collective-permute-start = (bf16[192,384]{1,0:T(8,128)(2,1)}, bf16[192,384]{1,0:T(8,128)(2,1)S(1)}, u32[]{:S(2)}, u32[]{:S(2)}) collective-permute-start(bf16[192,384]{1,0:T(8,128)(2,1)} %get-tuple-element.23), channel_id=1, source_target_pairs={{32,0},{64,32},{96,64},{128,96},{160,128},{192,160},{224,192},{256... | collective-permute-start | bytes 442376 | tf_op jit(solution)/shard_map/ppermute | solution.py:382
  23.7 0.0 copy-start.3
  23.7 0.5 pause_kernel.1.refs_11_
  24.3 1.9 %collective-permute-done.2.refs_9_ = bf16[128,384]{1,0:T(8,128)(2,1)S(1)} collective-permute-done((bf16[128,384]{1,0:T(8,128)(2,1)}, bf16[128,384]{1,0:T(8,128)(2,1)S(1)}, u32[]{:S(2)}, u32[]{:S(2)}) %collective-permute-start.2) | collective-permute-done | bytes 98336 | tf_op jit(solution)/shard_map/ppermute | solution.py:384
  26.2 2.2 %collective-permute-done.refs_7_ = bf16[192,384]{1,0:T(8,128)(2,1)S(1)} collective-permute-done((bf16[192,384]{1,0:T(8,128)(2,1)}, bf16[192,384]{1,0:T(8,128)(2,1)S(1)}, u32[]{:S(2)}, u32[]{:S(2)}) %collective-permute-start) | collective-permute-done | bytes 147488 | tf_op jit(solution)/shard_map/ppermute | solution.py:382
  28.4 5.6 %window_kernel.1 = (bf16[2304,128]{1,0:T(8,128)(2,1)S(1)}, bf16[2,384,384]{2,1,0:T(8,128)(2,1)S(1)}, bf16[12,384,128]{2,1,0:T(8,128)(2,1)S(1)}, bf16[384,384]{1,0:T(8,128)(2,1)S(1)}) custom-call(s32[1]{0:T(128)} %bitcast.refs_0_, s32[2,16]{1,0:T(2,128)S(1)} %bitcast.6, bf16[2,8,16,384]{3,2,1,0:T(8,128)(2,1)S(1)} %copy-done.1, ...), custom_call_target="tpu_custom_call" | custom-call | tf_op jit(solution)/shard_map/window_kernel/pallas_call | solution.py:67
  34.0 2.1 %collective-permute-start.3 = (bf16[2304,128]{1,0:T(8,128)(2,1)S(1)}, bf16[2304,128]{1,0:T(8,128)(2,1)S(1)}, u32[]{:S(2)}, u32[]{:S(2)}) collective-permute-start(bf16[2304,128]{1,0:T(8,128)(2,1)S(1)} %get-tuple-element.30), channel_id=1, source_target_pairs={{0,32},{32,0},{1,33},{33,1},{2,34},{34,2},{3,35},{35,3},{4,36},{36... | collective-permute-start | bytes 1769480 | tf_op jit(solution)/shard_map/ppermute | solution.py:352
  36.1 1.3 %branch_kernel.1 = (bf16[2304,128]{1,0:T(8,128)(2,1)S(1)}, bf16[128,384]{1,0:T(8,128)(2,1)S(1)}, bf16[96,384]{1,0:T(8,128)(2,1)S(1)}, bf16[96,384]{1,0:T(8,128)(2,1)S(1)}, bf16[160,384]{1,0:T(8,128)(2,1)S(1)}) custom-call(s32[1]{0:T(128)} %bitcast.refs_0_, bf16[2,384,384]{2,1,0:T(8,128)(2,1)S(1)} %get-tuple-element.26.refs_1_, ...), custom_call_target="tpu_custom_call" | custom-call | flops 30000001024 | tf_op jit(solution)/shard_map/branch_kernel/pallas_call | solution.py:67
  37.4 0.5 collective-permute-done.3.refs_1_
  37.9 1.0 add_kernel.1
  38.9 15.4 %all-to-all-start = ((bf16[16,144,128]{2,1,0:T(8,128)(2,1)}), bf16[16,144,128]{2,1,0:T(8,128)(2,1)S(1)}, u32[]{:S(2)}, u32[]{:S(2)}) async-start(bf16[16,144,128]{2,1,0:T(8,128)(2,1)} %bitcast.2), calls=%async_computation | async-start | bytes 1179648 | tf_op jit(solution)/shard_map/all_to_all | solution.py:339
  54.3 3.3 %collective-permute-start.4 = (bf16[96,384]{1,0:T(8,128)(2,1)S(1)}, bf16[96,384]{1,0:T(8,128)(2,1)S(1)}, u32[]{:S(2)}, u32[]{:S(2)}) collective-permute-start(bf16[96,384]{1,0:T(8,128)(2,1)S(1)} %get-tuple-element.32), channel_id=1, source_target_pairs={{0,1},{1,2},{2,3},{3,4},{4,5},{5,6},{6,7},{7,8},{8,9},{9,10},{10,1... | collective-permute-start | bytes 221192 | tf_op jit(solution)/shard_map/ppermute | solution.py:402
  57.6 7.5 %all-to-all-done = bf16[16,144,128]{2,1,0:T(8,128)(2,1)S(1)} async-done(((bf16[16,144,128]{2,1,0:T(8,128)(2,1)}), bf16[16,144,128]{2,1,0:T(8,128)(2,1)S(1)}, u32[]{:S(2)}, u32[]{:S(2)}) %all-to-all-start) | async-done | bytes 589856 | tf_op jit(solution)/shard_map/all_to_all | solution.py:339
  65.0 0.1 reduce_sum.24
  65.1 0.7 reshape.24
  65.8 3.5 %all-to-all-start.1 = ((bf16[16,9,128]{2,1,0:T(8,128)(2,1)}), bf16[16,9,128]{2,1,0:T(8,128)(2,1)S(1)}, u32[]{:S(2)}, u32[]{:S(2)}) async-start(bf16[16,9,128]{2,1,0:T(8,128)(2,1)} %reshape.24), calls=%async_computation.1 | async-start | bytes 131072 | tf_op jit(solution)/shard_map/all_to_all | solution.py:339
  69.3 0.0 copy-start.7
  69.3 11.6 %all-to-all-done.1 = bf16[16,9,128]{2,1,0:T(8,128)(2,1)S(1)} async-done(((bf16[16,9,128]{2,1,0:T(8,128)(2,1)}), bf16[16,9,128]{2,1,0:T(8,128)(2,1)S(1)}, u32[]{:S(2)}, u32[]{:S(2)}) %all-to-all-start.1) | async-done | bytes 36896 | tf_op jit(solution)/shard_map/all_to_all | solution.py:339
  81.0 0.6 broadcast_in_dim.6
  81.6 3.5 %all-to-all-start.2 = ((bf16[16,9,128]{2,1,0:T(8,128)(2,1)}), bf16[16,9,128]{2,1,0:T(8,128)(2,1)S(1)}, u32[]{:S(2)}, u32[]{:S(2)}) async-start(bf16[16,9,128]{2,1,0:T(8,128)(2,1)} %broadcast_in_dim.6), calls=%async_computation.2 | async-start | bytes 131072 | tf_op jit(solution)/shard_map/all_to_all | solution.py:339
  85.1 5.0 %collective-permute-start.5 = (bf16[128,384]{1,0:T(8,128)(2,1)S(1)}, bf16[128,384]{1,0:T(8,128)(2,1)S(1)}, u32[]{:S(2)}, u32[]{:S(2)}) collective-permute-start(bf16[128,384]{1,0:T(8,128)(2,1)S(1)} %join_kernel.1), channel_id=1, source_target_pairs={{0,32},{32,64},{64,96},{96,128},{128,160},{160,192},{192,224},{224... | collective-permute-start | bytes 294920 | tf_op jit(solution)/shard_map/ppermute | solution.py:410
  90.2 6.6 %all-to-all-done.2 = bf16[16,9,128]{2,1,0:T(8,128)(2,1)S(1)} async-done(((bf16[16,9,128]{2,1,0:T(8,128)(2,1)}), bf16[16,9,128]{2,1,0:T(8,128)(2,1)S(1)}, u32[]{:S(2)}, u32[]{:S(2)}) %all-to-all-start.2) | async-done | bytes 36896 | tf_op jit(solution)/shard_map/all_to_all | solution.py:339
  96.8 0.9 broadcast_in_dim.15
  97.7 8.3 %all-to-all-start.3 = ((bf16[16,144,128]{2,1,0:T(8,128)(2,1)}), bf16[16,144,128]{2,1,0:T(8,128)(2,1)S(1)}, u32[]{:S(2)}, u32[]{:S(2)}) async-start(bf16[16,144,128]{2,1,0:T(8,128)(2,1)} %broadcast_in_dim.15), calls=%async_computation.3 | async-start | bytes 1179648 | tf_op jit(solution)/shard_map/all_to_all | solution.py:339
  106.0 1.3 %token_kernel.1 = bf16[2,8,16,384]{3,2,1,0:T(8,128)(2,1)} custom-call(bf16[2,8,16,384]{3,2,1,0:T(8,128)(2,1)S(1)} %copy-done.2, bf16[128,256]{1,0:T(8,128)(2,1)S(1)} %copy-done.7, bf16[128,384]{1,0:T(8,128)(2,1)S(1)} %get-tuple-element.34.refs_2_, bf16[160,384]{1,0:T(8,128)(2,1)S(1)} %get-tuple-element.35.refs_3_, ...), custom_call_target="tpu_custom_call" | custom-call | flops 30000001024 | tf_op jit(solution)/shard_map/token_kernel/pallas_call | solution.py:67
  107.2 10.9 %all-to-all-done.3 = bf16[16,144,128]{2,1,0:T(8,128)(2,1)S(1)} async-done(((bf16[16,144,128]{2,1,0:T(8,128)(2,1)}), bf16[16,144,128]{2,1,0:T(8,128)(2,1)S(1)}, u32[]{:S(2)}, u32[]{:S(2)}) %all-to-all-start.3) | async-done | bytes 589856 | tf_op jit(solution)/shard_map/all_to_all | solution.py:339
  118.2 2.9 %collective-permute-start.6 = (bf16[2304,128]{1,0:T(8,128)(2,1)S(1)}, bf16[2304,128]{1,0:T(8,128)(2,1)S(1)}, u32[]{:S(2)}, u32[]{:S(2)}) collective-permute-start(bf16[2304,128]{1,0:T(8,128)(2,1)S(1)} %bitcast.4), channel_id=1, source_target_pairs={{0,32},{32,0},{1,33},{33,1},{2,34},{34,2},{3,35},{35,3},{4,36},{36... | collective-permute-start | bytes 1769480 | tf_op jit(solution)/shard_map/ppermute | solution.py:352
  121.1 1.6 %collective-permute-done.6.refs_3_ = bf16[2304,128]{1,0:T(8,128)(2,1)S(1)} collective-permute-done((bf16[2304,128]{1,0:T(8,128)(2,1)S(1)}, bf16[2304,128]{1,0:T(8,128)(2,1)S(1)}, u32[]{:S(2)}, u32[]{:S(2)}) %collective-permute-start.6) | collective-permute-done | bytes 589856 | tf_op jit(solution)/shard_map/ppermute | solution.py:352
  122.7 1.6 %result_kernel.1 = (bf16[384,1152]{1,0:T(8,128)(2,1)}, bf16[384,384]{1,0:T(8,128)(2,1)}, bf16[384]{0:T(512)(128)(2,1)}) custom-call(s32[1]{0:T(128)} %bitcast.refs_0_, bf16[384,1152]{1,0:T(8,128)(2,1)S(1)} %copy-done, bf16[2304,128]{1,0:T(8,128)(2,1)S(1)} %bitcast.5, bf16[2304,128]{1,0:T(8,128)(2,1)S(1)} %collective-permute-done.6.refs_3_, ...), custom_call_target="tpu_custom_call" | custom-call | tf_op jit(solution)/shard_map/result_kernel/pallas_call | solution.py:67
  (20 shorter events, 0.1 us)
Async XLA Ops:
  2.6 21.7 %collective-permute-start.1 = (bf16[64,384]{1,0:T(8,128)(2,1)}, bf16[64,384]{1,0:T(8,128)(2,1)S(1)}, u32[]{:S(2)}, u32[]{:S(2)}) collective-permute-start(bf16[64,384]{1,0:T(8,128)(2,1)} %get-tuple-element.24), channel_id=1, source_target_pairs={{33,0},{34,1},{35,2},{36,3},{37,4},{38,5},{39,6},{40,7},{41,8},{42... | collective-permute-start | bytes 147464 | tf_op jit(solution)/shard_map/ppermute | solution.py:383
  19.3 6.9 %collective-permute-start.2 = (bf16[128,384]{1,0:T(8,128)(2,1)}, bf16[128,384]{1,0:T(8,128)(2,1)S(1)}, u32[]{:S(2)}, u32[]{:S(2)}) collective-permute-start(bf16[128,384]{1,0:T(8,128)(2,1)} %get-tuple-element.25), channel_id=1, source_target_pairs={{1,0},{2,1},{3,2},{4,3},{5,4},{6,5},{7,6},{8,7},{9,8},{10,9},{11,1... | collective-permute-start | bytes 294920 | tf_op jit(solution)/shard_map/ppermute | solution.py:384
  21.7 6.7 %collective-permute-start = (bf16[192,384]{1,0:T(8,128)(2,1)}, bf16[192,384]{1,0:T(8,128)(2,1)S(1)}, u32[]{:S(2)}, u32[]{:S(2)}) collective-permute-start(bf16[192,384]{1,0:T(8,128)(2,1)} %get-tuple-element.23), channel_id=1, source_target_pairs={{32,0},{64,32},{96,64},{128,96},{160,128},{192,160},{224,192},{256... | collective-permute-start | bytes 442376 | tf_op jit(solution)/shard_map/ppermute | solution.py:382
  23.6 4.7 %copy-start = (bf16[384,1152]{1,0:T(8,128)(2,1)S(1)}, bf16[384,1152]{1,0:T(8,128)(2,1)}, u32[]{:S(2)}) copy-start(bf16[384,1152]{1,0:T(8,128)(2,1)} %refs_1_.4) | copy-start | bytes 2654212
  23.6 4.7 %copy-start.1 = (bf16[2,8,16,384]{3,2,1,0:T(8,128)(2,1)S(1)}, bf16[2,8,16,384]{3,2,1,0:T(8,128)(2,1)}, u32[]{:S(2)}) copy-start(bf16[2,8,16,384]{3,2,1,0:T(8,128)(2,1)} %refs_2_.2) | copy-start | bytes 589828
  23.7 4.7 %copy-start.2 = (bf16[2,8,16,384]{3,2,1,0:T(8,128)(2,1)S(1)}, bf16[2,8,16,384]{3,2,1,0:T(8,128)(2,1)}, u32[]{:S(2)}) copy-start(bf16[2,8,16,384]{3,2,1,0:T(8,128)(2,1)} %refs_0_.3) | copy-start | bytes 589828
  23.7 4.7 %copy-start.3 = (bf16[544,512]{1,0:T(8,128)(2,1)S(1)}, bf16[544,512]{1,0:T(8,128)(2,1)}, u32[]{:S(2)}) copy-start(bf16[544,512]{1,0:T(8,128)(2,1)} %constant.31.clone.refs_3_.refs_4_) | copy-start | bytes 1671172
  23.7 4.7 %copy-start.4 = (bf16[384,384]{1,0:T(8,128)(2,1)S(1)}, bf16[384,384]{1,0:T(8,128)(2,1)}, u32[]{:S(2)}) copy-start(bf16[384,384]{1,0:T(8,128)(2,1)} %refs_6_.2) | copy-start | bytes 884740
  23.7 4.7 %copy-start.5 = (bf16[384]{0:T(512)(128)(2,1)S(1)}, bf16[384]{0:T(512)(128)(2,1)}, u32[]{:S(2)}) copy-start(bf16[384]{0:T(512)(128)(2,1)} %refs_4_.4) | copy-start | bytes 2308
  23.7 4.7 %copy-start.6 = (s32[16,2]{0,1:T(2,128)S(1)}, s32[16,2]{0,1:T(2,128)}, u32[]{:S(2)}) copy-start(s32[16,2]{0,1:T(2,128)} %param.11) | copy-start | bytes 388
  34.0 3.9 %collective-permute-start.3 = (bf16[2304,128]{1,0:T(8,128)(2,1)S(1)}, bf16[2304,128]{1,0:T(8,128)(2,1)S(1)}, u32[]{:S(2)}, u32[]{:S(2)}) collective-permute-start(bf16[2304,128]{1,0:T(8,128)(2,1)S(1)} %get-tuple-element.30), channel_id=1, source_target_pairs={{0,32},{32,0},{1,33},{33,1},{2,34},{34,2},{3,35},{35,3},{4,36},{36... | collective-permute-start | bytes 1769480 | tf_op jit(solution)/shard_map/ppermute | solution.py:352
  38.9 26.2 %all-to-all-start = ((bf16[16,144,128]{2,1,0:T(8,128)(2,1)}), bf16[16,144,128]{2,1,0:T(8,128)(2,1)S(1)}, u32[]{:S(2)}, u32[]{:S(2)}) async-start(bf16[16,144,128]{2,1,0:T(8,128)(2,1)} %bitcast.2), calls=%async_computation | async-start | bytes 1179648 | tf_op jit(solution)/shard_map/all_to_all | solution.py:339
  54.3 15.0 %collective-permute-start.4 = (bf16[96,384]{1,0:T(8,128)(2,1)S(1)}, bf16[96,384]{1,0:T(8,128)(2,1)S(1)}, u32[]{:S(2)}, u32[]{:S(2)}) collective-permute-start(bf16[96,384]{1,0:T(8,128)(2,1)S(1)} %get-tuple-element.32), channel_id=1, source_target_pairs={{0,1},{1,2},{2,3},{3,4},{4,5},{5,6},{6,7},{7,8},{8,9},{9,10},{10,1... | collective-permute-start | bytes 221192 | tf_op jit(solution)/shard_map/ppermute | solution.py:402
  65.8 15.2 %all-to-all-start.1 = ((bf16[16,9,128]{2,1,0:T(8,128)(2,1)}), bf16[16,9,128]{2,1,0:T(8,128)(2,1)S(1)}, u32[]{:S(2)}, u32[]{:S(2)}) async-start(bf16[16,9,128]{2,1,0:T(8,128)(2,1)} %reshape.24), calls=%async_computation.1 | async-start | bytes 131072 | tf_op jit(solution)/shard_map/all_to_all | solution.py:339
  69.3 36.7 %copy-start.7 = (bf16[128,256]{1,0:T(8,128)(2,1)S(1)}, bf16[128,256]{1,0:T(8,128)(2,1)}, u32[]{:S(2)}) copy-start(bf16[128,256]{1,0:T(8,128)(2,1)} %constant.32.clone.refs_1_) | copy-start | bytes 196612
  81.6 15.1 %all-to-all-start.2 = ((bf16[16,9,128]{2,1,0:T(8,128)(2,1)}), bf16[16,9,128]{2,1,0:T(8,128)(2,1)S(1)}, u32[]{:S(2)}, u32[]{:S(2)}) async-start(bf16[16,9,128]{2,1,0:T(8,128)(2,1)} %broadcast_in_dim.6), calls=%async_computation.2 | async-start | bytes 131072 | tf_op jit(solution)/shard_map/all_to_all | solution.py:339
  85.1 20.8 %collective-permute-start.5 = (bf16[128,384]{1,0:T(8,128)(2,1)S(1)}, bf16[128,384]{1,0:T(8,128)(2,1)S(1)}, u32[]{:S(2)}, u32[]{:S(2)}) collective-permute-start(bf16[128,384]{1,0:T(8,128)(2,1)S(1)} %join_kernel.1), channel_id=1, source_target_pairs={{0,32},{32,64},{64,96},{96,128},{128,160},{160,192},{192,224},{224... | collective-permute-start | bytes 294920 | tf_op jit(solution)/shard_map/ppermute | solution.py:410
  97.7 20.5 %all-to-all-start.3 = ((bf16[16,144,128]{2,1,0:T(8,128)(2,1)}), bf16[16,144,128]{2,1,0:T(8,128)(2,1)S(1)}, u32[]{:S(2)}, u32[]{:S(2)}) async-start(bf16[16,144,128]{2,1,0:T(8,128)(2,1)} %broadcast_in_dim.15), calls=%async_computation.3 | async-start | bytes 1179648 | tf_op jit(solution)/shard_map/all_to_all | solution.py:339
  118.2 4.5 %collective-permute-start.6 = (bf16[2304,128]{1,0:T(8,128)(2,1)S(1)}, bf16[2304,128]{1,0:T(8,128)(2,1)S(1)}, u32[]{:S(2)}, u32[]{:S(2)}) collective-permute-start(bf16[2304,128]{1,0:T(8,128)(2,1)S(1)} %bitcast.4), channel_id=1, source_target_pairs={{0,32},{32,0},{1,33},{33,1},{2,34},{34,2},{3,35},{35,3},{4,36},{36... | collective-permute-start | bytes 1769480 | tf_op jit(solution)/shard_map/ppermute | solution.py:352

commit v7 on v6

--- a/solution.py
+++ b/solution.py
@@ -17,7 +17,20 @@
 LAT = ("zhi", "x", "core")
 LON = ("zlo", "y")
 PLANE = ("x", "y")
-RING = ("zhi", "zlo")
+ALL = ("zhi", "x", "core", "zlo", "y")
+
+
+def rings(first):
+    order = [(first + i) % 16 for i in range(16)]
+    return [
+        [(((z // 8 * 4 + x) * 2 + core) * 8 + z % 8) * 4 + y for z in order]
+        for x in range(4)
+        for core in range(2)
+        for y in range(4)
+    ]
+
+
+RINGS = rings(8)
 F32 = jnp.float32
 BF16 = jnp.bfloat16
 LONG = 3 * 10**10
@@ -76,16 +89,16 @@
     )(*scalars, *far, *args, *after)
 
 
-PICK = (slice(0, 128), slice(128, 224), slice(256, 288), slice(384, 416))
+PICK = slice(0, 288)
 PUT = 256
-EDGE_PICK = (slice(256, 384), slice(384, 416))
-EDGE_PUT = 384
+EDGE_PICK = slice(128, 288)
+EDGE_PUT = 544
 
 
 def constants():
-    pick = np.zeros((2 * WIN, 512), np.float32)
+    pick = np.zeros((2 * WIN, 288), np.float32)
     back = np.zeros((288, 2 * WIN), np.float32)
-    edge = np.zeros((WIN, 256), np.float32)
+    edge = np.zeros((WIN, 160), np.float32)
     edge_back = np.zeros((160, WIN), np.float32)
     for w in range(2):
         for level in range(2):
@@ -96,7 +109,7 @@
                     corner = level * 16 + row * 4 + col - 16
                     grid = level * 64 + row * 16 + col
                     if col >= 16:
-                        pick[token, (256 if below else 384) + corner] = 1
+                        pick[token, (224 if below else 256) + corner] = 1
                         back[(224 if below else 256) + corner, token] = 1
                     elif below:
                         inner = level * 48 + row * 12 + col - 4
@@ -109,11 +122,11 @@
                         token = w * 64 + level * 32 + r * 8 + c
                         edge[token, 128 + corner if col >= 16 else grid] = 1
                         edge_back[128 + corner if col >= 16 else grid, token] = 1
-    packed = np.zeros((544, 512), np.float32)
-    packed[0:256] = pick
+    packed = np.zeros((704, 384), np.float32)
+    packed[0:256, 0:288] = pick[:, 0:288]
     packed[256:544, 0:256] = back
-    packed[256:384, 256:512] = edge
-    packed[384:544, 256:384] = edge_back
+    packed[544:704, 0:128] = edge_back
+    packed[544:672, 128:288] = edge
     return packed
 
 
@@ -211,34 +224,42 @@
             right[3 + group, rows] = dot(d_scores, query_heads).astype(BF16)
             right[6 + group, rows] = dot(weights, d_out_heads).astype(BF16)
 
-    def assembled(i, ref):
-        return (
-            dot(const[0:256, PICK[0]], ref[:, 4:8].reshape(WIN, dim))
-            + dot(const[0:256, PICK[1]], lat[i * 96 : (i + 1) * 96])
-            + dot(const[0:256, PICK[2]], diag[i * 32 : (i + 1) * 32])
-            + dot(const[0:256, PICK[3]], lon[i * 32 : (i + 1) * 32])
+    def sources(i, ref):
+        return jnp.concatenate(
+            [
+                ref[:, 4:8].reshape(WIN, dim),
+                lat[i * 96 : (i + 1) * 96],
+                diag[i * 32 : (i + 1) * 32],
+                lon[i * 32 : (i + 1) * 32],
+            ],
+            0,
         )
+
+    def edge_sources(i, ref):
+        return jnp.concatenate(
+            [ref[:, 0:4].reshape(WIN, dim), lon[64 + i * 32 : 64 + (i + 1) * 32]], 0
+        )
+
+    def assembled(matrix, tokens, cotangents):
+        both = dot(matrix, jnp.concatenate([tokens, cotangents], 1))
+        return both[:, 0:dim], both[:, dim : 2 * dim]
 
     def ocean(band, rows, size):
         first = lax.broadcasted_iota(jnp.int32, (rows, 1), 0) < size
         return jnp.where(first, ocean_mask[0, band], ocean_mask[1, band]).astype(F32)
 
-    g = (assembled(1, cot) * ocean(lat_index, 2 * WIN, WIN)).astype(BF16)
-    project(assembled(0, tok), g, 0)
+    x, g = assembled(const[0:256, PICK], sources(0, tok), sources(1, cot))
+    project(x, (g * ocean(lat_index, 2 * WIN, WIN)).astype(BF16), 0)
     lower_differs = ((key_at // 8 % 8 >= 4) != (query_at // 8 % 8 >= 4)).astype(jnp.int32)
     for w in range(2):
         attend(w * WIN, lower_differs * last_band > 0)
 
     @pl.when(lat_index == 0)
     def _():
-        def edge(i, ref):
-            return dot(const[256:384, EDGE_PICK[0]], ref[:, 0:4].reshape(WIN, dim)) + dot(
-                const[256:384, EDGE_PICK[1]], lon[64 + i * 32 : 64 + (i + 1) * 32]
-            )
-
         last = ocean_mask.shape[1] - 1
-        edge_g = (edge(1, cot) * ocean(last, WIN, 64)).astype(BF16)
-        project(edge(0, tok), edge_g, 2 * WIN)
+        matrix = const[EDGE_PUT : EDGE_PUT + WIN, EDGE_PICK]
+        edge_x, edge_g = assembled(matrix, edge_sources(0, tok), edge_sources(1, cot))
+        project(edge_x, (edge_g * ocean(last, WIN, 64)).astype(BF16), 2 * WIN)
         attend(2 * WIN, key_at // 64 != query_at // 64)
         half_sums(left, right, other, 1 - core, 3 * WIN)
 
@@ -269,7 +290,7 @@
     @pl.when(lat_index == 0)
     def _():
         half_sums(left, right, mine, core, 3 * WIN)
-        edge_back[...] = dot(const[EDGE_PUT : EDGE_PUT + 160, 256:384], branch(2 * WIN, WIN)).astype(BF16)
+        edge_back[...] = dot(const[EDGE_PUT : EDGE_PUT + 160, 0:128], branch(2 * WIN, WIN)).astype(BF16)
 
     @pl.when(lat_index != 0)
     def _():
@@ -343,9 +364,12 @@
     return jnp.sum(parts.astype(F32), 0).astype(BF16)
 
 
-def spread_along(part, axis):
-    parts = jnp.broadcast_to(part[None], (lax.axis_size(axis),) + part.shape)
-    return exchange(parts, axis)
+def ring_exchange(parts):
+    return lax.all_to_all(parts, ALL, 0, 0, axis_index_groups=RINGS, tiled=False)
+
+
+def copies(part):
+    return jnp.broadcast_to(part[None], (16,) + part.shape)
 
 
 def swapped(array):
@@ -402,14 +426,14 @@
     side = lax.ppermute(side_back, LON, east)
     (mine,) = call(add_kernel, [((half, LANES), BF16)], mine, swapped(other))
     mine = summed(exchange(mine.reshape(16, half // 16, LANES), PLANE))
-    mine = summed(exchange(mine.reshape(16, half // 256, LANES), RING))
+    mine = summed(ring_exchange(mine.reshape(16, half // 256, LANES)))
     (rows_back,) = call(
         join_kernel, [((WIN, dim), BF16)], lat_back, side, flops=LONG
     )
     mine, rows_back = tied(mine, rows_back)
     rows_back = lax.ppermute(rows_back, LAT, south)
-    mine = spread_along(mine, RING).reshape(half // 16, LANES)
-    mine = spread_along(mine, PLANE).reshape(half, LANES)
+    mine = ring_exchange(copies(mine)).reshape(half // 16, LANES)
+    mine = exchange(copies(mine), PLANE).reshape(half, LANES)
     (token_grad,) = call(
         token_kernel, [(tokens.shape, BF16)],
         own_back, edge_back, rows_back, side,

time: 125 us -> 122 us (0.976)
  waiting for transfers between devices: 42.8 us -> 26.1 us
  starting transfers between devices: 65 us -> 79.7 us
    all_to_all x0 -> x2, starting transfers between devices: none -> 23.3 us  [ring_exchange(): lax.all_to_all(parts, ALL, 0, 0, axis_index_groups=RINGS, tiled=False)]
    all_to_all x4 -> x2, waiting for transfers between devices: 36.6 us -> 16.8 us  [exchange(): return lax.all_to_all(parts, axis, 0, 0, tiled=False)]
    all_to_all x4 -> x2, starting transfers between devices: 30.7 us -> 20.2 us  [exchange(): return lax.all_to_all(parts, axis, 0, 0, tiled=False)]
    all_to_all x0 -> x2, waiting for transfers between devices: none -> 3.1 us  [ring_exchange(): lax.all_to_all(parts, ALL, 0, 0, axis_index_groups=RINGS, tiled=False)]
    ppermute x2, starting transfers between devices: 4.99 us -> 6.48 us  [swapped(): return lax.ppermute(array, 'core', [(0, 1), (1, 0)])]
  transfers between devices with their start and end apart: 11 -> 11, of which waited for: 8 -> 7; matrix products, arithmetic and copies ran while one was open for 1% -> 1% of each run, Pallas kernels for 2% -> 3%
where the time goes in v7:
time: 122 us
  starting transfers between devices  79.7 us (65%)
  waiting for transfers between devices  26.1 us (21%)
  Pallas kernels  12.6 us (10%)
  local copies, waits for them, and re-layouts  2.27 us (2%)
    all_to_all x2, starting transfers between devices, ring_exchange(): lax.all_to_all(parts, ALL, 0, 0, axis_index_groups=RINGS, tiled=False)  23.3 us
    all_to_all x2, starting transfers between devices, exchange(): return lax.all_to_all(parts, axis, 0, 0, tiled=False)  20.2 us
    all_to_all x2, waiting for transfers between devices, exchange(): return lax.all_to_all(parts, axis, 0, 0, tiled=False)  16.8 us
    ppermute x1, starting transfers between devices, local(): diag = lax.ppermute(diag, LAT + LON, back(diagonal))  16.7 us
    pallas_call x8, Pallas kernels, call(): pl.pallas_call(body, out_shape=[jax.ShapeDtypeStruct(s, d) for s, d in ou...  12.6 us
    ppermute x2, starting transfers between devices, swapped(): return lax.ppermute(array, 'core', [(0, 1), (1, 0)])  6.48 us
    ppermute x1, starting transfers between devices, local(): rows_back = lax.ppermute(rows_back, LAT, south)  5.43 us
    ppermute x1, starting transfers between devices, local(): side = lax.ppermute(side_back, LON, east)  3.26 us
  transfers between devices with their start and end apart: 11, of which 7 were waited for; matrix products, arithmetic and copies ran while one was open for 1% of the time, Pallas kernels for 3%

profile of v7, /device:TPU:1, one launch (start us, length us, event | category | flops | bytes accessed | tf_op | source)
XLA Modules:
  0.0 121.7 jit_solution(16959559365218714928)
XLA Ops:
  0.6 2.0 %send_kernel.1 = (bf16[192,384]{1,0:T(8,128)(2,1)}, bf16[64,384]{1,0:T(8,128)(2,1)}, bf16[128,384]{1,0:T(8,128)(2,1)}) custom-call(bf16[2,8,16,384]{3,2,1,0:T(8,128)(2,1)} %refs_2_.2, bf16[2,8,16,384]{3,2,1,0:T(8,128)(2,1)} %refs_0_.3, bf16[128,128]{1,0:T(8,128)(2,1)} %constant.30.clone.refs_2_), custom_call_target="tpu_custom_call" | custom-call | tf_op jit(solution)/shard_map/send_kernel/pallas_call | solution.py:80
  2.6 16.7 %collective-permute-start.1 = (bf16[64,384]{1,0:T(8,128)(2,1)}, bf16[64,384]{1,0:T(8,128)(2,1)S(1)}, u32[]{:S(2)}, u32[]{:S(2)}) collective-permute-start(bf16[64,384]{1,0:T(8,128)(2,1)} %get-tuple-element.24), channel_id=1, source_target_pairs={{33,0},{34,1},{35,2},{36,3},{37,4},{38,5},{39,6},{40,7},{41,8},{42... | collective-permute-start | bytes 147464 | tf_op jit(solution)/shard_map/ppermute | solution.py:407
  19.3 2.4 %collective-permute-start.2 = (bf16[128,384]{1,0:T(8,128)(2,1)}, bf16[128,384]{1,0:T(8,128)(2,1)S(1)}, u32[]{:S(2)}, u32[]{:S(2)}) collective-permute-start(bf16[128,384]{1,0:T(8,128)(2,1)} %get-tuple-element.25), channel_id=1, source_target_pairs={{1,0},{2,1},{3,2},{4,3},{5,4},{6,5},{7,6},{8,7},{9,8},{10,9},{11,1... | collective-permute-start | bytes 294920 | tf_op jit(solution)/shard_map/ppermute | solution.py:408
  21.7 1.9 %collective-permute-start = (bf16[192,384]{1,0:T(8,128)(2,1)}, bf16[192,384]{1,0:T(8,128)(2,1)S(1)}, u32[]{:S(2)}, u32[]{:S(2)}) collective-permute-start(bf16[192,384]{1,0:T(8,128)(2,1)} %get-tuple-element.23), channel_id=1, source_target_pairs={{32,0},{64,32},{96,64},{128,96},{160,128},{192,160},{224,192},{256... | collective-permute-start | bytes 442376 | tf_op jit(solution)/shard_map/ppermute | solution.py:406
  23.7 0.0 copy-start.2
  23.7 0.0 copy-start.3
  23.7 0.5 pause_kernel.1.refs_11_
  24.3 1.9 %collective-permute-done.2.refs_9_ = bf16[128,384]{1,0:T(8,128)(2,1)S(1)} collective-permute-done((bf16[128,384]{1,0:T(8,128)(2,1)}, bf16[128,384]{1,0:T(8,128)(2,1)S(1)}, u32[]{:S(2)}, u32[]{:S(2)}) %collective-permute-start.2) | collective-permute-done | bytes 98336 | tf_op jit(solution)/shard_map/ppermute | solution.py:408
  26.2 2.2 %collective-permute-done.refs_7_ = bf16[192,384]{1,0:T(8,128)(2,1)S(1)} collective-permute-done((bf16[192,384]{1,0:T(8,128)(2,1)}, bf16[192,384]{1,0:T(8,128)(2,1)S(1)}, u32[]{:S(2)}, u32[]{:S(2)}) %collective-permute-start) | collective-permute-done | bytes 147488 | tf_op jit(solution)/shard_map/ppermute | solution.py:406
  28.4 5.0 %window_kernel.1 = (bf16[2304,128]{1,0:T(8,128)(2,1)S(1)}, bf16[2,384,384]{2,1,0:T(8,128)(2,1)S(1)}, bf16[12,384,128]{2,1,0:T(8,128)(2,1)S(1)}, bf16[384,384]{1,0:T(8,128)(2,1)S(1)}) custom-call(s32[1]{0:T(128)} %bitcast.refs_0_, s32[2,16]{1,0:T(2,128)S(1)} %bitcast.6, bf16[2,8,16,384]{3,2,1,0:T(8,128)(2,1)S(1)} %copy-done.1, ...), custom_call_target="tpu_custom_call" | custom-call | tf_op jit(solution)/shard_map/window_kernel/pallas_call | solution.py:80
  33.4 2.0 %collective-permute-start.3 = (bf16[2304,128]{1,0:T(8,128)(2,1)S(1)}, bf16[2304,128]{1,0:T(8,128)(2,1)S(1)}, u32[]{:S(2)}, u32[]{:S(2)}) collective-permute-start(bf16[2304,128]{1,0:T(8,128)(2,1)S(1)} %get-tuple-element.30), channel_id=1, source_target_pairs={{0,32},{32,0},{1,33},{33,1},{2,34},{34,2},{3,35},{35,3},{4,36},{36... | collective-permute-start | bytes 1769480 | tf_op jit(solution)/shard_map/ppermute | solution.py:376
  35.5 1.3 %branch_kernel.1 = (bf16[2304,128]{1,0:T(8,128)(2,1)S(1)}, bf16[128,384]{1,0:T(8,128)(2,1)S(1)}, bf16[96,384]{1,0:T(8,128)(2,1)S(1)}, bf16[96,384]{1,0:T(8,128)(2,1)S(1)}, bf16[160,384]{1,0:T(8,128)(2,1)S(1)}) custom-call(s32[1]{0:T(128)} %bitcast.refs_0_, bf16[2,384,384]{2,1,0:T(8,128)(2,1)S(1)} %get-tuple-element.26.refs_1_, ...), custom_call_target="tpu_custom_call" | custom-call | flops 30000001024 | tf_op jit(solution)/shard_map/branch_kernel/pallas_call | solution.py:80
  36.8 0.6 collective-permute-done.3.refs_1_
  37.3 1.0 add_kernel.1
  38.3 15.4 %all-to-all-start = ((bf16[16,144,128]{2,1,0:T(8,128)(2,1)}), bf16[16,144,128]{2,1,0:T(8,128)(2,1)S(1)}, u32[]{:S(2)}, u32[]{:S(2)}) async-start(bf16[16,144,128]{2,1,0:T(8,128)(2,1)} %bitcast.2), calls=%async_computation | async-start | bytes 1179648 | tf_op jit(solution)/shard_map/all_to_all | solution.py:360
  53.7 3.3 %collective-permute-start.4 = (bf16[96,384]{1,0:T(8,128)(2,1)S(1)}, bf16[96,384]{1,0:T(8,128)(2,1)S(1)}, u32[]{:S(2)}, u32[]{:S(2)}) collective-permute-start(bf16[96,384]{1,0:T(8,128)(2,1)S(1)} %get-tuple-element.32), channel_id=1, source_target_pairs={{0,1},{1,2},{2,3},{3,4},{4,5},{5,6},{6,7},{7,8},{8,9},{9,10},{10,1... | collective-permute-start | bytes 221192 | tf_op jit(solution)/shard_map/ppermute | solution.py:426
  57.0 7.5 %all-to-all-done = bf16[16,144,128]{2,1,0:T(8,128)(2,1)S(1)} async-done(((bf16[16,144,128]{2,1,0:T(8,128)(2,1)}), bf16[16,144,128]{2,1,0:T(8,128)(2,1)S(1)}, u32[]{:S(2)}, u32[]{:S(2)}) %all-to-all-start) | async-done | bytes 589856 | tf_op jit(solution)/shard_map/all_to_all | solution.py:360
  64.5 0.1 reduce_sum.24
  64.5 0.7 reshape.24
  65.2 11.5 %all-to-all-start.1 = ((bf16[16,9,128]{2,1,0:T(8,128)(2,1)}), bf16[16,9,128]{2,1,0:T(8,128)(2,1)S(1)}, u32[]{:S(2)}, u32[]{:S(2)}) async-start(bf16[16,9,128]{2,1,0:T(8,128)(2,1)} %reshape.24), calls=%async_computation.1 | async-start | bytes 131072 | tf_op jit(solution)/shard_map/all_to_all | solution.py:368
  76.7 0.0 copy-start.7
  76.7 3.1 %all-to-all-done.1 = bf16[16,9,128]{2,1,0:T(8,128)(2,1)S(1)} async-done(((bf16[16,9,128]{2,1,0:T(8,128)(2,1)}), bf16[16,9,128]{2,1,0:T(8,128)(2,1)S(1)}, u32[]{:S(2)}, u32[]{:S(2)}) %all-to-all-start.1) | async-done | bytes 36896 | tf_op jit(solution)/shard_map/all_to_all | solution.py:368
  79.8 0.6 broadcast_in_dim.6
  80.5 11.9 %all-to-all-start.2 = ((bf16[16,9,128]{2,1,0:T(8,128)(2,1)}), bf16[16,9,128]{2,1,0:T(8,128)(2,1)S(1)}, u32[]{:S(2)}, u32[]{:S(2)}) async-start(bf16[16,9,128]{2,1,0:T(8,128)(2,1)} %broadcast_in_dim.6), calls=%async_computation.2 | async-start | bytes 131072 | tf_op jit(solution)/shard_map/all_to_all | solution.py:368
  92.3 5.4 %collective-permute-start.5 = (bf16[128,384]{1,0:T(8,128)(2,1)S(1)}, bf16[128,384]{1,0:T(8,128)(2,1)S(1)}, u32[]{:S(2)}, u32[]{:S(2)}) collective-permute-start(bf16[128,384]{1,0:T(8,128)(2,1)S(1)} %join_kernel.1), channel_id=1, source_target_pairs={{0,32},{32,64},{64,96},{96,128},{128,160},{160,192},{192,224},{224... | collective-permute-start | bytes 294920 | tf_op jit(solution)/shard_map/ppermute | solution.py:434
  97.8 0.9 broadcast_in_dim.15
  98.7 4.8 %all-to-all-start.3 = ((bf16[16,144,128]{2,1,0:T(8,128)(2,1)}), bf16[16,144,128]{2,1,0:T(8,128)(2,1)S(1)}, u32[]{:S(2)}, u32[]{:S(2)}) async-start(bf16[16,144,128]{2,1,0:T(8,128)(2,1)} %broadcast_in_dim.15), calls=%async_computation.3 | async-start | bytes 1179648 | tf_op jit(solution)/shard_map/all_to_all | solution.py:360
  103.5 1.3 %token_kernel.1 = bf16[2,8,16,384]{3,2,1,0:T(8,128)(2,1)} custom-call(bf16[2,8,16,384]{3,2,1,0:T(8,128)(2,1)S(1)} %copy-done.2, bf16[128,256]{1,0:T(8,128)(2,1)S(1)} %copy-done.7, bf16[128,384]{1,0:T(8,128)(2,1)S(1)} %get-tuple-element.34.refs_2_, bf16[160,384]{1,0:T(8,128)(2,1)S(1)} %get-tuple-element.35.refs_3_, ...), custom_call_target="tpu_custom_call" | custom-call | flops 30000001024 | tf_op jit(solution)/shard_map/token_kernel/pallas_call | solution.py:80
  104.8 9.3 %all-to-all-done.3 = bf16[16,144,128]{2,1,0:T(8,128)(2,1)S(1)} async-done(((bf16[16,144,128]{2,1,0:T(8,128)(2,1)}), bf16[16,144,128]{2,1,0:T(8,128)(2,1)S(1)}, u32[]{:S(2)}, u32[]{:S(2)}) %all-to-all-start.3) | async-done | bytes 589856 | tf_op jit(solution)/shard_map/all_to_all | solution.py:360
  114.1 4.5 %collective-permute-start.6 = (bf16[2304,128]{1,0:T(8,128)(2,1)S(1)}, bf16[2304,128]{1,0:T(8,128)(2,1)S(1)}, u32[]{:S(2)}, u32[]{:S(2)}) collective-permute-start(bf16[2304,128]{1,0:T(8,128)(2,1)S(1)} %bitcast.4), channel_id=1, source_target_pairs={{0,32},{32,0},{1,33},{33,1},{2,34},{34,2},{3,35},{35,3},{4,36},{36... | collective-permute-start | bytes 1769480 | tf_op jit(solution)/shard_map/ppermute | solution.py:376
  118.5 1.6 %collective-permute-done.6.refs_3_ = bf16[2304,128]{1,0:T(8,128)(2,1)S(1)} collective-permute-done((bf16[2304,128]{1,0:T(8,128)(2,1)S(1)}, bf16[2304,128]{1,0:T(8,128)(2,1)S(1)}, u32[]{:S(2)}, u32[]{:S(2)}) %collective-permute-start.6) | collective-permute-done | bytes 589856 | tf_op jit(solution)/shard_map/ppermute | solution.py:376
  120.1 1.6 %result_kernel.1 = (bf16[384,1152]{1,0:T(8,128)(2,1)}, bf16[384,384]{1,0:T(8,128)(2,1)}, bf16[384]{0:T(512)(128)(2,1)}) custom-call(s32[1]{0:T(128)} %bitcast.refs_0_, bf16[384,1152]{1,0:T(8,128)(2,1)S(1)} %copy-done, bf16[2304,128]{1,0:T(8,128)(2,1)S(1)} %bitcast.5, bf16[2304,128]{1,0:T(8,128)(2,1)S(1)} %collective-permute-done.6.refs_3_, ...), custom_call_target="tpu_custom_call" | custom-call | tf_op jit(solution)/shard_map/result_kernel/pallas_call | solution.py:80
  (20 shorter events, 0.1 us)
Async XLA Ops:
  2.6 21.7 %collective-permute-start.1 = (bf16[64,384]{1,0:T(8,128)(2,1)}, bf16[64,384]{1,0:T(8,128)(2,1)S(1)}, u32[]{:S(2)}, u32[]{:S(2)}) collective-permute-start(bf16[64,384]{1,0:T(8,128)(2,1)} %get-tuple-element.24), channel_id=1, source_target_pairs={{33,0},{34,1},{35,2},{36,3},{37,4},{38,5},{39,6},{40,7},{41,8},{42... | collective-permute-start | bytes 147464 | tf_op jit(solution)/shard_map/ppermute | solution.py:407
  19.3 6.9 %collective-permute-start.2 = (bf16[128,384]{1,0:T(8,128)(2,1)}, bf16[128,384]{1,0:T(8,128)(2,1)S(1)}, u32[]{:S(2)}, u32[]{:S(2)}) collective-permute-start(bf16[128,384]{1,0:T(8,128)(2,1)} %get-tuple-element.25), channel_id=1, source_target_pairs={{1,0},{2,1},{3,2},{4,3},{5,4},{6,5},{7,6},{8,7},{9,8},{10,9},{11,1... | collective-permute-start | bytes 294920 | tf_op jit(solution)/shard_map/ppermute | solution.py:408
  21.7 6.7 %collective-permute-start = (bf16[192,384]{1,0:T(8,128)(2,1)}, bf16[192,384]{1,0:T(8,128)(2,1)S(1)}, u32[]{:S(2)}, u32[]{:S(2)}) collective-permute-start(bf16[192,384]{1,0:T(8,128)(2,1)} %get-tuple-element.23), channel_id=1, source_target_pairs={{32,0},{64,32},{96,64},{128,96},{160,128},{192,160},{224,192},{256... | collective-permute-start | bytes 442376 | tf_op jit(solution)/shard_map/ppermute | solution.py:406
  23.6 4.7 %copy-start = (bf16[384,1152]{1,0:T(8,128)(2,1)S(1)}, bf16[384,1152]{1,0:T(8,128)(2,1)}, u32[]{:S(2)}) copy-start(bf16[384,1152]{1,0:T(8,128)(2,1)} %refs_1_.4) | copy-start | bytes 2654212
  23.6 4.7 %copy-start.1 = (bf16[2,8,16,384]{3,2,1,0:T(8,128)(2,1)S(1)}, bf16[2,8,16,384]{3,2,1,0:T(8,128)(2,1)}, u32[]{:S(2)}) copy-start(bf16[2,8,16,384]{3,2,1,0:T(8,128)(2,1)} %refs_2_.2) | copy-start | bytes 589828
  23.7 4.7 %copy-start.2 = (bf16[2,8,16,384]{3,2,1,0:T(8,128)(2,1)S(1)}, bf16[2,8,16,384]{3,2,1,0:T(8,128)(2,1)}, u32[]{:S(2)}) copy-start(bf16[2,8,16,384]{3,2,1,0:T(8,128)(2,1)} %refs_0_.3) | copy-start | bytes 589828
  23.7 4.7 %copy-start.3 = (bf16[704,384]{1,0:T(8,128)(2,1)S(1)}, bf16[704,384]{1,0:T(8,128)(2,1)}, u32[]{:S(2)}) copy-start(bf16[704,384]{1,0:T(8,128)(2,1)} %constant.31.clone.refs_3_.refs_4_) | copy-start | bytes 1622020
  23.7 4.7 %copy-start.4 = (bf16[384,384]{1,0:T(8,128)(2,1)S(1)}, bf16[384,384]{1,0:T(8,128)(2,1)}, u32[]{:S(2)}) copy-start(bf16[384,384]{1,0:T(8,128)(2,1)} %refs_6_.2) | copy-start | bytes 884740
  23.7 4.7 %copy-start.5 = (bf16[384]{0:T(512)(128)(2,1)S(1)}, bf16[384]{0:T(512)(128)(2,1)}, u32[]{:S(2)}) copy-start(bf16[384]{0:T(512)(128)(2,1)} %refs_4_.4) | copy-start | bytes 2308
  23.7 4.7 %copy-start.6 = (s32[16,2]{0,1:T(2,128)S(1)}, s32[16,2]{0,1:T(2,128)}, u32[]{:S(2)}) copy-start(s32[16,2]{0,1:T(2,128)} %param.11) | copy-start | bytes 388
  33.4 3.9 %collective-permute-start.3 = (bf16[2304,128]{1,0:T(8,128)(2,1)S(1)}, bf16[2304,128]{1,0:T(8,128)(2,1)S(1)}, u32[]{:S(2)}, u32[]{:S(2)}) collective-permute-start(bf16[2304,128]{1,0:T(8,128)(2,1)S(1)} %get-tuple-element.30), channel_id=1, source_target_pairs={{0,32},{32,0},{1,33},{33,1},{2,34},{34,2},{3,35},{35,3},{4,36},{36... | collective-permute-start | bytes 1769480 | tf_op jit(solution)/shard_map/ppermute | solution.py:376
  38.3 26.2 %all-to-all-start = ((bf16[16,144,128]{2,1,0:T(8,128)(2,1)}), bf16[16,144,128]{2,1,0:T(8,128)(2,1)S(1)}, u32[]{:S(2)}, u32[]{:S(2)}) async-start(bf16[16,144,128]{2,1,0:T(8,128)(2,1)} %bitcast.2), calls=%async_computation | async-start | bytes 1179648 | tf_op jit(solution)/shard_map/all_to_all | solution.py:360
  53.7 23.0 %collective-permute-start.4 = (bf16[96,384]{1,0:T(8,128)(2,1)S(1)}, bf16[96,384]{1,0:T(8,128)(2,1)S(1)}, u32[]{:S(2)}, u32[]{:S(2)}) collective-permute-start(bf16[96,384]{1,0:T(8,128)(2,1)S(1)} %get-tuple-element.32), channel_id=1, source_target_pairs={{0,1},{1,2},{2,3},{3,4},{4,5},{5,6},{6,7},{7,8},{8,9},{9,10},{10,1... | collective-permute-start | bytes 221192 | tf_op jit(solution)/shard_map/ppermute | solution.py:426
  65.2 14.6 %all-to-all-start.1 = ((bf16[16,9,128]{2,1,0:T(8,128)(2,1)}), bf16[16,9,128]{2,1,0:T(8,128)(2,1)S(1)}, u32[]{:S(2)}, u32[]{:S(2)}) async-start(bf16[16,9,128]{2,1,0:T(8,128)(2,1)} %reshape.24), calls=%async_computation.1 | async-start | bytes 131072 | tf_op jit(solution)/shard_map/all_to_all | solution.py:368
  76.7 26.8 %copy-start.7 = (bf16[128,256]{1,0:T(8,128)(2,1)S(1)}, bf16[128,256]{1,0:T(8,128)(2,1)}, u32[]{:S(2)}) copy-start(bf16[128,256]{1,0:T(8,128)(2,1)} %constant.32.clone.refs_1_) | copy-start | bytes 196612
  80.5 17.3 %all-to-all-start.2 = ((bf16[16,9,128]{2,1,0:T(8,128)(2,1)}), bf16[16,9,128]{2,1,0:T(8,128)(2,1)S(1)}, u32[]{:S(2)}, u32[]{:S(2)}) async-start(bf16[16,9,128]{2,1,0:T(8,128)(2,1)} %broadcast_in_dim.6), calls=%async_computation.2 | async-start | bytes 131072 | tf_op jit(solution)/shard_map/all_to_all | solution.py:368
  92.3 11.1 %collective-permute-start.5 = (bf16[128,384]{1,0:T(8,128)(2,1)S(1)}, bf16[128,384]{1,0:T(8,128)(2,1)S(1)}, u32[]{:S(2)}, u32[]{:S(2)}) collective-permute-start(bf16[128,384]{1,0:T(8,128)(2,1)S(1)} %join_kernel.1), channel_id=1, source_target_pairs={{0,32},{32,64},{64,96},{96,128},{128,160},{160,192},{192,224},{224... | collective-permute-start | bytes 294920 | tf_op jit(solution)/shard_map/ppermute | solution.py:434
  98.7 15.3 %all-to-all-start.3 = ((bf16[16,144,128]{2,1,0:T(8,128)(2,1)}), bf16[16,144,128]{2,1,0:T(8,128)(2,1)S(1)}, u32[]{:S(2)}, u32[]{:S(2)}) async-start(bf16[16,144,128]{2,1,0:T(8,128)(2,1)} %broadcast_in_dim.15), calls=%async_computation.3 | async-start | bytes 1179648 | tf_op jit(solution)/shard_map/all_to_all | solution.py:360
  114.1 6.1 %collective-permute-start.6 = (bf16[2304,128]{1,0:T(8,128)(2,1)S(1)}, bf16[2304,128]{1,0:T(8,128)(2,1)S(1)}, u32[]{:S(2)}, u32[]{:S(2)}) collective-permute-start(bf16[2304,128]{1,0:T(8,128)(2,1)S(1)} %bitcast.4), channel_id=1, source_target_pairs={{0,32},{32,0},{1,33},{33,1},{2,34},{34,2},{3,35},{35,3},{4,36},{36... | collective-permute-start | bytes 1769480 | tf_op jit(solution)/shard_map/ppermute | solution.py:376

commit v8 on v7

--- a/solution.py
+++ b/solution.py
@@ -16,7 +16,6 @@
 WIN = 128
 LAT = ("zhi", "x", "core")
 LON = ("zlo", "y")
-PLANE = ("x", "y")
 ALL = ("zhi", "x", "core", "zlo", "y")
 
 
@@ -30,7 +29,12 @@
     ]
 
 
-RINGS = rings(8)
+RINGS = rings(7)
+PLANES = [
+    [(((z // 8 * 4 + (x + 3) % 4) * 2 + core) * 8 + z % 8) * 4 + y for x in range(4) for y in range(4)]
+    for z in range(16)
+    for core in range(2)
+]
 F32 = jnp.float32
 BF16 = jnp.bfloat16
 LONG = 3 * 10**10
@@ -356,16 +360,12 @@
         write((other, mine))
 
 
-def exchange(parts, axis):
-    return lax.all_to_all(parts, axis, 0, 0, tiled=False)
+def exchange(parts, groups):
+    return lax.all_to_all(parts, ALL, 0, 0, axis_index_groups=groups, tiled=False)
 
 
 def summed(parts):
     return jnp.sum(parts.astype(F32), 0).astype(BF16)
-
-
-def ring_exchange(parts):
-    return lax.all_to_all(parts, ALL, 0, 0, axis_index_groups=RINGS, tiled=False)
 
 
 def copies(part):
@@ -425,15 +425,15 @@
 
     side = lax.ppermute(side_back, LON, east)
     (mine,) = call(add_kernel, [((half, LANES), BF16)], mine, swapped(other))
-    mine = summed(exchange(mine.reshape(16, half // 16, LANES), PLANE))
-    mine = summed(ring_exchange(mine.reshape(16, half // 256, LANES)))
+    mine = summed(exchange(mine.reshape(16, half // 16, LANES), PLANES))
+    mine = summed(exchange(mine.reshape(16, half // 256, LANES), RINGS))
     (rows_back,) = call(
         join_kernel, [((WIN, dim), BF16)], lat_back, side, flops=LONG
     )
     mine, rows_back = tied(mine, rows_back)
     rows_back = lax.ppermute(rows_back, LAT, south)
-    mine = ring_exchange(copies(mine)).reshape(half // 16, LANES)
-    mine = exchange(copies(mine), PLANE).reshape(half, LANES)
+    mine = exchange(copies(mine), RINGS).reshape(half // 16, LANES)
+    mine = exchange(copies(mine), PLANES).reshape(half, LANES)
     (token_grad,) = call(
         token_kernel, [(tokens.shape, BF16)],
         own_back, edge_back, rows_back, side,

time: 122 us -> 121 us (level)
  waiting for transfers between devices: 26.1 us -> 24.2 us
    all_to_all x4, waiting for transfers between devices: 19.9 us -> 17.9 us  [exchange(): lax.all_to_all(parts, ALL, 0, 0, axis_index_groups=groups, tiled=False)]
    all_to_all x4, starting transfers between devices: 43.5 us -> 42.1 us  [exchange(): lax.all_to_all(parts, ALL, 0, 0, axis_index_groups=groups, tiled=False)]
where the time goes in v8:
time: 121 us; the launch traced here: 120 us
  starting transfers between devices  80 us (66%)
  waiting for transfers between devices  24.2 us (20%)
  Pallas kernels  12.6 us (10%)
  local copies, waits for them, and re-layouts  2.27 us (2%)
    all_to_all x4, starting transfers between devices, exchange(): lax.all_to_all(parts, ALL, 0, 0, axis_index_groups=groups, tiled=False)  42.1 us
    all_to_all x4, waiting for transfers between devices, exchange(): lax.all_to_all(parts, ALL, 0, 0, axis_index_groups=groups, tiled=False)  17.9 us
    ppermute x1, starting transfers between devices, local(): diag = lax.ppermute(diag, LAT + LON, back(diagonal))  16.7 us
    pallas_call x8, Pallas kernels, call(): pl.pallas_call(body, out_shape=[jax.ShapeDtypeStruct(s, d) for s, d in ou...  12.6 us
    ppermute x2, starting transfers between devices, swapped(): return lax.ppermute(array, 'core', [(0, 1), (1, 0)])  7.28 us
    ppermute x1, starting transfers between devices, local(): rows_back = lax.ppermute(rows_back, LAT, south)  6.51 us
    ppermute x1, starting transfers between devices, local(): side = lax.ppermute(side_back, LON, east)  3.09 us
  transfers between devices with their start and end apart: 11, of which 7 were waited for; matrix products, arithmetic and copies ran while one was open for 1% of the time, Pallas kernels for 3%

profile of v8, /device:TPU:1, one launch (start us, length us, event | category | flops | bytes accessed | tf_op | source)
XLA Modules:
  0.0 120.1 jit_solution(16082958723093714563)
XLA Ops:
  0.6 2.0 %send_kernel.1 = (bf16[192,384]{1,0:T(8,128)(2,1)}, bf16[64,384]{1,0:T(8,128)(2,1)}, bf16[128,384]{1,0:T(8,128)(2,1)}) custom-call(bf16[2,8,16,384]{3,2,1,0:T(8,128)(2,1)} %refs_2_.2, bf16[2,8,16,384]{3,2,1,0:T(8,128)(2,1)} %refs_0_.3, bf16[128,128]{1,0:T(8,128)(2,1)} %constant.30.clone.refs_2_), custom_call_target="tpu_custom_call" | custom-call | tf_op jit(solution)/shard_map/send_kernel/pallas_call | solution.py:84
  2.6 16.7 %collective-permute-start.1 = (bf16[64,384]{1,0:T(8,128)(2,1)}, bf16[64,384]{1,0:T(8,128)(2,1)S(1)}, u32[]{:S(2)}, u32[]{:S(2)}) collective-permute-start(bf16[64,384]{1,0:T(8,128)(2,1)} %get-tuple-element.24), channel_id=1, source_target_pairs={{33,0},{34,1},{35,2},{36,3},{37,4},{38,5},{39,6},{40,7},{41,8},{42... | collective-permute-start | bytes 147464 | tf_op jit(solution)/shard_map/ppermute | solution.py:407
  19.3 2.4 %collective-permute-start.2 = (bf16[128,384]{1,0:T(8,128)(2,1)}, bf16[128,384]{1,0:T(8,128)(2,1)S(1)}, u32[]{:S(2)}, u32[]{:S(2)}) collective-permute-start(bf16[128,384]{1,0:T(8,128)(2,1)} %get-tuple-element.25), channel_id=1, source_target_pairs={{1,0},{2,1},{3,2},{4,3},{5,4},{6,5},{7,6},{8,7},{9,8},{10,9},{11,1... | collective-permute-start | bytes 294920 | tf_op jit(solution)/shard_map/ppermute | solution.py:408
  21.7 1.9 %collective-permute-start = (bf16[192,384]{1,0:T(8,128)(2,1)}, bf16[192,384]{1,0:T(8,128)(2,1)S(1)}, u32[]{:S(2)}, u32[]{:S(2)}) collective-permute-start(bf16[192,384]{1,0:T(8,128)(2,1)} %get-tuple-element.23), channel_id=1, source_target_pairs={{32,0},{64,32},{96,64},{128,96},{160,128},{192,160},{224,192},{256... | collective-permute-start | bytes 442376 | tf_op jit(solution)/shard_map/ppermute | solution.py:406
  23.6 0.0 copy-start
  23.7 0.0 copy-start.3
  23.7 0.5 pause_kernel.1.refs_11_
  24.3 1.9 %collective-permute-done.2.refs_9_ = bf16[128,384]{1,0:T(8,128)(2,1)S(1)} collective-permute-done((bf16[128,384]{1,0:T(8,128)(2,1)}, bf16[128,384]{1,0:T(8,128)(2,1)S(1)}, u32[]{:S(2)}, u32[]{:S(2)}) %collective-permute-start.2) | collective-permute-done | bytes 98336 | tf_op jit(solution)/shard_map/ppermute | solution.py:408
  26.2 2.2 %collective-permute-done.refs_7_ = bf16[192,384]{1,0:T(8,128)(2,1)S(1)} collective-permute-done((bf16[192,384]{1,0:T(8,128)(2,1)}, bf16[192,384]{1,0:T(8,128)(2,1)S(1)}, u32[]{:S(2)}, u32[]{:S(2)}) %collective-permute-start) | collective-permute-done | bytes 147488 | tf_op jit(solution)/shard_map/ppermute | solution.py:406
  28.4 5.0 %window_kernel.1 = (bf16[2304,128]{1,0:T(8,128)(2,1)S(1)}, bf16[2,384,384]{2,1,0:T(8,128)(2,1)S(1)}, bf16[12,384,128]{2,1,0:T(8,128)(2,1)S(1)}, bf16[384,384]{1,0:T(8,128)(2,1)S(1)}) custom-call(s32[1]{0:T(128)} %bitcast.refs_0_, s32[2,16]{1,0:T(2,128)S(1)} %bitcast.6, bf16[2,8,16,384]{3,2,1,0:T(8,128)(2,1)S(1)} %copy-done.1, ...), custom_call_target="tpu_custom_call" | custom-call | tf_op jit(solution)/shard_map/window_kernel/pallas_call | solution.py:84
  33.4 2.0 %collective-permute-start.3 = (bf16[2304,128]{1,0:T(8,128)(2,1)S(1)}, bf16[2304,128]{1,0:T(8,128)(2,1)S(1)}, u32[]{:S(2)}, u32[]{:S(2)}) collective-permute-start(bf16[2304,128]{1,0:T(8,128)(2,1)S(1)} %get-tuple-element.30), channel_id=1, source_target_pairs={{0,32},{32,0},{1,33},{33,1},{2,34},{34,2},{3,35},{35,3},{4,36},{36... | collective-permute-start | bytes 1769480 | tf_op jit(solution)/shard_map/ppermute | solution.py:376
  35.5 1.3 %branch_kernel.1 = (bf16[2304,128]{1,0:T(8,128)(2,1)S(1)}, bf16[128,384]{1,0:T(8,128)(2,1)S(1)}, bf16[96,384]{1,0:T(8,128)(2,1)S(1)}, bf16[96,384]{1,0:T(8,128)(2,1)S(1)}, bf16[160,384]{1,0:T(8,128)(2,1)S(1)}) custom-call(s32[1]{0:T(128)} %bitcast.refs_0_, bf16[2,384,384]{2,1,0:T(8,128)(2,1)S(1)} %get-tuple-element.26.refs_1_, ...), custom_call_target="tpu_custom_call" | custom-call | flops 30000001024 | tf_op jit(solution)/shard_map/branch_kernel/pallas_call | solution.py:84
  36.8 0.6 collective-permute-done.3.refs_1_
  37.3 1.0 add_kernel.1
  38.3 16.7 %all-to-all-start = ((bf16[16,144,128]{2,1,0:T(8,128)(2,1)}), bf16[16,144,128]{2,1,0:T(8,128)(2,1)S(1)}, u32[]{:S(2)}, u32[]{:S(2)}) async-start(bf16[16,144,128]{2,1,0:T(8,128)(2,1)} %bitcast.2), calls=%async_computation | async-start | bytes 1179648 | tf_op jit(solution)/shard_map/all_to_all | solution.py:364
  55.0 3.1 %collective-permute-start.4 = (bf16[96,384]{1,0:T(8,128)(2,1)S(1)}, bf16[96,384]{1,0:T(8,128)(2,1)S(1)}, u32[]{:S(2)}, u32[]{:S(2)}) collective-permute-start(bf16[96,384]{1,0:T(8,128)(2,1)S(1)} %get-tuple-element.32), channel_id=1, source_target_pairs={{0,1},{1,2},{2,3},{3,4},{4,5},{5,6},{6,7},{7,8},{8,9},{9,10},{10,1... | collective-permute-start | bytes 221192 | tf_op jit(solution)/shard_map/ppermute | solution.py:426
  58.1 6.1 %all-to-all-done = bf16[16,144,128]{2,1,0:T(8,128)(2,1)S(1)} async-done(((bf16[16,144,128]{2,1,0:T(8,128)(2,1)}), bf16[16,144,128]{2,1,0:T(8,128)(2,1)S(1)}, u32[]{:S(2)}, u32[]{:S(2)}) %all-to-all-start) | async-done | bytes 589856 | tf_op jit(solution)/shard_map/all_to_all | solution.py:364
  64.2 0.1 reduce_sum.24
  64.3 0.7 reshape.24
  64.9 9.4 %all-to-all-start.1 = ((bf16[16,9,128]{2,1,0:T(8,128)(2,1)}), bf16[16,9,128]{2,1,0:T(8,128)(2,1)S(1)}, u32[]{:S(2)}, u32[]{:S(2)}) async-start(bf16[16,9,128]{2,1,0:T(8,128)(2,1)} %reshape.24), calls=%async_computation.1 | async-start | bytes 131072 | tf_op jit(solution)/shard_map/all_to_all | solution.py:364
  74.3 0.0 copy-start.7
  74.3 5.2 %all-to-all-done.1 = bf16[16,9,128]{2,1,0:T(8,128)(2,1)S(1)} async-done(((bf16[16,9,128]{2,1,0:T(8,128)(2,1)}), bf16[16,9,128]{2,1,0:T(8,128)(2,1)S(1)}, u32[]{:S(2)}, u32[]{:S(2)}) %all-to-all-start.1) | async-done | bytes 36896 | tf_op jit(solution)/shard_map/all_to_all | solution.py:364
  79.6 0.6 broadcast_in_dim.6
  80.2 9.5 %all-to-all-start.2 = ((bf16[16,9,128]{2,1,0:T(8,128)(2,1)}), bf16[16,9,128]{2,1,0:T(8,128)(2,1)S(1)}, u32[]{:S(2)}, u32[]{:S(2)}) async-start(bf16[16,9,128]{2,1,0:T(8,128)(2,1)} %broadcast_in_dim.6), calls=%async_computation.2 | async-start | bytes 131072 | tf_op jit(solution)/shard_map/all_to_all | solution.py:364
  89.7 6.5 %collective-permute-start.5 = (bf16[128,384]{1,0:T(8,128)(2,1)S(1)}, bf16[128,384]{1,0:T(8,128)(2,1)S(1)}, u32[]{:S(2)}, u32[]{:S(2)}) collective-permute-start(bf16[128,384]{1,0:T(8,128)(2,1)S(1)} %join_kernel.1), channel_id=1, source_target_pairs={{0,32},{32,64},{64,96},{96,128},{128,160},{160,192},{192,224},{224... | collective-permute-start | bytes 294920 | tf_op jit(solution)/shard_map/ppermute | solution.py:434
  96.3 0.9 broadcast_in_dim.15
  97.2 6.6 %all-to-all-start.3 = ((bf16[16,144,128]{2,1,0:T(8,128)(2,1)}), bf16[16,144,128]{2,1,0:T(8,128)(2,1)S(1)}, u32[]{:S(2)}, u32[]{:S(2)}) async-start(bf16[16,144,128]{2,1,0:T(8,128)(2,1)} %broadcast_in_dim.15), calls=%async_computation.3 | async-start | bytes 1179648 | tf_op jit(solution)/shard_map/all_to_all | solution.py:364
  103.8 1.3 %token_kernel.1 = bf16[2,8,16,384]{3,2,1,0:T(8,128)(2,1)} custom-call(bf16[2,8,16,384]{3,2,1,0:T(8,128)(2,1)S(1)} %copy-done.2, bf16[128,256]{1,0:T(8,128)(2,1)S(1)} %copy-done.7, bf16[128,384]{1,0:T(8,128)(2,1)S(1)} %get-tuple-element.34.refs_2_, bf16[160,384]{1,0:T(8,128)(2,1)S(1)} %get-tuple-element.35.refs_3_, ...), custom_call_target="tpu_custom_call" | custom-call | flops 30000001024 | tf_op jit(solution)/shard_map/token_kernel/pallas_call | solution.py:84
  105.0 6.6 %all-to-all-done.3 = bf16[16,144,128]{2,1,0:T(8,128)(2,1)S(1)} async-done(((bf16[16,144,128]{2,1,0:T(8,128)(2,1)}), bf16[16,144,128]{2,1,0:T(8,128)(2,1)S(1)}, u32[]{:S(2)}, u32[]{:S(2)}) %all-to-all-start.3) | async-done | bytes 589856 | tf_op jit(solution)/shard_map/all_to_all | solution.py:364
  111.6 5.3 %collective-permute-start.6 = (bf16[2304,128]{1,0:T(8,128)(2,1)S(1)}, bf16[2304,128]{1,0:T(8,128)(2,1)S(1)}, u32[]{:S(2)}, u32[]{:S(2)}) collective-permute-start(bf16[2304,128]{1,0:T(8,128)(2,1)S(1)} %bitcast.4), channel_id=1, source_target_pairs={{0,32},{32,0},{1,33},{33,1},{2,34},{34,2},{3,35},{35,3},{4,36},{36... | collective-permute-start | bytes 1769480 | tf_op jit(solution)/shard_map/ppermute | solution.py:376
  116.9 1.6 %collective-permute-done.6.refs_3_ = bf16[2304,128]{1,0:T(8,128)(2,1)S(1)} collective-permute-done((bf16[2304,128]{1,0:T(8,128)(2,1)S(1)}, bf16[2304,128]{1,0:T(8,128)(2,1)S(1)}, u32[]{:S(2)}, u32[]{:S(2)}) %collective-permute-start.6) | collective-permute-done | bytes 589856 | tf_op jit(solution)/shard_map/ppermute | solution.py:376
  118.5 1.6 %result_kernel.1 = (bf16[384,1152]{1,0:T(8,128)(2,1)}, bf16[384,384]{1,0:T(8,128)(2,1)}, bf16[384]{0:T(512)(128)(2,1)}) custom-call(s32[1]{0:T(128)} %bitcast.refs_0_, bf16[384,1152]{1,0:T(8,128)(2,1)S(1)} %copy-done, bf16[2304,128]{1,0:T(8,128)(2,1)S(1)} %bitcast.5, bf16[2304,128]{1,0:T(8,128)(2,1)S(1)} %collective-permute-done.6.refs_3_, ...), custom_call_target="tpu_custom_call" | custom-call | tf_op jit(solution)/shard_map/result_kernel/pallas_call | solution.py:84
  (20 shorter events, 0.1 us)
Async XLA Ops:
  2.6 21.7 %collective-permute-start.1 = (bf16[64,384]{1,0:T(8,128)(2,1)}, bf16[64,384]{1,0:T(8,128)(2,1)S(1)}, u32[]{:S(2)}, u32[]{:S(2)}) collective-permute-start(bf16[64,384]{1,0:T(8,128)(2,1)} %get-tuple-element.24), channel_id=1, source_target_pairs={{33,0},{34,1},{35,2},{36,3},{37,4},{38,5},{39,6},{40,7},{41,8},{42... | collective-permute-start | bytes 147464 | tf_op jit(solution)/shard_map/ppermute | solution.py:407
  19.3 6.9 %collective-permute-start.2 = (bf16[128,384]{1,0:T(8,128)(2,1)}, bf16[128,384]{1,0:T(8,128)(2,1)S(1)}, u32[]{:S(2)}, u32[]{:S(2)}) collective-permute-start(bf16[128,384]{1,0:T(8,128)(2,1)} %get-tuple-element.25), channel_id=1, source_target_pairs={{1,0},{2,1},{3,2},{4,3},{5,4},{6,5},{7,6},{8,7},{9,8},{10,9},{11,1... | collective-permute-start | bytes 294920 | tf_op jit(solution)/shard_map/ppermute | solution.py:408
  21.7 6.7 %collective-permute-start = (bf16[192,384]{1,0:T(8,128)(2,1)}, bf16[192,384]{1,0:T(8,128)(2,1)S(1)}, u32[]{:S(2)}, u32[]{:S(2)}) collective-permute-start(bf16[192,384]{1,0:T(8,128)(2,1)} %get-tuple-element.23), channel_id=1, source_target_pairs={{32,0},{64,32},{96,64},{128,96},{160,128},{192,160},{224,192},{256... | collective-permute-start | bytes 442376 | tf_op jit(solution)/shard_map/ppermute | solution.py:406
  23.6 4.7 %copy-start = (bf16[384,1152]{1,0:T(8,128)(2,1)S(1)}, bf16[384,1152]{1,0:T(8,128)(2,1)}, u32[]{:S(2)}) copy-start(bf16[384,1152]{1,0:T(8,128)(2,1)} %refs_1_.4) | copy-start | bytes 2654212
  23.6 4.7 %copy-start.1 = (bf16[2,8,16,384]{3,2,1,0:T(8,128)(2,1)S(1)}, bf16[2,8,16,384]{3,2,1,0:T(8,128)(2,1)}, u32[]{:S(2)}) copy-start(bf16[2,8,16,384]{3,2,1,0:T(8,128)(2,1)} %refs_2_.2) | copy-start | bytes 589828
  23.7 4.7 %copy-start.2 = (bf16[2,8,16,384]{3,2,1,0:T(8,128)(2,1)S(1)}, bf16[2,8,16,384]{3,2,1,0:T(8,128)(2,1)}, u32[]{:S(2)}) copy-start(bf16[2,8,16,384]{3,2,1,0:T(8,128)(2,1)} %refs_0_.3) | copy-start | bytes 589828
  23.7 4.7 %copy-start.3 = (bf16[704,384]{1,0:T(8,128)(2,1)S(1)}, bf16[704,384]{1,0:T(8,128)(2,1)}, u32[]{:S(2)}) copy-start(bf16[704,384]{1,0:T(8,128)(2,1)} %constant.31.clone.refs_3_.refs_4_) | copy-start | bytes 1622020
  23.7 4.7 %copy-start.4 = (bf16[384,384]{1,0:T(8,128)(2,1)S(1)}, bf16[384,384]{1,0:T(8,128)(2,1)}, u32[]{:S(2)}) copy-start(bf16[384,384]{1,0:T(8,128)(2,1)} %refs_6_.2) | copy-start | bytes 884740
  23.7 4.7 %copy-start.5 = (bf16[384]{0:T(512)(128)(2,1)S(1)}, bf16[384]{0:T(512)(128)(2,1)}, u32[]{:S(2)}) copy-start(bf16[384]{0:T(512)(128)(2,1)} %refs_4_.4) | copy-start | bytes 2308
  23.7 4.7 %copy-start.6 = (s32[16,2]{0,1:T(2,128)S(1)}, s32[16,2]{0,1:T(2,128)}, u32[]{:S(2)}) copy-start(s32[16,2]{0,1:T(2,128)} %param.11) | copy-start | bytes 388
  33.4 3.9 %collective-permute-start.3 = (bf16[2304,128]{1,0:T(8,128)(2,1)S(1)}, bf16[2304,128]{1,0:T(8,128)(2,1)S(1)}, u32[]{:S(2)}, u32[]{:S(2)}) collective-permute-start(bf16[2304,128]{1,0:T(8,128)(2,1)S(1)} %get-tuple-element.30), channel_id=1, source_target_pairs={{0,32},{32,0},{1,33},{33,1},{2,34},{34,2},{3,35},{35,3},{4,36},{36... | collective-permute-start | bytes 1769480 | tf_op jit(solution)/shard_map/ppermute | solution.py:376
  38.3 25.9 %all-to-all-start = ((bf16[16,144,128]{2,1,0:T(8,128)(2,1)}), bf16[16,144,128]{2,1,0:T(8,128)(2,1)S(1)}, u32[]{:S(2)}, u32[]{:S(2)}) async-start(bf16[16,144,128]{2,1,0:T(8,128)(2,1)} %bitcast.2), calls=%async_computation | async-start | bytes 1179648 | tf_op jit(solution)/shard_map/all_to_all | solution.py:364
  55.0 19.3 %collective-permute-start.4 = (bf16[96,384]{1,0:T(8,128)(2,1)S(1)}, bf16[96,384]{1,0:T(8,128)(2,1)S(1)}, u32[]{:S(2)}, u32[]{:S(2)}) collective-permute-start(bf16[96,384]{1,0:T(8,128)(2,1)S(1)} %get-tuple-element.32), channel_id=1, source_target_pairs={{0,1},{1,2},{2,3},{3,4},{4,5},{5,6},{6,7},{7,8},{8,9},{9,10},{10,1... | collective-permute-start | bytes 221192 | tf_op jit(solution)/shard_map/ppermute | solution.py:426
  64.9 14.6 %all-to-all-start.1 = ((bf16[16,9,128]{2,1,0:T(8,128)(2,1)}), bf16[16,9,128]{2,1,0:T(8,128)(2,1)S(1)}, u32[]{:S(2)}, u32[]{:S(2)}) async-start(bf16[16,9,128]{2,1,0:T(8,128)(2,1)} %reshape.24), calls=%async_computation.1 | async-start | bytes 131072 | tf_op jit(solution)/shard_map/all_to_all | solution.py:364
  74.3 29.4 %copy-start.7 = (bf16[128,256]{1,0:T(8,128)(2,1)S(1)}, bf16[128,256]{1,0:T(8,128)(2,1)}, u32[]{:S(2)}) copy-start(bf16[128,256]{1,0:T(8,128)(2,1)} %constant.32.clone.refs_1_) | copy-start | bytes 196612
  80.2 16.0 %all-to-all-start.2 = ((bf16[16,9,128]{2,1,0:T(8,128)(2,1)}), bf16[16,9,128]{2,1,0:T(8,128)(2,1)S(1)}, u32[]{:S(2)}, u32[]{:S(2)}) async-start(bf16[16,9,128]{2,1,0:T(8,128)(2,1)} %broadcast_in_dim.6), calls=%async_computation.2 | async-start | bytes 131072 | tf_op jit(solution)/shard_map/all_to_all | solution.py:364
  89.7 14.0 %collective-permute-start.5 = (bf16[128,384]{1,0:T(8,128)(2,1)S(1)}, bf16[128,384]{1,0:T(8,128)(2,1)S(1)}, u32[]{:S(2)}, u32[]{:S(2)}) collective-permute-start(bf16[128,384]{1,0:T(8,128)(2,1)S(1)} %join_kernel.1), channel_id=1, source_target_pairs={{0,32},{32,64},{64,96},{96,128},{128,160},{160,192},{192,224},{224... | collective-permute-start | bytes 294920 | tf_op jit(solution)/shard_map/ppermute | solution.py:434
  97.2 14.4 %all-to-all-start.3 = ((bf16[16,144,128]{2,1,0:T(8,128)(2,1)}), bf16[16,144,128]{2,1,0:T(8,128)(2,1)S(1)}, u32[]{:S(2)}, u32[]{:S(2)}) async-start(bf16[16,144,128]{2,1,0:T(8,128)(2,1)} %broadcast_in_dim.15), calls=%async_computation.3 | async-start | bytes 1179648 | tf_op jit(solution)/shard_map/all_to_all | solution.py:364
  111.6 6.9 %collective-permute-start.6 = (bf16[2304,128]{1,0:T(8,128)(2,1)S(1)}, bf16[2304,128]{1,0:T(8,128)(2,1)S(1)}, u32[]{:S(2)}, u32[]{:S(2)}) collective-permute-start(bf16[2304,128]{1,0:T(8,128)(2,1)S(1)} %bitcast.4), channel_id=1, source_target_pairs={{0,32},{32,0},{1,33},{33,1},{2,34},{34,2},{3,35},{35,3},{4,36},{36... | collective-permute-start | bytes 1769480 | tf_op jit(solution)/shard_map/ppermute | solution.py:376

commit v9 on v8

--- a/solution.py
+++ b/solution.py
@@ -144,9 +144,9 @@
 
 
 def send_kernel(tok, cot, columns, lat_out, diag_out, lon_out):
-    refs = [tok.get(), cot.get()]
     pick = columns.get()[...]
-    for i, ref in enumerate(refs):
+    for i, fetch in enumerate((tok, cot)):
+        ref = fetch.get()
         upper = dot(pick, ref[:, 0:4].reshape(WIN, -1)).astype(BF16)
         lower = dot(pick[0:32], ref[:, 4:8].reshape(WIN, -1)).astype(BF16)
         lat_out[i * 96 : (i + 1) * 96] = upper[32:128]

time: 121 us -> 121 us (level)
  no operation moved by 1% of the time
where the time goes in v9:
time: 121 us; the launch traced here: 120 us
  starting transfers between devices  80 us (66%)
  waiting for transfers between devices  24.2 us (20%)
  Pallas kernels  12.7 us (10%)
  local copies, waits for them, and re-layouts  2.27 us (2%)
    all_to_all x4, starting transfers between devices, exchange(): lax.all_to_all(parts, ALL, 0, 0, axis_index_groups=groups, tiled=False)  42.1 us
    all_to_all x4, waiting for transfers between devices, exchange(): lax.all_to_all(parts, ALL, 0, 0, axis_index_groups=groups, tiled=False)  17.9 us
    ppermute x1, starting transfers between devices, local(): diag = lax.ppermute(diag, LAT + LON, back(diagonal))  16.7 us
    pallas_call x8, Pallas kernels, call(): pl.pallas_call(body, out_shape=[jax.ShapeDtypeStruct(s, d) for s, d in ou...  12.7 us
    ppermute x2, starting transfers between devices, swapped(): return lax.ppermute(array, 'core', [(0, 1), (1, 0)])  7.27 us
    ppermute x1, starting transfers between devices, local(): rows_back = lax.ppermute(rows_back, LAT, south)  6.51 us
    ppermute x1, starting transfers between devices, local(): side = lax.ppermute(side_back, LON, east)  3.09 us
  transfers between devices with their start and end apart: 11, of which 7 were waited for; matrix products, arithmetic and copies ran while one was open for 1% of the time, Pallas kernels for 3%

profile of v9, /device:TPU:1, one launch (start us, length us, event | category | flops | bytes accessed | tf_op | source)
XLA Modules:
  0.0 120.2 jit_solution(17234484589004590793)
XLA Ops:
  0.6 2.0 %send_kernel.1 = (bf16[192,384]{1,0:T(8,128)(2,1)}, bf16[64,384]{1,0:T(8,128)(2,1)}, bf16[128,384]{1,0:T(8,128)(2,1)}) custom-call(bf16[2,8,16,384]{3,2,1,0:T(8,128)(2,1)} %refs_2_.2, bf16[2,8,16,384]{3,2,1,0:T(8,128)(2,1)} %refs_0_.3, bf16[128,128]{1,0:T(8,128)(2,1)} %constant.30.clone.refs_2_), custom_call_target="tpu_custom_call" | custom-call | tf_op jit(solution)/shard_map/send_kernel/pallas_call | solution.py:84
  2.7 16.7 %collective-permute-start.1 = (bf16[64,384]{1,0:T(8,128)(2,1)}, bf16[64,384]{1,0:T(8,128)(2,1)S(1)}, u32[]{:S(2)}, u32[]{:S(2)}) collective-permute-start(bf16[64,384]{1,0:T(8,128)(2,1)} %get-tuple-element.24), channel_id=1, source_target_pairs={{33,0},{34,1},{35,2},{36,3},{37,4},{38,5},{39,6},{40,7},{41,8},{42... | collective-permute-start | bytes 147464 | tf_op jit(solution)/shard_map/ppermute | solution.py:407
  19.4 2.4 %collective-permute-start.2 = (bf16[128,384]{1,0:T(8,128)(2,1)}, bf16[128,384]{1,0:T(8,128)(2,1)S(1)}, u32[]{:S(2)}, u32[]{:S(2)}) collective-permute-start(bf16[128,384]{1,0:T(8,128)(2,1)} %get-tuple-element.25), channel_id=1, source_target_pairs={{1,0},{2,1},{3,2},{4,3},{5,4},{6,5},{7,6},{8,7},{9,8},{10,9},{11,1... | collective-permute-start | bytes 294920 | tf_op jit(solution)/shard_map/ppermute | solution.py:408
  21.8 1.9 %collective-permute-start = (bf16[192,384]{1,0:T(8,128)(2,1)}, bf16[192,384]{1,0:T(8,128)(2,1)S(1)}, u32[]{:S(2)}, u32[]{:S(2)}) collective-permute-start(bf16[192,384]{1,0:T(8,128)(2,1)} %get-tuple-element.23), channel_id=1, source_target_pairs={{32,0},{64,32},{96,64},{128,96},{160,128},{192,160},{224,192},{256... | collective-permute-start | bytes 442376 | tf_op jit(solution)/shard_map/ppermute | solution.py:406
  23.7 0.0 copy-start.1
  23.7 0.0 copy-start.3
  23.8 0.5 pause_kernel.1.refs_11_
  24.3 1.9 %collective-permute-done.2.refs_9_ = bf16[128,384]{1,0:T(8,128)(2,1)S(1)} collective-permute-done((bf16[128,384]{1,0:T(8,128)(2,1)}, bf16[128,384]{1,0:T(8,128)(2,1)S(1)}, u32[]{:S(2)}, u32[]{:S(2)}) %collective-permute-start.2) | collective-permute-done | bytes 98336 | tf_op jit(solution)/shard_map/ppermute | solution.py:408
  26.3 2.2 %collective-permute-done.refs_7_ = bf16[192,384]{1,0:T(8,128)(2,1)S(1)} collective-permute-done((bf16[192,384]{1,0:T(8,128)(2,1)}, bf16[192,384]{1,0:T(8,128)(2,1)S(1)}, u32[]{:S(2)}, u32[]{:S(2)}) %collective-permute-start) | collective-permute-done | bytes 147488 | tf_op jit(solution)/shard_map/ppermute | solution.py:406
  28.5 5.0 %window_kernel.1 = (bf16[2304,128]{1,0:T(8,128)(2,1)S(1)}, bf16[2,384,384]{2,1,0:T(8,128)(2,1)S(1)}, bf16[12,384,128]{2,1,0:T(8,128)(2,1)S(1)}, bf16[384,384]{1,0:T(8,128)(2,1)S(1)}) custom-call(s32[1]{0:T(128)} %bitcast.refs_0_, s32[2,16]{1,0:T(2,128)S(1)} %bitcast.6, bf16[2,8,16,384]{3,2,1,0:T(8,128)(2,1)S(1)} %copy-done.1, ...), custom_call_target="tpu_custom_call" | custom-call | tf_op jit(solution)/shard_map/window_kernel/pallas_call | solution.py:84
  33.5 2.0 %collective-permute-start.3 = (bf16[2304,128]{1,0:T(8,128)(2,1)S(1)}, bf16[2304,128]{1,0:T(8,128)(2,1)S(1)}, u32[]{:S(2)}, u32[]{:S(2)}) collective-permute-start(bf16[2304,128]{1,0:T(8,128)(2,1)S(1)} %get-tuple-element.30), channel_id=1, source_target_pairs={{0,32},{32,0},{1,33},{33,1},{2,34},{34,2},{3,35},{35,3},{4,36},{36... | collective-permute-start | bytes 1769480 | tf_op jit(solution)/shard_map/ppermute | solution.py:376
  35.5 1.3 %branch_kernel.1 = (bf16[2304,128]{1,0:T(8,128)(2,1)S(1)}, bf16[128,384]{1,0:T(8,128)(2,1)S(1)}, bf16[96,384]{1,0:T(8,128)(2,1)S(1)}, bf16[96,384]{1,0:T(8,128)(2,1)S(1)}, bf16[160,384]{1,0:T(8,128)(2,1)S(1)}) custom-call(s32[1]{0:T(128)} %bitcast.refs_0_, bf16[2,384,384]{2,1,0:T(8,128)(2,1)S(1)} %get-tuple-element.26.refs_1_, ...), custom_call_target="tpu_custom_call" | custom-call | flops 30000001024 | tf_op jit(solution)/shard_map/branch_kernel/pallas_call | solution.py:84
  36.9 0.6 collective-permute-done.3.refs_1_
  37.4 1.0 add_kernel.1
  38.4 16.7 %all-to-all-start = ((bf16[16,144,128]{2,1,0:T(8,128)(2,1)}), bf16[16,144,128]{2,1,0:T(8,128)(2,1)S(1)}, u32[]{:S(2)}, u32[]{:S(2)}) async-start(bf16[16,144,128]{2,1,0:T(8,128)(2,1)} %bitcast.2), calls=%async_computation | async-start | bytes 1179648 | tf_op jit(solution)/shard_map/all_to_all | solution.py:364
  55.1 3.1 %collective-permute-start.4 = (bf16[96,384]{1,0:T(8,128)(2,1)S(1)}, bf16[96,384]{1,0:T(8,128)(2,1)S(1)}, u32[]{:S(2)}, u32[]{:S(2)}) collective-permute-start(bf16[96,384]{1,0:T(8,128)(2,1)S(1)} %get-tuple-element.32), channel_id=1, source_target_pairs={{0,1},{1,2},{2,3},{3,4},{4,5},{5,6},{6,7},{7,8},{8,9},{9,10},{10,1... | collective-permute-start | bytes 221192 | tf_op jit(solution)/shard_map/ppermute | solution.py:426
  58.2 6.1 %all-to-all-done = bf16[16,144,128]{2,1,0:T(8,128)(2,1)S(1)} async-done(((bf16[16,144,128]{2,1,0:T(8,128)(2,1)}), bf16[16,144,128]{2,1,0:T(8,128)(2,1)S(1)}, u32[]{:S(2)}, u32[]{:S(2)}) %all-to-all-start) | async-done | bytes 589856 | tf_op jit(solution)/shard_map/all_to_all | solution.py:364
  64.3 0.1 reduce_sum.24
  64.4 0.7 reshape.24
  65.0 9.4 %all-to-all-start.1 = ((bf16[16,9,128]{2,1,0:T(8,128)(2,1)}), bf16[16,9,128]{2,1,0:T(8,128)(2,1)S(1)}, u32[]{:S(2)}, u32[]{:S(2)}) async-start(bf16[16,9,128]{2,1,0:T(8,128)(2,1)} %reshape.24), calls=%async_computation.1 | async-start | bytes 131072 | tf_op jit(solution)/shard_map/all_to_all | solution.py:364
  74.4 0.0 copy-start.7
  74.4 5.2 %all-to-all-done.1 = bf16[16,9,128]{2,1,0:T(8,128)(2,1)S(1)} async-done(((bf16[16,9,128]{2,1,0:T(8,128)(2,1)}), bf16[16,9,128]{2,1,0:T(8,128)(2,1)S(1)}, u32[]{:S(2)}, u32[]{:S(2)}) %all-to-all-start.1) | async-done | bytes 36896 | tf_op jit(solution)/shard_map/all_to_all | solution.py:364
  79.7 0.6 broadcast_in_dim.6
  80.3 9.5 %all-to-all-start.2 = ((bf16[16,9,128]{2,1,0:T(8,128)(2,1)}), bf16[16,9,128]{2,1,0:T(8,128)(2,1)S(1)}, u32[]{:S(2)}, u32[]{:S(2)}) async-start(bf16[16,9,128]{2,1,0:T(8,128)(2,1)} %broadcast_in_dim.6), calls=%async_computation.2 | async-start | bytes 131072 | tf_op jit(solution)/shard_map/all_to_all | solution.py:364
  89.8 6.5 %collective-permute-start.5 = (bf16[128,384]{1,0:T(8,128)(2,1)S(1)}, bf16[128,384]{1,0:T(8,128)(2,1)S(1)}, u32[]{:S(2)}, u32[]{:S(2)}) collective-permute-start(bf16[128,384]{1,0:T(8,128)(2,1)S(1)} %join_kernel.1), channel_id=1, source_target_pairs={{0,32},{32,64},{64,96},{96,128},{128,160},{160,192},{192,224},{224... | collective-permute-start | bytes 294920 | tf_op jit(solution)/shard_map/ppermute | solution.py:434
  96.3 0.9 broadcast_in_dim.15
  97.2 6.6 %all-to-all-start.3 = ((bf16[16,144,128]{2,1,0:T(8,128)(2,1)}), bf16[16,144,128]{2,1,0:T(8,128)(2,1)S(1)}, u32[]{:S(2)}, u32[]{:S(2)}) async-start(bf16[16,144,128]{2,1,0:T(8,128)(2,1)} %broadcast_in_dim.15), calls=%async_computation.3 | async-start | bytes 1179648 | tf_op jit(solution)/shard_map/all_to_all | solution.py:364
  103.8 1.3 %token_kernel.1 = bf16[2,8,16,384]{3,2,1,0:T(8,128)(2,1)} custom-call(bf16[2,8,16,384]{3,2,1,0:T(8,128)(2,1)S(1)} %copy-done.2, bf16[128,256]{1,0:T(8,128)(2,1)S(1)} %copy-done.7, bf16[128,384]{1,0:T(8,128)(2,1)S(1)} %get-tuple-element.34.refs_2_, bf16[160,384]{1,0:T(8,128)(2,1)S(1)} %get-tuple-element.35.refs_3_, ...), custom_call_target="tpu_custom_call" | custom-call | flops 30000001024 | tf_op jit(solution)/shard_map/token_kernel/pallas_call | solution.py:84
  105.1 6.6 %all-to-all-done.3 = bf16[16,144,128]{2,1,0:T(8,128)(2,1)S(1)} async-done(((bf16[16,144,128]{2,1,0:T(8,128)(2,1)}), bf16[16,144,128]{2,1,0:T(8,128)(2,1)S(1)}, u32[]{:S(2)}, u32[]{:S(2)}) %all-to-all-start.3) | async-done | bytes 589856 | tf_op jit(solution)/shard_map/all_to_all | solution.py:364
  111.7 5.3 %collective-permute-start.6 = (bf16[2304,128]{1,0:T(8,128)(2,1)S(1)}, bf16[2304,128]{1,0:T(8,128)(2,1)S(1)}, u32[]{:S(2)}, u32[]{:S(2)}) collective-permute-start(bf16[2304,128]{1,0:T(8,128)(2,1)S(1)} %bitcast.4), channel_id=1, source_target_pairs={{0,32},{32,0},{1,33},{33,1},{2,34},{34,2},{3,35},{35,3},{4,36},{36... | collective-permute-start | bytes 1769480 | tf_op jit(solution)/shard_map/ppermute | solution.py:376
  117.0 1.6 %collective-permute-done.6.refs_3_ = bf16[2304,128]{1,0:T(8,128)(2,1)S(1)} collective-permute-done((bf16[2304,128]{1,0:T(8,128)(2,1)S(1)}, bf16[2304,128]{1,0:T(8,128)(2,1)S(1)}, u32[]{:S(2)}, u32[]{:S(2)}) %collective-permute-start.6) | collective-permute-done | bytes 589856 | tf_op jit(solution)/shard_map/ppermute | solution.py:376
  118.6 1.6 %result_kernel.1 = (bf16[384,1152]{1,0:T(8,128)(2,1)}, bf16[384,384]{1,0:T(8,128)(2,1)}, bf16[384]{0:T(512)(128)(2,1)}) custom-call(s32[1]{0:T(128)} %bitcast.refs_0_, bf16[384,1152]{1,0:T(8,128)(2,1)S(1)} %copy-done, bf16[2304,128]{1,0:T(8,128)(2,1)S(1)} %bitcast.5, bf16[2304,128]{1,0:T(8,128)(2,1)S(1)} %collective-permute-done.6.refs_3_, ...), custom_call_target="tpu_custom_call" | custom-call | tf_op jit(solution)/shard_map/result_kernel/pallas_call | solution.py:84
  (20 shorter events, 0.1 us)
Async XLA Ops:
  2.7 21.7 %collective-permute-start.1 = (bf16[64,384]{1,0:T(8,128)(2,1)}, bf16[64,384]{1,0:T(8,128)(2,1)S(1)}, u32[]{:S(2)}, u32[]{:S(2)}) collective-permute-start(bf16[64,384]{1,0:T(8,128)(2,1)} %get-tuple-element.24), channel_id=1, source_target_pairs={{33,0},{34,1},{35,2},{36,3},{37,4},{38,5},{39,6},{40,7},{41,8},{42... | collective-permute-start | bytes 147464 | tf_op jit(solution)/shard_map/ppermute | solution.py:407
  19.4 6.9 %collective-permute-start.2 = (bf16[128,384]{1,0:T(8,128)(2,1)}, bf16[128,384]{1,0:T(8,128)(2,1)S(1)}, u32[]{:S(2)}, u32[]{:S(2)}) collective-permute-start(bf16[128,384]{1,0:T(8,128)(2,1)} %get-tuple-element.25), channel_id=1, source_target_pairs={{1,0},{2,1},{3,2},{4,3},{5,4},{6,5},{7,6},{8,7},{9,8},{10,9},{11,1... | collective-permute-start | bytes 294920 | tf_op jit(solution)/shard_map/ppermute | solution.py:408
  21.8 6.7 %collective-permute-start = (bf16[192,384]{1,0:T(8,128)(2,1)}, bf16[192,384]{1,0:T(8,128)(2,1)S(1)}, u32[]{:S(2)}, u32[]{:S(2)}) collective-permute-start(bf16[192,384]{1,0:T(8,128)(2,1)} %get-tuple-element.23), channel_id=1, source_target_pairs={{32,0},{64,32},{96,64},{128,96},{160,128},{192,160},{224,192},{256... | collective-permute-start | bytes 442376 | tf_op jit(solution)/shard_map/ppermute | solution.py:406
  23.7 4.7 %copy-start = (bf16[384,1152]{1,0:T(8,128)(2,1)S(1)}, bf16[384,1152]{1,0:T(8,128)(2,1)}, u32[]{:S(2)}) copy-start(bf16[384,1152]{1,0:T(8,128)(2,1)} %refs_1_.4) | copy-start | bytes 2654212
  23.7 4.7 %copy-start.1 = (bf16[2,8,16,384]{3,2,1,0:T(8,128)(2,1)S(1)}, bf16[2,8,16,384]{3,2,1,0:T(8,128)(2,1)}, u32[]{:S(2)}) copy-start(bf16[2,8,16,384]{3,2,1,0:T(8,128)(2,1)} %refs_2_.2) | copy-start | bytes 589828
  23.7 4.7 %copy-start.2 = (bf16[2,8,16,384]{3,2,1,0:T(8,128)(2,1)S(1)}, bf16[2,8,16,384]{3,2,1,0:T(8,128)(2,1)}, u32[]{:S(2)}) copy-start(bf16[2,8,16,384]{3,2,1,0:T(8,128)(2,1)} %refs_0_.3) | copy-start | bytes 589828
  23.7 4.7 %copy-start.3 = (bf16[704,384]{1,0:T(8,128)(2,1)S(1)}, bf16[704,384]{1,0:T(8,128)(2,1)}, u32[]{:S(2)}) copy-start(bf16[704,384]{1,0:T(8,128)(2,1)} %constant.31.clone.refs_3_.refs_4_) | copy-start | bytes 1622020
  23.8 4.7 %copy-start.4 = (bf16[384,384]{1,0:T(8,128)(2,1)S(1)}, bf16[384,384]{1,0:T(8,128)(2,1)}, u32[]{:S(2)}) copy-start(bf16[384,384]{1,0:T(8,128)(2,1)} %refs_6_.2) | copy-start | bytes 884740
  23.8 4.7 %copy-start.5 = (bf16[384]{0:T(512)(128)(2,1)S(1)}, bf16[384]{0:T(512)(128)(2,1)}, u32[]{:S(2)}) copy-start(bf16[384]{0:T(512)(128)(2,1)} %refs_4_.4) | copy-start | bytes 2308
  23.8 4.7 %copy-start.6 = (s32[16,2]{0,1:T(2,128)S(1)}, s32[16,2]{0,1:T(2,128)}, u32[]{:S(2)}) copy-start(s32[16,2]{0,1:T(2,128)} %param.11) | copy-start | bytes 388
  33.5 3.9 %collective-permute-start.3 = (bf16[2304,128]{1,0:T(8,128)(2,1)S(1)}, bf16[2304,128]{1,0:T(8,128)(2,1)S(1)}, u32[]{:S(2)}, u32[]{:S(2)}) collective-permute-start(bf16[2304,128]{1,0:T(8,128)(2,1)S(1)} %get-tuple-element.30), channel_id=1, source_target_pairs={{0,32},{32,0},{1,33},{33,1},{2,34},{34,2},{3,35},{35,3},{4,36},{36... | collective-permute-start | bytes 1769480 | tf_op jit(solution)/shard_map/ppermute | solution.py:376
  38.4 25.9 %all-to-all-start = ((bf16[16,144,128]{2,1,0:T(8,128)(2,1)}), bf16[16,144,128]{2,1,0:T(8,128)(2,1)S(1)}, u32[]{:S(2)}, u32[]{:S(2)}) async-start(bf16[16,144,128]{2,1,0:T(8,128)(2,1)} %bitcast.2), calls=%async_computation | async-start | bytes 1179648 | tf_op jit(solution)/shard_map/all_to_all | solution.py:364
  55.1 19.3 %collective-permute-start.4 = (bf16[96,384]{1,0:T(8,128)(2,1)S(1)}, bf16[96,384]{1,0:T(8,128)(2,1)S(1)}, u32[]{:S(2)}, u32[]{:S(2)}) collective-permute-start(bf16[96,384]{1,0:T(8,128)(2,1)S(1)} %get-tuple-element.32), channel_id=1, source_target_pairs={{0,1},{1,2},{2,3},{3,4},{4,5},{5,6},{6,7},{7,8},{8,9},{9,10},{10,1... | collective-permute-start | bytes 221192 | tf_op jit(solution)/shard_map/ppermute | solution.py:426
  65.0 14.6 %all-to-all-start.1 = ((bf16[16,9,128]{2,1,0:T(8,128)(2,1)}), bf16[16,9,128]{2,1,0:T(8,128)(2,1)S(1)}, u32[]{:S(2)}, u32[]{:S(2)}) async-start(bf16[16,9,128]{2,1,0:T(8,128)(2,1)} %reshape.24), calls=%async_computation.1 | async-start | bytes 131072 | tf_op jit(solution)/shard_map/all_to_all | solution.py:364
  74.4 29.4 %copy-start.7 = (bf16[128,256]{1,0:T(8,128)(2,1)S(1)}, bf16[128,256]{1,0:T(8,128)(2,1)}, u32[]{:S(2)}) copy-start(bf16[128,256]{1,0:T(8,128)(2,1)} %constant.32.clone.refs_1_) | copy-start | bytes 196612
  80.3 16.0 %all-to-all-start.2 = ((bf16[16,9,128]{2,1,0:T(8,128)(2,1)}), bf16[16,9,128]{2,1,0:T(8,128)(2,1)S(1)}, u32[]{:S(2)}, u32[]{:S(2)}) async-start(bf16[16,9,128]{2,1,0:T(8,128)(2,1)} %broadcast_in_dim.6), calls=%async_computation.2 | async-start | bytes 131072 | tf_op jit(solution)/shard_map/all_to_all | solution.py:364
  89.8 14.0 %collective-permute-start.5 = (bf16[128,384]{1,0:T(8,128)(2,1)S(1)}, bf16[128,384]{1,0:T(8,128)(2,1)S(1)}, u32[]{:S(2)}, u32[]{:S(2)}) collective-permute-start(bf16[128,384]{1,0:T(8,128)(2,1)S(1)} %join_kernel.1), channel_id=1, source_target_pairs={{0,32},{32,64},{64,96},{96,128},{128,160},{160,192},{192,224},{224... | collective-permute-start | bytes 294920 | tf_op jit(solution)/shard_map/ppermute | solution.py:434
  97.2 14.4 %all-to-all-start.3 = ((bf16[16,144,128]{2,1,0:T(8,128)(2,1)}), bf16[16,144,128]{2,1,0:T(8,128)(2,1)S(1)}, u32[]{:S(2)}, u32[]{:S(2)}) async-start(bf16[16,144,128]{2,1,0:T(8,128)(2,1)} %broadcast_in_dim.15), calls=%async_computation.3 | async-start | bytes 1179648 | tf_op jit(solution)/shard_map/all_to_all | solution.py:364
  111.7 6.9 %collective-permute-start.6 = (bf16[2304,128]{1,0:T(8,128)(2,1)S(1)}, bf16[2304,128]{1,0:T(8,128)(2,1)S(1)}, u32[]{:S(2)}, u32[]{:S(2)}) collective-permute-start(bf16[2304,128]{1,0:T(8,128)(2,1)S(1)} %bitcast.4), channel_id=1, source_target_pairs={{0,32},{32,0},{1,33},{33,1},{2,34},{34,2},{3,35},{35,3},{4,36},{36... | collective-permute-start | bytes 1769480 | tf_op jit(solution)/shard_map/ppermute | solution.py:376

commit v10 on v9

--- a/solution.py
+++ b/solution.py
@@ -31,7 +31,7 @@
 
 RINGS = rings(7)
 PLANES = [
-    [(((z // 8 * 4 + (x + 3) % 4) * 2 + core) * 8 + z % 8) * 4 + y for x in range(4) for y in range(4)]
+    [(((z // 8 * 4 + (x + 3 * core) % 4) * 2 + core) * 8 + z % 8) * 4 + y for x in range(4) for y in range(4)]
     for z in range(16)
     for core in range(2)
 ]

time: 121 us -> 121 us (level)
  no operation moved by 1% of the time
where the time goes in v10:
time: 121 us; the launch traced here: 120 us
  starting transfers between devices  80 us (66%)
  waiting for transfers between devices  24.5 us (20%)
  Pallas kernels  12.7 us (10%)
  local copies, waits for them, and re-layouts  2.27 us (2%)
    all_to_all x4, starting transfers between devices, exchange(): lax.all_to_all(parts, ALL, 0, 0, axis_index_groups=groups, tiled=False)  42.4 us
    all_to_all x4, waiting for transfers between devices, exchange(): lax.all_to_all(parts, ALL, 0, 0, axis_index_groups=groups, tiled=False)  18.2 us
    ppermute x1, starting transfers between devices, local(): diag = lax.ppermute(diag, LAT + LON, back(diagonal))  16.7 us
    pallas_call x8, Pallas kernels, call(): pl.pallas_call(body, out_shape=[jax.ShapeDtypeStruct(s, d) for s, d in ou...  12.7 us
    ppermute x2, starting transfers between devices, swapped(): return lax.ppermute(array, 'core', [(0, 1), (1, 0)])  7.23 us
    ppermute x1, starting transfers between devices, local(): rows_back = lax.ppermute(rows_back, LAT, south)  6.26 us
    ppermute x1, starting transfers between devices, local(): side = lax.ppermute(side_back, LON, east)  3.09 us
  transfers between devices with their start and end apart: 11, of which 7 were waited for; matrix products, arithmetic and copies ran while one was open for 1% of the time, Pallas kernels for 3%

profile of v10, /device:TPU:1, one launch (start us, length us, event | category | flops | bytes accessed | tf_op | source)
XLA Modules:
  0.0 120.5 jit_solution(18248615408024285363)
XLA Ops:
  0.6 2.0 %send_kernel.1 = (bf16[192,384]{1,0:T(8,128)(2,1)}, bf16[64,384]{1,0:T(8,128)(2,1)}, bf16[128,384]{1,0:T(8,128)(2,1)}) custom-call(bf16[2,8,16,384]{3,2,1,0:T(8,128)(2,1)} %refs_2_.2, bf16[2,8,16,384]{3,2,1,0:T(8,128)(2,1)} %refs_0_.3, bf16[128,128]{1,0:T(8,128)(2,1)} %constant.30.clone.refs_2_), custom_call_target="tpu_custom_call" | custom-call | tf_op jit(solution)/shard_map/send_kernel/pallas_call | solution.py:84
  2.7 16.7 %collective-permute-start.1 = (bf16[64,384]{1,0:T(8,128)(2,1)}, bf16[64,384]{1,0:T(8,128)(2,1)S(1)}, u32[]{:S(2)}, u32[]{:S(2)}) collective-permute-start(bf16[64,384]{1,0:T(8,128)(2,1)} %get-tuple-element.24), channel_id=1, source_target_pairs={{33,0},{34,1},{35,2},{36,3},{37,4},{38,5},{39,6},{40,7},{41,8},{42... | collective-permute-start | bytes 147464 | tf_op jit(solution)/shard_map/ppermute | solution.py:407
  19.4 2.4 %collective-permute-start.2 = (bf16[128,384]{1,0:T(8,128)(2,1)}, bf16[128,384]{1,0:T(8,128)(2,1)S(1)}, u32[]{:S(2)}, u32[]{:S(2)}) collective-permute-start(bf16[128,384]{1,0:T(8,128)(2,1)} %get-tuple-element.25), channel_id=1, source_target_pairs={{1,0},{2,1},{3,2},{4,3},{5,4},{6,5},{7,6},{8,7},{9,8},{10,9},{11,1... | collective-permute-start | bytes 294920 | tf_op jit(solution)/shard_map/ppermute | solution.py:408
  21.8 1.9 %collective-permute-start = (bf16[192,384]{1,0:T(8,128)(2,1)}, bf16[192,384]{1,0:T(8,128)(2,1)S(1)}, u32[]{:S(2)}, u32[]{:S(2)}) collective-permute-start(bf16[192,384]{1,0:T(8,128)(2,1)} %get-tuple-element.23), channel_id=1, source_target_pairs={{32,0},{64,32},{96,64},{128,96},{160,128},{192,160},{224,192},{256... | collective-permute-start | bytes 442376 | tf_op jit(solution)/shard_map/ppermute | solution.py:406
  23.7 0.0 copy-start
  23.7 0.0 copy-start.3
  23.8 0.5 pause_kernel.1.refs_11_
  24.3 1.9 %collective-permute-done.2.refs_9_ = bf16[128,384]{1,0:T(8,128)(2,1)S(1)} collective-permute-done((bf16[128,384]{1,0:T(8,128)(2,1)}, bf16[128,384]{1,0:T(8,128)(2,1)S(1)}, u32[]{:S(2)}, u32[]{:S(2)}) %collective-permute-start.2) | collective-permute-done | bytes 98336 | tf_op jit(solution)/shard_map/ppermute | solution.py:408
  26.3 2.2 %collective-permute-done.refs_7_ = bf16[192,384]{1,0:T(8,128)(2,1)S(1)} collective-permute-done((bf16[192,384]{1,0:T(8,128)(2,1)}, bf16[192,384]{1,0:T(8,128)(2,1)S(1)}, u32[]{:S(2)}, u32[]{:S(2)}) %collective-permute-start) | collective-permute-done | bytes 147488 | tf_op jit(solution)/shard_map/ppermute | solution.py:406
  28.5 5.0 %window_kernel.1 = (bf16[2304,128]{1,0:T(8,128)(2,1)S(1)}, bf16[2,384,384]{2,1,0:T(8,128)(2,1)S(1)}, bf16[12,384,128]{2,1,0:T(8,128)(2,1)S(1)}, bf16[384,384]{1,0:T(8,128)(2,1)S(1)}) custom-call(s32[1]{0:T(128)} %bitcast.refs_0_, s32[2,16]{1,0:T(2,128)S(1)} %bitcast.6, bf16[2,8,16,384]{3,2,1,0:T(8,128)(2,1)S(1)} %copy-done.1, ...), custom_call_target="tpu_custom_call" | custom-call | tf_op jit(solution)/shard_map/window_kernel/pallas_call | solution.py:84
  33.5 2.0 %collective-permute-start.3 = (bf16[2304,128]{1,0:T(8,128)(2,1)S(1)}, bf16[2304,128]{1,0:T(8,128)(2,1)S(1)}, u32[]{:S(2)}, u32[]{:S(2)}) collective-permute-start(bf16[2304,128]{1,0:T(8,128)(2,1)S(1)} %get-tuple-element.30), channel_id=1, source_target_pairs={{0,32},{32,0},{1,33},{33,1},{2,34},{34,2},{3,35},{35,3},{4,36},{36... | collective-permute-start | bytes 1769480 | tf_op jit(solution)/shard_map/ppermute | solution.py:376
  35.5 1.3 %branch_kernel.1 = (bf16[2304,128]{1,0:T(8,128)(2,1)S(1)}, bf16[128,384]{1,0:T(8,128)(2,1)S(1)}, bf16[96,384]{1,0:T(8,128)(2,1)S(1)}, bf16[96,384]{1,0:T(8,128)(2,1)S(1)}, bf16[160,384]{1,0:T(8,128)(2,1)S(1)}) custom-call(s32[1]{0:T(128)} %bitcast.refs_0_, bf16[2,384,384]{2,1,0:T(8,128)(2,1)S(1)} %get-tuple-element.26.refs_1_, ...), custom_call_target="tpu_custom_call" | custom-call | flops 30000001024 | tf_op jit(solution)/shard_map/branch_kernel/pallas_call | solution.py:84
  36.9 0.6 collective-permute-done.3.refs_1_
  37.4 1.0 add_kernel.1
  38.4 16.7 %all-to-all-start = ((bf16[16,144,128]{2,1,0:T(8,128)(2,1)}), bf16[16,144,128]{2,1,0:T(8,128)(2,1)S(1)}, u32[]{:S(2)}, u32[]{:S(2)}) async-start(bf16[16,144,128]{2,1,0:T(8,128)(2,1)} %bitcast.2), calls=%async_computation | async-start | bytes 1179648 | tf_op jit(solution)/shard_map/all_to_all | solution.py:364
  55.1 3.1 %collective-permute-start.4 = (bf16[96,384]{1,0:T(8,128)(2,1)S(1)}, bf16[96,384]{1,0:T(8,128)(2,1)S(1)}, u32[]{:S(2)}, u32[]{:S(2)}) collective-permute-start(bf16[96,384]{1,0:T(8,128)(2,1)S(1)} %get-tuple-element.32), channel_id=1, source_target_pairs={{0,1},{1,2},{2,3},{3,4},{4,5},{5,6},{6,7},{7,8},{8,9},{9,10},{10,1... | collective-permute-start | bytes 221192 | tf_op jit(solution)/shard_map/ppermute | solution.py:426
  58.2 6.3 %all-to-all-done = bf16[16,144,128]{2,1,0:T(8,128)(2,1)S(1)} async-done(((bf16[16,144,128]{2,1,0:T(8,128)(2,1)}), bf16[16,144,128]{2,1,0:T(8,128)(2,1)S(1)}, u32[]{:S(2)}, u32[]{:S(2)}) %all-to-all-start) | async-done | bytes 589856 | tf_op jit(solution)/shard_map/all_to_all | solution.py:364
  64.5 0.1 reduce_sum.24
  64.6 0.7 reshape.24
  65.2 9.4 %all-to-all-start.1 = ((bf16[16,9,128]{2,1,0:T(8,128)(2,1)}), bf16[16,9,128]{2,1,0:T(8,128)(2,1)S(1)}, u32[]{:S(2)}, u32[]{:S(2)}) async-start(bf16[16,9,128]{2,1,0:T(8,128)(2,1)} %reshape.24), calls=%async_computation.1 | async-start | bytes 131072 | tf_op jit(solution)/shard_map/all_to_all | solution.py:364
  74.6 0.0 copy-start.7
  74.6 5.2 %all-to-all-done.1 = bf16[16,9,128]{2,1,0:T(8,128)(2,1)S(1)} async-done(((bf16[16,9,128]{2,1,0:T(8,128)(2,1)}), bf16[16,9,128]{2,1,0:T(8,128)(2,1)S(1)}, u32[]{:S(2)}, u32[]{:S(2)}) %all-to-all-start.1) | async-done | bytes 36896 | tf_op jit(solution)/shard_map/all_to_all | solution.py:364
  79.9 0.6 broadcast_in_dim.6
  80.5 9.5 %all-to-all-start.2 = ((bf16[16,9,128]{2,1,0:T(8,128)(2,1)}), bf16[16,9,128]{2,1,0:T(8,128)(2,1)S(1)}, u32[]{:S(2)}, u32[]{:S(2)}) async-start(bf16[16,9,128]{2,1,0:T(8,128)(2,1)} %broadcast_in_dim.6), calls=%async_computation.2 | async-start | bytes 131072 | tf_op jit(solution)/shard_map/all_to_all | solution.py:364
  90.0 6.3 %collective-permute-start.5 = (bf16[128,384]{1,0:T(8,128)(2,1)S(1)}, bf16[128,384]{1,0:T(8,128)(2,1)S(1)}, u32[]{:S(2)}, u32[]{:S(2)}) collective-permute-start(bf16[128,384]{1,0:T(8,128)(2,1)S(1)} %join_kernel.1), channel_id=1, source_target_pairs={{0,32},{32,64},{64,96},{96,128},{128,160},{160,192},{192,224},{224... | collective-permute-start | bytes 294920 | tf_op jit(solution)/shard_map/ppermute | solution.py:434
  96.3 0.9 broadcast_in_dim.15
  97.2 6.8 %all-to-all-start.3 = ((bf16[16,144,128]{2,1,0:T(8,128)(2,1)}), bf16[16,144,128]{2,1,0:T(8,128)(2,1)S(1)}, u32[]{:S(2)}, u32[]{:S(2)}) async-start(bf16[16,144,128]{2,1,0:T(8,128)(2,1)} %broadcast_in_dim.15), calls=%async_computation.3 | async-start | bytes 1179648 | tf_op jit(solution)/shard_map/all_to_all | solution.py:364
  104.1 1.3 %token_kernel.1 = bf16[2,8,16,384]{3,2,1,0:T(8,128)(2,1)} custom-call(bf16[2,8,16,384]{3,2,1,0:T(8,128)(2,1)S(1)} %copy-done.2, bf16[128,256]{1,0:T(8,128)(2,1)S(1)} %copy-done.7, bf16[128,384]{1,0:T(8,128)(2,1)S(1)} %get-tuple-element.34.refs_2_, bf16[160,384]{1,0:T(8,128)(2,1)S(1)} %get-tuple-element.35.refs_3_, ...), custom_call_target="tpu_custom_call" | custom-call | flops 30000001024 | tf_op jit(solution)/shard_map/token_kernel/pallas_call | solution.py:84
  105.3 6.7 %all-to-all-done.3 = bf16[16,144,128]{2,1,0:T(8,128)(2,1)S(1)} async-done(((bf16[16,144,128]{2,1,0:T(8,128)(2,1)}), bf16[16,144,128]{2,1,0:T(8,128)(2,1)S(1)}, u32[]{:S(2)}, u32[]{:S(2)}) %all-to-all-start.3) | async-done | bytes 589856 | tf_op jit(solution)/shard_map/all_to_all | solution.py:364
  112.0 5.2 %collective-permute-start.6 = (bf16[2304,128]{1,0:T(8,128)(2,1)S(1)}, bf16[2304,128]{1,0:T(8,128)(2,1)S(1)}, u32[]{:S(2)}, u32[]{:S(2)}) collective-permute-start(bf16[2304,128]{1,0:T(8,128)(2,1)S(1)} %bitcast.4), channel_id=1, source_target_pairs={{0,32},{32,0},{1,33},{33,1},{2,34},{34,2},{3,35},{35,3},{4,36},{36... | collective-permute-start | bytes 1769480 | tf_op jit(solution)/shard_map/ppermute | solution.py:376
  117.2 1.6 %collective-permute-done.6.refs_3_ = bf16[2304,128]{1,0:T(8,128)(2,1)S(1)} collective-permute-done((bf16[2304,128]{1,0:T(8,128)(2,1)S(1)}, bf16[2304,128]{1,0:T(8,128)(2,1)S(1)}, u32[]{:S(2)}, u32[]{:S(2)}) %collective-permute-start.6) | collective-permute-done | bytes 589856 | tf_op jit(solution)/shard_map/ppermute | solution.py:376
  118.9 1.6 %result_kernel.1 = (bf16[384,1152]{1,0:T(8,128)(2,1)}, bf16[384,384]{1,0:T(8,128)(2,1)}, bf16[384]{0:T(512)(128)(2,1)}) custom-call(s32[1]{0:T(128)} %bitcast.refs_0_, bf16[384,1152]{1,0:T(8,128)(2,1)S(1)} %copy-done, bf16[2304,128]{1,0:T(8,128)(2,1)S(1)} %bitcast.5, bf16[2304,128]{1,0:T(8,128)(2,1)S(1)} %collective-permute-done.6.refs_3_, ...), custom_call_target="tpu_custom_call" | custom-call | tf_op jit(solution)/shard_map/result_kernel/pallas_call | solution.py:84
  (20 shorter events, 0.1 us)
Async XLA Ops:
  2.7 21.7 %collective-permute-start.1 = (bf16[64,384]{1,0:T(8,128)(2,1)}, bf16[64,384]{1,0:T(8,128)(2,1)S(1)}, u32[]{:S(2)}, u32[]{:S(2)}) collective-permute-start(bf16[64,384]{1,0:T(8,128)(2,1)} %get-tuple-element.24), channel_id=1, source_target_pairs={{33,0},{34,1},{35,2},{36,3},{37,4},{38,5},{39,6},{40,7},{41,8},{42... | collective-permute-start | bytes 147464 | tf_op jit(solution)/shard_map/ppermute | solution.py:407
  19.4 6.9 %collective-permute-start.2 = (bf16[128,384]{1,0:T(8,128)(2,1)}, bf16[128,384]{1,0:T(8,128)(2,1)S(1)}, u32[]{:S(2)}, u32[]{:S(2)}) collective-permute-start(bf16[128,384]{1,0:T(8,128)(2,1)} %get-tuple-element.25), channel_id=1, source_target_pairs={{1,0},{2,1},{3,2},{4,3},{5,4},{6,5},{7,6},{8,7},{9,8},{10,9},{11,1... | collective-permute-start | bytes 294920 | tf_op jit(solution)/shard_map/ppermute | solution.py:408
  21.8 6.7 %collective-permute-start = (bf16[192,384]{1,0:T(8,128)(2,1)}, bf16[192,384]{1,0:T(8,128)(2,1)S(1)}, u32[]{:S(2)}, u32[]{:S(2)}) collective-permute-start(bf16[192,384]{1,0:T(8,128)(2,1)} %get-tuple-element.23), channel_id=1, source_target_pairs={{32,0},{64,32},{96,64},{128,96},{160,128},{192,160},{224,192},{256... | collective-permute-start | bytes 442376 | tf_op jit(solution)/shard_map/ppermute | solution.py:406
  23.7 4.7 %copy-start = (bf16[384,1152]{1,0:T(8,128)(2,1)S(1)}, bf16[384,1152]{1,0:T(8,128)(2,1)}, u32[]{:S(2)}) copy-start(bf16[384,1152]{1,0:T(8,128)(2,1)} %refs_1_.4) | copy-start | bytes 2654212
  23.7 4.7 %copy-start.1 = (bf16[2,8,16,384]{3,2,1,0:T(8,128)(2,1)S(1)}, bf16[2,8,16,384]{3,2,1,0:T(8,128)(2,1)}, u32[]{:S(2)}) copy-start(bf16[2,8,16,384]{3,2,1,0:T(8,128)(2,1)} %refs_2_.2) | copy-start | bytes 589828
  23.7 4.7 %copy-start.2 = (bf16[2,8,16,384]{3,2,1,0:T(8,128)(2,1)S(1)}, bf16[2,8,16,384]{3,2,1,0:T(8,128)(2,1)}, u32[]{:S(2)}) copy-start(bf16[2,8,16,384]{3,2,1,0:T(8,128)(2,1)} %refs_0_.3) | copy-start | bytes 589828
  23.7 4.7 %copy-start.3 = (bf16[704,384]{1,0:T(8,128)(2,1)S(1)}, bf16[704,384]{1,0:T(8,128)(2,1)}, u32[]{:S(2)}) copy-start(bf16[704,384]{1,0:T(8,128)(2,1)} %constant.31.clone.refs_3_.refs_4_) | copy-start | bytes 1622020
  23.8 4.7 %copy-start.4 = (bf16[384,384]{1,0:T(8,128)(2,1)S(1)}, bf16[384,384]{1,0:T(8,128)(2,1)}, u32[]{:S(2)}) copy-start(bf16[384,384]{1,0:T(8,128)(2,1)} %refs_6_.2) | copy-start | bytes 884740
  23.8 4.7 %copy-start.5 = (bf16[384]{0:T(512)(128)(2,1)S(1)}, bf16[384]{0:T(512)(128)(2,1)}, u32[]{:S(2)}) copy-start(bf16[384]{0:T(512)(128)(2,1)} %refs_4_.4) | copy-start | bytes 2308
  23.8 4.7 %copy-start.6 = (s32[16,2]{0,1:T(2,128)S(1)}, s32[16,2]{0,1:T(2,128)}, u32[]{:S(2)}) copy-start(s32[16,2]{0,1:T(2,128)} %param.11) | copy-start | bytes 388
  33.5 3.9 %collective-permute-start.3 = (bf16[2304,128]{1,0:T(8,128)(2,1)S(1)}, bf16[2304,128]{1,0:T(8,128)(2,1)S(1)}, u32[]{:S(2)}, u32[]{:S(2)}) collective-permute-start(bf16[2304,128]{1,0:T(8,128)(2,1)S(1)} %get-tuple-element.30), channel_id=1, source_target_pairs={{0,32},{32,0},{1,33},{33,1},{2,34},{34,2},{3,35},{35,3},{4,36},{36... | collective-permute-start | bytes 1769480 | tf_op jit(solution)/shard_map/ppermute | solution.py:376
  38.4 26.1 %all-to-all-start = ((bf16[16,144,128]{2,1,0:T(8,128)(2,1)}), bf16[16,144,128]{2,1,0:T(8,128)(2,1)S(1)}, u32[]{:S(2)}, u32[]{:S(2)}) async-start(bf16[16,144,128]{2,1,0:T(8,128)(2,1)} %bitcast.2), calls=%async_computation | async-start | bytes 1179648 | tf_op jit(solution)/shard_map/all_to_all | solution.py:364
  55.1 19.5 %collective-permute-start.4 = (bf16[96,384]{1,0:T(8,128)(2,1)S(1)}, bf16[96,384]{1,0:T(8,128)(2,1)S(1)}, u32[]{:S(2)}, u32[]{:S(2)}) collective-permute-start(bf16[96,384]{1,0:T(8,128)(2,1)S(1)} %get-tuple-element.32), channel_id=1, source_target_pairs={{0,1},{1,2},{2,3},{3,4},{4,5},{5,6},{6,7},{7,8},{8,9},{9,10},{10,1... | collective-permute-start | bytes 221192 | tf_op jit(solution)/shard_map/ppermute | solution.py:426
  65.2 14.6 %all-to-all-start.1 = ((bf16[16,9,128]{2,1,0:T(8,128)(2,1)}), bf16[16,9,128]{2,1,0:T(8,128)(2,1)S(1)}, u32[]{:S(2)}, u32[]{:S(2)}) async-start(bf16[16,9,128]{2,1,0:T(8,128)(2,1)} %reshape.24), calls=%async_computation.1 | async-start | bytes 131072 | tf_op jit(solution)/shard_map/all_to_all | solution.py:364
  74.6 29.4 %copy-start.7 = (bf16[128,256]{1,0:T(8,128)(2,1)S(1)}, bf16[128,256]{1,0:T(8,128)(2,1)}, u32[]{:S(2)}) copy-start(bf16[128,256]{1,0:T(8,128)(2,1)} %constant.32.clone.refs_1_) | copy-start | bytes 196612
  80.5 15.8 %all-to-all-start.2 = ((bf16[16,9,128]{2,1,0:T(8,128)(2,1)}), bf16[16,9,128]{2,1,0:T(8,128)(2,1)S(1)}, u32[]{:S(2)}, u32[]{:S(2)}) async-start(bf16[16,9,128]{2,1,0:T(8,128)(2,1)} %broadcast_in_dim.6), calls=%async_computation.2 | async-start | bytes 131072 | tf_op jit(solution)/shard_map/all_to_all | solution.py:364
  90.0 14.0 %collective-permute-start.5 = (bf16[128,384]{1,0:T(8,128)(2,1)S(1)}, bf16[128,384]{1,0:T(8,128)(2,1)S(1)}, u32[]{:S(2)}, u32[]{:S(2)}) collective-permute-start(bf16[128,384]{1,0:T(8,128)(2,1)S(1)} %join_kernel.1), channel_id=1, source_target_pairs={{0,32},{32,64},{64,96},{96,128},{128,160},{160,192},{192,224},{224... | collective-permute-start | bytes 294920 | tf_op jit(solution)/shard_map/ppermute | solution.py:434
  97.2 14.8 %all-to-all-start.3 = ((bf16[16,144,128]{2,1,0:T(8,128)(2,1)}), bf16[16,144,128]{2,1,0:T(8,128)(2,1)S(1)}, u32[]{:S(2)}, u32[]{:S(2)}) async-start(bf16[16,144,128]{2,1,0:T(8,128)(2,1)} %broadcast_in_dim.15), calls=%async_computation.3 | async-start | bytes 1179648 | tf_op jit(solution)/shard_map/all_to_all | solution.py:364
  112.0 6.8 %collective-permute-start.6 = (bf16[2304,128]{1,0:T(8,128)(2,1)S(1)}, bf16[2304,128]{1,0:T(8,128)(2,1)S(1)}, u32[]{:S(2)}, u32[]{:S(2)}) collective-permute-start(bf16[2304,128]{1,0:T(8,128)(2,1)S(1)} %bitcast.4), channel_id=1, source_target_pairs={{0,32},{32,0},{1,33},{33,1},{2,34},{34,2},{3,35},{35,3},{4,36},{36... | collective-permute-start | bytes 1769480 | tf_op jit(solution)/shard_map/ppermute | solution.py:376
